TPU v7x, 32 devices: a whole 2x2x4 slice. The times are simulated.
32 devices in a mesh: grp: 2 (over y), pts: 8 (over z, x), rcv: 2 (over core).
Axes of the slice: x: 2, y: 2, z: 4, core: 2. Of those that a mesh axis runs over, the one named last changes fastest.
Arguments:
- src_green: float32 [2, 128, 2048], P(None, 'grp', 'pts'), parts along dimension 1, may hold values from -0.125 to 0.125
- rcv_green: float32 [2, 2048, 2048], P(None, ('grp', 'rcv'), 'pts'), parts along dimension 1, may hold values from -6 to 6
- model: float32 [4096], P(('grp', 'pts')), parts along dimension 0, may hold values from -6 to 6
- observed: float32 [128, 2, 1024], P(('grp', 'pts'), None, 'rcv'), parts along dimension 0, may hold values from -30 to 30, as said below
Outputs:
- gradient: float32 [4096], P(('grp', 'pts')), parts along dimension 0
There are 2 independent parts, one for each index of `grp`. A program takes and returns all parts, laid end to end along the dimension named above; each array names one. Nothing has to cross between parts.
Inputs may be any that keep to these rules, and one draw needn't show every extreme that they name: `observed`: complex data (real and imaginary parts) whose scale varies with the source.
All inputs are finite; a program needn't handle non-finite values.
Results may differ from a plain program's by a relative error of at most 0.000068.
Values sent between devices are 32-bit elements; how exact they have to be, the bound alone decides.
No kernel may reach another device: no remote copies, remote signals or barrier semaphores. Data moves between devices by JAX's collectives and lax.ppermute only.
A program may use at most 64 MiB of HBM per device.

v0:
```python
import jax
import jax.numpy as jnp
from jax import lax
from jax.sharding import PartitionSpec as P


def modelled_data(scaled, rcv_green):
    highest = lax.Precision.HIGHEST
    real_part = jnp.dot(
        scaled[0], rcv_green[0].T, precision=highest, preferred_element_type=jnp.float32
    ) - jnp.dot(scaled[1], rcv_green[1].T, precision=highest, preferred_element_type=jnp.float32)
    imag_part = jnp.dot(
        scaled[0], rcv_green[1].T, precision=highest, preferred_element_type=jnp.float32
    ) + jnp.dot(scaled[1], rcv_green[0].T, precision=highest, preferred_element_type=jnp.float32)
    return jnp.stack([real_part, imag_part], axis=1)


def image_terms(weighted, rcv_green, src_rows):
    highest = lax.Precision.HIGHEST
    back_real = jnp.dot(
        weighted[:, 0, :], rcv_green[0], precision=highest, preferred_element_type=jnp.float32
    ) + jnp.dot(
        weighted[:, 1, :], rcv_green[1], precision=highest, preferred_element_type=jnp.float32
    )
    back_imag = jnp.dot(
        weighted[:, 1, :], rcv_green[0], precision=highest, preferred_element_type=jnp.float32
    ) - jnp.dot(
        weighted[:, 0, :], rcv_green[1], precision=highest, preferred_element_type=jnp.float32
    )
    return jnp.sum(src_rows[0] * back_real + src_rows[1] * back_imag, axis=0)


def cauchy_weights(resid, spread_sq):
    energy = resid[:, 0, :] ** 2 + resid[:, 1, :] ** 2
    return resid / (1.0 + energy / spread_sq)[:, None, :]


def local(src_green, rcv_green, model, observed):
    num_sources = src_green.shape[1]
    num_points = src_green.shape[2] * lax.axis_size("pts")
    num_receivers = rcv_green.shape[1] * lax.axis_size("rcv")
    scaled = src_green * model[None, None, :]
    all_observed = lax.all_gather(observed, "pts", axis=0, tiled=True)
    modelled = lax.psum(modelled_data(scaled, rcv_green), "pts")
    resid = modelled - all_observed
    energy_sum = jnp.sum(resid[:, 0, :] ** 2 + resid[:, 1, :] ** 2)
    total = lax.psum(energy_sum, "rcv")
    spread_sq = total / (num_sources * num_receivers) + 1e-06
    weighted = cauchy_weights(resid, spread_sq)
    partial_image = image_terms(weighted, rcv_green, src_green)
    image = lax.psum(partial_image, "rcv")
    return image * jnp.sqrt(jnp.float32(num_points) / (num_receivers * num_sources))


def solution(mesh):
    placed = (
        P(None, "grp", "pts"),
        P(None, ("grp", "rcv"), "pts"),
        P(("grp", "pts")),
        P(("grp", "pts"), None, "rcv"),
    )
    return jax.shard_map(
        local, mesh=mesh, in_specs=placed, out_specs=P(("grp", "pts")), check_vma=False
    )
```

profile of v0, /device:TPU:0, one launch (start us, length us, event | category | flops | bytes accessed | tf_op | source)
XLA Modules:
  0.0 103.9 jit_solution(12044138015975517374)
XLA Ops:
  6.5 0.0 copy-start
  6.5 0.0 all-reduce.2.cloned.1.call-start
  6.5 1.0 broadcast_multiply_fusion
  7.5 1.6 %fusion.16 = f32[64,512]{1,0:T(8,128)S(1)} fusion(f32[2,512,256]{2,1,0:T(8,128)} %param.5, f32[2,64,256]{2,1,0:T(8,128)S(1)} %broadcast_multiply_fusion), kind=kOutput, calls=%fused_computation.20 | convolution fusion | flops 100663296 | bytes 720896 | tf_op jit(solution)/shard_map/dot_general | solution.py:9
  9.2 1.6 %fusion.8 = f32[64,512]{1,0:T(8,128)S(1)} fusion(f32[2,512,256]{2,1,0:T(8,128)} %param.5, f32[2,64,256]{2,1,0:T(8,128)S(1)} %broadcast_multiply_fusion), kind=kOutput, calls=%fused_computation.12 | convolution fusion | flops 100663296 | bytes 720896 | tf_op jit(solution)/shard_map/dot_general | solution.py:12
  10.8 0.0 copy-done
  10.9 0.6 fusion.1
  11.5 0.6 fusion
  12.1 0.7 pad_maximum_fusion
  12.8 0.0 all-reduce.2.cloned.1.call-update
  12.8 0.7 copy-done.2
  13.6 32.7 %all_gather.3 = f32[64,2,512]{2,0,1:T(8,128)S(1)} all-gather(f32[8,2,512]{2,0,1:T(8,128)S(1)} %copy.5), channel_id=1, replica_groups=mesh['grp'=2,'pts'=8,'rcv'=2] {'pts'}, dimensions={0}, use_global_device_ids=true | all-gather | bytes 294912 | tf_op jit(solution)/shard_map/all_gather | solution.py:43
  46.2 40.3 %all-reduce.2.cloned.1.call-done = f32[64,2,512]{2,0,1:T(8,128)} async-done(((f32[64,2,512]{2,0,1:T(8,128)}), f32[64,2,512]{2,0,1:T(8,128)}) %all-reduce.2.cloned.1.call-update) | async-done | bytes 262160 | tf_op jit(solution)/shard_map/psum | solution.py:44
  86.5 1.0 sub.10
  87.5 0.6 fusion.27
  88.1 3.1 %psum.22 = f32[]{:T(128)} all-reduce(f32[]{:T(128)} %fusion.27), channel_id=1, replica_groups=mesh['grp'=2,'pts'=8,'rcv'=2] {'rcv'}, use_global_device_ids=true, to_apply=%region_2.0 | all-reduce | flops 1 | bytes 8 | tf_op jit(solution)/shard_map/psum | solution.py:47
  91.9 0.4 fusion.13
  92.3 0.0 copy-start.1
  92.3 0.4 fusion.11
  92.7 0.5 copy-done.1
  93.2 0.4 fusion.4
  93.6 0.4 fusion.5
  94.0 2.5 %psum.23 = f32[256]{0:T(256)S(1)} all-reduce(f32[256]{0:T(256)S(1)} %fusion.5), channel_id=1, replica_groups=mesh['grp'=2,'pts'=8,'rcv'=2] {'rcv'}, use_global_device_ids=true, to_apply=%region_4.0 | all-reduce | flops 256 | bytes 2048 | tf_op jit(solution)/shard_map/psum | solution.py:51
  96.5 0.6 broadcast_multiply_fusion.1
  (4 shorter events, 0.1 us)
Async XLA Ops:
  6.5 4.3 %copy-start = (f32[2,512,256]{2,1,0:T(8,128)S(1)}, f32[2,512,256]{2,1,0:T(8,128)}, u32[]{:S(2)}) copy-start(f32[2,512,256]{2,1,0:T(8,128)} %param.5) | copy-start | bytes 3145732
  6.5 80.0 %all-reduce.2.cloned.1.call-start = ((), (), s32[]{:S(2)}) async-start(), calls=%async_computation | async-start | bytes 524288 | tf_op jit(solution)/shard_map/psum | solution.py:44
  12.8 0.8 copy-start.2
  92.3 0.9 copy-start.1
Sparse Core Ops, SparseCore 0:
  12.9 73.5 all-reduce.1
where the time goes:
time: 104 us
  waiting for transfers between devices  40.3 us (39%)
  blocking collectives  38.2 us (37%)
  between operations  14.1 us (14%)
  matrix products  6.05 us (6%)
  other arithmetic  3.97 us (4%)
  local copies, waits for them, and re-layouts  1.26 us (1%)
    psum x1, waiting for transfers between devices, local(): modelled = lax.psum(modelled_data(scaled, rcv_green), 'pts')  40.3 us
    all_gather x1, blocking collectives, local(): all_observed = lax.all_gather(observed, 'pts', axis=0, tiled=True)  32.7 us
    psum x1, blocking collectives, local(): total = lax.psum(energy_sum, 'rcv')  3.08 us
    psum x1, blocking collectives, local(): image = lax.psum(partial_image, 'rcv')  2.47 us
  transfers between devices with their start and end apart: 1, of which 1 were waited for; matrix products, arithmetic and copies ran while one was open for 0% of the time, Pallas kernels for 0%

commit v1 on v0

v1 whole, which is shorter than its diff:
```python
import jax
import jax.numpy as jnp
from jax import lax
from jax.sharding import PartitionSpec as P


def dot(a, b, contract):
    return lax.dot_general(
        a, b, (contract, ((), ())), precision=lax.Precision.HIGH, preferred_element_type=jnp.float32
    )


def swap_pairs(points, cores, bit_of):
    return [
        (p * cores + c, (p ^ (1 << bit_of(c))) * cores + c) for p in range(points) for c in range(cores)
    ]


def swap(array, points, cores, bit_of):
    return lax.ppermute(array, ("pts", "rcv"), swap_pairs(points, cores, bit_of))


def modelled_part(stacked, rcv_part):
    num_sources = stacked.shape[0] // 2
    by_real = dot(stacked, rcv_part[0], ((1,), (1,)))
    by_imag = dot(stacked, rcv_part[1], ((1,), (1,)))
    real_part = by_real[:num_sources] - by_imag[num_sources:]
    imag_part = by_imag[:num_sources] + by_real[num_sources:]
    return jnp.stack([real_part, imag_part], axis=0)


def local(src_green, rcv_green, model, observed):
    num_sources = src_green.shape[1]
    points, cores = lax.axis_size("pts"), lax.axis_size("rcv")
    num_points = src_green.shape[2] * points
    num_receivers = rcv_green.shape[1] * cores
    me, core = lax.axis_index("pts"), lax.axis_index("rcv")
    bits = points.bit_length() - 1
    assert points == 1 << bits
    order = [[(k + c) % bits for k in range(bits)] for c in range(cores)]
    half = rcv_green.shape[1] // 2

    scaled = src_green * model[None, None, :]
    stacked = scaled.reshape(2 * num_sources, scaled.shape[2])
    first_bit = jnp.array([o[0] for o in order], jnp.int32)[core]
    side = lax.rem(lax.shift_right_logical(me, first_bit), 2)
    own_observed = jnp.transpose(observed, (1, 0, 2))

    def part(which):
        rcv_part = lax.dynamic_slice_in_dim(rcv_green, which * half, half, axis=1)
        obs_part = lax.dynamic_slice_in_dim(own_observed, which * half, half, axis=2)
        full = modelled_part(stacked, rcv_part)
        rows = jnp.zeros_like(full)
        rows = lax.dynamic_update_slice_in_dim(rows, obs_part, me * observed.shape[0], axis=1)
        return full - rows

    sent = part(1 - side)
    arrived = swap(sent, points, cores, lambda c: order[c][0])
    resid = part(side) + arrived
    for k in range(1, bits):
        resid = resid + swap(resid, points, cores, lambda c, k=k: order[c][k])
    other = swap(resid, points, cores, lambda c: order[c][0])

    own_energy = resid[0] ** 2 + resid[1] ** 2
    other_energy = other[0] ** 2 + other[1] ** 2
    energy_sum = jnp.sum(own_energy) + jnp.sum(other_energy)
    total = lax.psum(energy_sum, "rcv") if cores != 2 else energy_sum + lax.ppermute(
        energy_sum, "rcv", [(0, 1), (1, 0)]
    )
    spread_sq = total / (num_sources * num_receivers) + 1e-06

    src_stack = src_green.reshape(2 * num_sources, -1)
    src_turned = jnp.concatenate([-src_green[1], src_green[0]], axis=0)

    def image(part_resid, energy, which):
        weighted = part_resid / (1.0 + energy / spread_sq)[None]
        rows = weighted.reshape(2 * num_sources, half)
        rcv_part = lax.dynamic_slice_in_dim(rcv_green, which * half, half, axis=1)
        to_real = dot(rows, src_stack, ((0,), (0,)))
        to_imag = dot(rows, src_turned, ((0,), (0,)))
        return jnp.sum(rcv_part[0] * to_real + rcv_part[1] * to_imag, axis=0)

    partial = image(resid, own_energy, side) + image(other, other_energy, 1 - side)
    partial = partial * jnp.sqrt(jnp.float32(num_points) / (num_receivers * num_sources))
    if cores != 2:
        return lax.psum(partial, "rcv")
    return partial + lax.ppermute(partial, "rcv", [(0, 1), (1, 0)])


def solution(mesh):
    placed = (
        P(None, "grp", "pts"),
        P(None, ("grp", "rcv"), "pts"),
        P(("grp", "pts")),
        P(("grp", "pts"), None, "rcv"),
    )
    return jax.shard_map(
        local, mesh=mesh, in_specs=placed, out_specs=P(("grp", "pts")), check_vma=False
    )
```

time: 104 us -> 34.7 us (0.33)
  the two profiles are of different devices: /device:TPU:0 before, /device:TPU:25 now
where the time goes in v1:
time: 34.7 us; the launch traced here: 34.5 us
  waiting for transfers between devices  16.9 us (49%)
  starting transfers between devices  7.37 us (21%)
  matrix products  4.5 us (13%)
  other arithmetic  2.95 us (9%)
  between operations  2.09 us (6%)
  local copies, waits for them, and re-layouts  0.75 us (2%)
    ppermute x4, waiting for transfers between devices, swap(): lax.ppermute(array, ('pts', 'rcv'), swap_pairs(points, cores, bit_of))  16 us
    ppermute x1, starting transfers between devices, local(): lax.ppermute(energy_sum, 'rcv', [(0, 1), (1, 0)])  5.32 us
    dot_general x8, matrix products, dot(): lax.dot_general(a, b, (contract, ((), ())), precision=lax.Precision.HIGH,...  4.5 us
    ppermute x4, starting transfers between devices, swap(): lax.ppermute(array, ('pts', 'rcv'), swap_pairs(points, cores, bit_of))  1.7 us
    reduce_sum x2, other arithmetic, local(): energy_sum = jnp.sum(own_energy) + jnp.sum(other_energy)  1.26 us
    mul x1, other arithmetic, local(): scaled = src_green * model[None, None, :]  0.92 us
    ppermute x1, waiting for transfers between devices, local(): return partial + lax.ppermute(partial, 'rcv', [(0, 1), (1, 0)])  0.86 us
    unnamed x8, local copies, waits for them, and re-layouts  0.69 us
  transfers between devices with their start and end apart: 6, of which 5 were waited for; matrix products, arithmetic and copies ran while one was open for 4% of the time, Pallas kernels for 0%

profile of v1, /device:TPU:25, one launch (start us, length us, event | category | flops | bytes accessed | tf_op | source)
XLA Modules:
  0.0 34.5 jit_solution(16831897155552040223)
XLA Ops:
  0.0 0.7 %copy-done.3 = f32[256]{0:T(256)S(1)} copy-done((f32[256]{0:T(256)S(1)}, f32[256]{0:T(256)}, u32[]{:S(2)}) %copy-start.3) | copy-done | bytes 1048
  0.7 0.9 %broadcast_multiply_fusion = f32[2,64,256]{2,1,0:T(8,128)S(1)} fusion(f32[2,64,256]{2,1,0:T(8,128)} %param.5, f32[256]{0:T(256)S(1)} %copy-done.3), kind=kLoop, calls=%fused_computation.42 | loop fusion | flops 32768 | bytes 263168 | tf_op jit(solution)/shard_map/mul | solution.py:43
  1.6 1.3 %fusion.7 = f32[128,256]{1,0:T(8,128)S(1)} fusion(f32[128,256]{1,0:T(8,128)S(1)} %bitcast.73, f32[2,512,256]{2,1,0:T(8,128)} %param.6, s32[]{:T(128)S(6)} %select_n.20), kind=kOutput, calls=%fused_computation.15 | convolution fusion | flops 50331648 | bytes 524292 | tf_op jit(solution)/shard_map/dot_general | solution.py:8
  3.0 1.3 %fusion.9 = f32[128,256]{1,0:T(8,128)S(1)} fusion(f32[128,256]{1,0:T(8,128)S(1)} %bitcast.74, f32[2,512,256]{2,1,0:T(8,128)} %param.6, s32[]{:T(128)S(6)} %add.91, s32[]{:T(128)S(6)} %select_n.20), kind=kOutput, calls=%fused_computation.17 | convolution fusion | flops 50331648 | bytes 524296 | tf_op jit(solution)/shard_map/dot_general | solution.py:8
  4.4 0.2 collective-permute-start
  4.6 0.3 fusion.8
  4.9 0.3 fusion.6
  5.3 3.3 %collective-permute-done = f32[2,64,256]{2,1,0:T(8,128)S(1)} collective-permute-done((f32[2,64,256]{2,1,0:T(8,128)S(1)}, f32[2,64,256]{2,1,0:T(8,128)S(1)}, u32[]{:S(2)}, u32[]{:S(2)}) %collective-permute-start) | collective-permute-done | bytes 131104 | tf_op jit(solution)/shard_map/ppermute | solution.py:20
  8.6 0.1 collective-permute-start.1
  8.7 6.1 %collective-permute-done.1 = f32[2,64,256]{2,1,0:T(8,128)S(1)} collective-permute-done((f32[2,64,256]{2,1,0:T(8,128)S(1)}, f32[2,64,256]{2,1,0:T(8,128)S(1)}, u32[]{:S(2)}, u32[]{:S(2)}) %collective-permute-start.1) | collective-permute-done | bytes 131104 | tf_op jit(solution)/shard_map/ppermute | solution.py:20
  14.8 1.3 %collective-permute-start.2 = (f32[2,64,256]{2,1,0:T(8,128)S(1)}, f32[2,64,256]{2,1,0:T(8,128)S(1)}, u32[]{:S(2)}, u32[]{:S(2)}) collective-permute-start(f32[2,64,256]{2,1,0:T(8,128)S(1)} %add.78), channel_id=1, source_target_pairs={{0,8},{1,3},{2,10},{3,1},{4,12},{5,7},{6,14},{7,5},{8,0},{9,11},{1... | collective-permute-start | bytes 393224 | tf_op jit(solution)/shard_map/ppermute | solution.py:20
  16.1 2.6 %collective-permute-done.2 = f32[2,64,256]{2,1,0:T(8,128)S(1)} collective-permute-done((f32[2,64,256]{2,1,0:T(8,128)S(1)}, f32[2,64,256]{2,1,0:T(8,128)S(1)}, u32[]{:S(2)}, u32[]{:S(2)}) %collective-permute-start.2) | collective-permute-done | bytes 131104 | tf_op jit(solution)/shard_map/ppermute | solution.py:20
  18.7 0.1 collective-permute-start.3
  18.8 0.6 %fusion.19 = f32[]{:T(128)} fusion(f32[2,64,256]{2,1,0:T(8,128)S(1)} %add.79), kind=kLoop, calls=%fused_computation.47 | loop fusion | flops 65535 | bytes 131076 | tf_op jit(solution)/shard_map/reduce_sum | solution.py:66
  19.4 4.1 %collective-permute-done.3 = f32[2,64,256]{2,1,0:T(8,128)S(1)} collective-permute-done((f32[2,64,256]{2,1,0:T(8,128)S(1)}, f32[2,64,256]{2,1,0:T(8,128)S(1)}, u32[]{:S(2)}, u32[]{:S(2)}) %collective-permute-start.3) | collective-permute-done | bytes 131104 | tf_op jit(solution)/shard_map/ppermute | solution.py:20
  23.5 0.6 %fusion.20 = f32[]{:T(128)} fusion(f32[2,64,256]{2,1,0:T(8,128)S(1)} %collective-permute-done.3), kind=kLoop, calls=%fused_computation.48 | loop fusion | flops 65535 | bytes 131076 | tf_op jit(solution)/shard_map/reduce_sum | solution.py:66
  25.4 5.3 %collective-permute-start.4 = (f32[]{:T(128)}, f32[]{:T(128)}, u32[]{:S(2)}, u32[]{:S(2)}) collective-permute-start(f32[]{:T(128)} %add.82), channel_id=1, source_target_pairs={{0,1},{1,0},{2,3},{3,2},{4,5},{5,4},{6,7},{7,6},{8,9},{9,8},{10,11... | collective-permute-start | bytes 20 | tf_op jit(solution)/shard_map/ppermute | solution.py:67
  31.4 0.3 convolution_multiply_fusion
  31.7 0.3 fusion.5
  32.1 0.3 convolution_multiply_fusion.1
  32.4 0.3 fusion.4
  32.7 0.3 collective-permute-start.5
  33.1 0.9 %collective-permute-done.5 = f32[256]{0:T(256)S(1)} collective-permute-done((f32[256]{0:T(256)S(1)}, f32[256]{0:T(256)S(1)}, u32[]{:S(2)}, u32[]{:S(2)}) %collective-permute-start.5) | collective-permute-done | bytes 1056 | tf_op jit(solution)/shard_map/ppermute | solution.py:87
  34.0 0.6 %add.90 = f32[256]{0:T(256)} add(f32[256]{0:T(256)S(1)} %add_multiply_fusion, f32[256]{0:T(256)S(1)} %collective-permute-done.5) | non-fusion elementwise | flops 256 | bytes 3072 | tf_op jit(solution)/shard_map/add | solution.py:87
  (24 shorter events, 0.3 us)
Async XLA Ops:
  0.0 0.7 %copy-start.3 = (f32[256]{0:T(256)S(1)}, f32[256]{0:T(256)}, u32[]{:S(2)}) copy-start(f32[256]{0:T(256)} %param.7) | copy-start | bytes 3076
  0.7 3.6 %copy-start.2 = (f32[8,2,512]{2,1,0:T(2,128)S(1)}, f32[8,2,512]{2,1,0:T(2,128)}, u32[]{:S(2)}) copy-start(f32[8,2,512]{2,1,0:T(2,128)} %param.8) | copy-start | bytes 98308
  1.6 3.0 %copy-start = (f32[2,512,256]{2,1,0:T(8,128)S(1)}, f32[2,512,256]{2,1,0:T(8,128)}, u32[]{:S(2)}) copy-start(f32[2,512,256]{2,1,0:T(8,128)} %param.6) | copy-start | bytes 3145732
  4.4 4.2 %collective-permute-start = (f32[2,64,256]{2,1,0:T(8,128)S(1)}, f32[2,64,256]{2,1,0:T(8,128)S(1)}, u32[]{:S(2)}, u32[]{:S(2)}) collective-permute-start(f32[2,64,256]{2,1,0:T(8,128)S(1)} %maximum_subtract_fusion.1), channel_id=1, source_target_pairs={{0,2},{1,5},{2,0},{3,7},{4,6},{5,1},{6,4},{7,3},{8,10},{9,13},{10,... | collective-permute-start | bytes 393224 | tf_op jit(solution)/shard_map/ppermute | solution.py:20
  8.6 6.2 %collective-permute-start.1 = (f32[2,64,256]{2,1,0:T(8,128)S(1)}, f32[2,64,256]{2,1,0:T(8,128)S(1)}, u32[]{:S(2)}, u32[]{:S(2)}) collective-permute-start(f32[2,64,256]{2,1,0:T(8,128)S(1)} %fusion.10), channel_id=1, source_target_pairs={{0,4},{1,9},{2,6},{3,11},{4,0},{5,13},{6,2},{7,15},{8,12},{9,1},{1... | collective-permute-start | bytes 393224 | tf_op jit(solution)/shard_map/ppermute | solution.py:20
  14.8 4.0 %copy-start.1 = (f32[2,64,256]{2,1,0:T(8,128)S(1)}, f32[2,64,256]{2,1,0:T(8,128)}, u32[]{:S(2)}) copy-start(f32[2,64,256]{2,1,0:T(8,128)} %param.5) | copy-start | bytes 393220
  14.8 3.9 %collective-permute-start.2 = (f32[2,64,256]{2,1,0:T(8,128)S(1)}, f32[2,64,256]{2,1,0:T(8,128)S(1)}, u32[]{:S(2)}, u32[]{:S(2)}) collective-permute-start(f32[2,64,256]{2,1,0:T(8,128)S(1)} %add.78), channel_id=1, source_target_pairs={{0,8},{1,3},{2,10},{3,1},{4,12},{5,7},{6,14},{7,5},{8,0},{9,11},{1... | collective-permute-start | bytes 393224 | tf_op jit(solution)/shard_map/ppermute | solution.py:20
  18.7 4.8 %collective-permute-start.3 = (f32[2,64,256]{2,1,0:T(8,128)S(1)}, f32[2,64,256]{2,1,0:T(8,128)S(1)}, u32[]{:S(2)}, u32[]{:S(2)}) collective-permute-start(f32[2,64,256]{2,1,0:T(8,128)S(1)} %add.79), channel_id=1, source_target_pairs={{0,2},{1,5},{2,0},{3,7},{4,6},{5,1},{6,4},{7,3},{8,10},{9,13},{10,... | collective-permute-start | bytes 393224 | tf_op jit(solution)/shard_map/ppermute | solution.py:20
  25.4 5.3 %collective-permute-start.4 = (f32[]{:T(128)}, f32[]{:T(128)}, u32[]{:S(2)}, u32[]{:S(2)}) collective-permute-start(f32[]{:T(128)} %add.82), channel_id=1, source_target_pairs={{0,1},{1,0},{2,3},{3,2},{4,5},{5,4},{6,7},{7,6},{8,9},{9,8},{10,11... | collective-permute-start | bytes 20 | tf_op jit(solution)/shard_map/ppermute | solution.py:67
  32.7 1.2 %collective-permute-start.5 = (f32[256]{0:T(256)S(1)}, f32[256]{0:T(256)S(1)}, u32[]{:S(2)}, u32[]{:S(2)}) collective-permute-start(f32[256]{0:T(256)S(1)} %add_multiply_fusion), channel_id=1, source_target_pairs={{0,1},{1,0},{2,3},{3,2},{4,5},{5,4},{6,7},{7,6},{8,9},{9,8},{10,11... | collective-permute-start | bytes 3080 | tf_op jit(solution)/shard_map/ppermute | solution.py:87

commit v2 on v0

v2 whole, which is shorter than its diff:
```python
import functools

import jax
import jax.numpy as jnp
from jax import lax
from jax.experimental import pallas as pl
from jax.experimental.pallas import tpu as pltpu
from jax.sharding import PartitionSpec as P

CHUNKS = 2
LANES_LAST = (((1,), (1,)), ((), ()))
PLAIN = (((1,), (0,)), ((), ()))
VMEM_LIMIT = 24 * 1024 * 1024
COST = 1


def split(x):
    high = x.astype(jnp.bfloat16)
    return high, (x - high.astype(jnp.float32)).astype(jnp.bfloat16)


def dot(a, b, dims):
    return lax.dot_general(a, b, dims, preferred_element_type=jnp.float32)


def stacked(real, imag):
    return [jnp.concatenate(rows, axis=0) for rows in ([real, imag], [-imag, real])]


def modelled_kernel(part, me_ref, src_ref, model_ref, rcv_ref, obs_ref, *refs):
    first = part == 0
    if first:
        out_ref, rcv_out, rows_ref, obs_held, placed_ref, src_held, model_held, sems = refs
    else:
        rows_ref, out_ref, rcv_out, obs_held, placed_ref, sems = refs
    receivers = out_ref.shape[0]
    own, sources = obs_ref.shape[0], src_ref.shape[1]
    here = pl.ds(part * receivers, receivers)
    copies = [
        pltpu.make_async_copy(rcv_ref.at[0, here, :], rcv_out.at[0], sems.at[0]),
        pltpu.make_async_copy(rcv_ref.at[1, here, :], rcv_out.at[1], sems.at[1]),
        pltpu.make_async_copy(obs_ref.at[:, :, here], obs_held, sems.at[2]),
    ]
    if first:
        inputs = [
            pltpu.make_async_copy(src_ref, src_held, sems.at[3]),
            pltpu.make_async_copy(model_ref, model_held, sems.at[4]),
        ]
        for copy in inputs:
            copy.start()
    for copy in copies:
        copy.start()
    placed_ref[...] = jnp.zeros_like(placed_ref)
    if first:
        for copy in inputs:
            copy.wait()
        model = model_held[...]
        for c, rows in enumerate(stacked(src_held[0] * model, src_held[1] * model)):
            rows_ref[c, 0], rows_ref[c, 1] = split(rows)
    copies[2].wait()
    for c in range(2):
        start = pl.multiple_of(c * sources + me_ref[0] * own, own)
        placed_ref[pl.ds(start, own), :] = obs_held[:, c, :]
    total = -placed_ref[...].T
    for c in range(2):
        copies[c].wait()
        rcv_high, rcv_low = split(rcv_out[c])
        total += dot(rcv_high, rows_ref[c, 0], LANES_LAST)
        total += dot(rcv_high, rows_ref[c, 1], LANES_LAST)
        total += dot(rcv_low, rows_ref[c, 0], LANES_LAST)
    out_ref[...] = total


def modelled_part(part, me, src_green, model, rcv_green, observed, rows):
    _, sources, points = src_green.shape
    receivers = rcv_green.shape[1] // CHUNKS
    own = observed.shape[0]
    in_hbm, in_vmem = pl.BlockSpec(memory_space=pltpu.HBM), pl.BlockSpec(memory_space=pltpu.VMEM)
    outs = [
        jax.ShapeDtypeStruct((receivers, 2 * sources), jnp.float32),
        jax.ShapeDtypeStruct((2, receivers, points), jnp.float32),
    ]
    scratch = [
        pltpu.VMEM((own, 2, receivers), jnp.float32),
        pltpu.VMEM((2 * sources, receivers), jnp.float32),
    ]
    if part == 0:
        outs.append(jax.ShapeDtypeStruct((2, 2, 2 * sources, points), jnp.bfloat16))
        scratch += [pltpu.VMEM(src_green.shape, jnp.float32), pltpu.VMEM(model.shape, jnp.float32)]
    scratch.append(pltpu.SemaphoreType.DMA((5 if part == 0 else 3,)))
    return pl.pallas_call(
        functools.partial(modelled_kernel, part),
        out_shape=outs,
        in_specs=[pl.BlockSpec(memory_space=pltpu.SMEM)] + [in_hbm] * 4 + [in_vmem] * len(rows),
        out_specs=[in_vmem] * len(outs),
        scratch_shapes=scratch,
        compiler_params=pltpu.CompilerParams(vmem_limit_bytes=VMEM_LIMIT),
        cost_estimate=pl.CostEstimate(flops=COST * 10**9, bytes_accessed=COST * 4 * 10**6, transcendentals=0),
        name=f"modelled_{part}",
    )(me, *(pltpu.with_memory_space_constraint(x, pltpu.HBM) for x in (src_green, model, rcv_green, observed)), *rows)


def image_kernel(count, scale, *refs):
    resid = [refs[:CHUNKS], refs[CHUNKS : 2 * CHUNKS]]
    src_ref, *rcv_own = refs[2 * CHUNKS : 3 * CHUNKS + 1]
    rcv_other = refs[3 * CHUNKS + 1]
    out_ref = refs[-1]
    sources, points = src_ref.shape[1:]
    rows = resid[0][0].shape[0]
    rcv = [rcv_own, [rcv_other.at[:, pl.ds(k * rows, rows), :] for k in range(CHUNKS)]]
    tile = min(rows, 256)

    def energy(group):
        total = jnp.zeros((8, 2 * sources), jnp.float32)
        for ref in group:
            total += jnp.sum((ref[...] ** 2).reshape(-1, 8, 2 * sources), axis=0)
        return jnp.sum(total)

    spread_sq = (energy(resid[0]) + energy(resid[1])) / count + 1e-06
    stacks = []
    for part in ([src_ref[0], src_ref[1]], [-src_ref[1], src_ref[0]]):
        high, low = split(jnp.concatenate(part, axis=0))
        stacks.append((jnp.concatenate([high, high], axis=0), low))

    sums = []
    for group, rcv_group in zip(resid, rcv):
        total = jnp.zeros((8, points), jnp.float32)
        for ref, rcv_ref in zip(group, rcv_group):
            for start in range(0, rows, tile):
                here = ref[start : start + tile, :]
                square = here * here
                both = square + pltpu.roll(square, sources, 1)
                weighted_high, weighted_low = split(here / (1.0 + both / spread_sq))
                wide = jnp.concatenate([weighted_high, weighted_low], axis=1)
                for c, (double, low) in enumerate(stacks):
                    terms = dot(wide, double, PLAIN) + dot(weighted_high, low, PLAIN)
                    terms = terms * rcv_ref[c, start : start + tile, :]
                    total += jnp.sum(terms.reshape(-1, 8, points), axis=0)
        sums.append(jnp.sum(total, axis=0, keepdims=True))
    out_ref[...] = (sums[0] + sums[1]) * scale


def image(own, other, src_green, rcv_own, rcv_other, count, scale):
    points = src_green.shape[2]
    whole = pl.BlockSpec(memory_space=pltpu.VMEM)
    return pl.pallas_call(
        functools.partial(image_kernel, count, scale),
        out_shape=jax.ShapeDtypeStruct((1, points), jnp.float32),
        in_specs=[whole] * (3 * CHUNKS + 2),
        out_specs=whole,
        compiler_params=pltpu.CompilerParams(vmem_limit_bytes=VMEM_LIMIT),
        name="image",
    )(*own, *other, src_green, *rcv_own, rcv_other)


def swap_points(array, bit_of):
    points, cores = lax.axis_size("pts"), lax.axis_size("rcv")
    pairs = [(p * cores + c, (p ^ (1 << bit_of[c])) * cores + c) for p in range(points) for c in range(cores)]
    return lax.ppermute(array, ("pts", "rcv"), pairs)


def swap_cores(array):
    return lax.ppermute(array, "rcv", [(0, 1), (1, 0)])


def local(src_green, rcv_green, model, observed):
    points, cores = lax.axis_size("pts"), lax.axis_size("rcv")
    bits = points.bit_length() - 1
    assert points == 1 << bits and cores == 2
    num_points = src_green.shape[2] * points
    count = src_green.shape[1] * rcv_green.shape[1] * cores
    scale = float((num_points / count) ** 0.5)
    me = lax.axis_index("pts").reshape(1)

    model = model.reshape(1, -1)
    resid, rcv_own, rows = [], [], []
    for part in range(CHUNKS):
        out, held, *made = modelled_part(part, me, src_green, model, rcv_green, observed, rows)
        resid.append(out)
        rcv_own.append(held)
        rows = made or rows
    for step in range(bits):
        bit_of = [(step - c) % bits for c in range(cores)]
        resid = [x + swap_points(x, bit_of) for x in resid]
    other = [swap_cores(x) for x in resid]
    rcv_other = swap_cores(rcv_green)
    return image(resid, other, src_green, rcv_own, rcv_other, count, scale).reshape(-1)


def solution(mesh):
    placed = (
        P(None, "grp", "pts"),
        P(None, ("grp", "rcv"), "pts"),
        P(("grp", "pts")),
        P(("grp", "pts"), None, "rcv"),
    )
    return jax.shard_map(
        local, mesh=mesh, in_specs=placed, out_specs=P(("grp", "pts")), check_vma=False
    )
```

time: 104 us -> 26.4 us (0.25)
  blocking collectives: 38.2 us -> 0 us
  waiting for transfers between devices: 40.3 us -> 8.66 us
  between operations: 14.1 us -> 0.05 us
  starting transfers between devices: 0.01 us -> 12.4 us
  matrix products: 6.05 us -> 0 us
  Pallas kernels: 0 us -> 5.05 us
  other arithmetic: 3.97 us -> 0.09 us
  local copies, waits for them, and re-layouts: 1.26 us -> 0.01 us
    psum x1 -> x0, waiting for transfers between devices: 40.3 us -> none  [local(): modelled = lax.psum(modelled_data(scaled, rcv_green), 'pts')]
    all_gather x1 -> x0, blocking collectives: 32.7 us -> none  [local(): all_observed = lax.all_gather(observed, 'pts', axis=0, tiled=True)]
    ppermute x0 -> x9, starting transfers between devices: none -> 12.4 us  [the longest x6 11.4 us: swap_points(): return lax.ppermute(array, ('pts', 'rcv'), pairs)]
    ppermute x0 -> x9, waiting for transfers between devices: none -> 8.66 us  [the longest x6 7.61 us: swap_points(): return lax.ppermute(array, ('pts', 'rcv'), pairs)]
    dot_general x8 -> x0, matrix products: 6.05 us -> none  [the longest x1 1.65 us: modelled_data(): jnp.dot(scaled[0], rcv_green[0].T, precision=highest, preferred_element_t...]
    psum x2 -> x0, blocking collectives: 5.55 us -> none  [the longest x1 3.08 us: local(): total = lax.psum(energy_sum, 'rcv')]
    pallas_call x0 -> x3, Pallas kernels: none -> 5.05 us  [the longest x2 3.58 us: modelled_part(): pl.pallas_call(functools.partial(modelled_kernel, part), out_shape=outs,...]
    mul x2 -> x0, other arithmetic: 1.57 us -> none  [the longest x1 1 us: local(): scaled = src_green * model[None, None, :]]
  transfers between devices with their start and end apart: 1 -> 9, of which waited for: 1 -> 7; matrix products, arithmetic and copies ran while one was open for 0% -> 0% of each run, Pallas kernels for 0% -> 14%
where the time goes in v2:
time: 26.4 us; the launch traced here: 26.2 us
  starting transfers between devices  12.4 us (47%)
  waiting for transfers between devices  8.66 us (33%)
  Pallas kernels  5.05 us (19%)
    ppermute x6, starting transfers between devices, swap_points(): return lax.ppermute(array, ('pts', 'rcv'), pairs)  11.4 us
    ppermute x6, waiting for transfers between devices, swap_points(): return lax.ppermute(array, ('pts', 'rcv'), pairs)  7.61 us
    pallas_call x2, Pallas kernels, modelled_part(): pl.pallas_call(functools.partial(modelled_kernel, part), out_shape=outs,...  3.58 us
    pallas_call x1, Pallas kernels, image(): pl.pallas_call(functools.partial(image_kernel, count, scale), out_shape=j...  1.47 us
    ppermute x3, waiting for transfers between devices, swap_cores(): return lax.ppermute(array, 'rcv', [(0, 1), (1, 0)])  1.05 us
    ppermute x3, starting transfers between devices, swap_cores(): return lax.ppermute(array, 'rcv', [(0, 1), (1, 0)])  1 us
  transfers between devices with their start and end apart: 9, of which 7 were waited for; matrix products, arithmetic and copies ran while one was open for 0% of the time, Pallas kernels for 14%

profile of v2, /device:TPU:0, one launch (start us, length us, event | category | flops | bytes accessed | tf_op | source)
XLA Modules:
  0.0 26.2 jit_solution(18336163923923513043)
XLA Ops:
  0.0 0.5 %collective-permute-start.8 = (f32[2,512,256]{2,1,0:T(8,128)}, f32[2,512,256]{2,1,0:T(8,128)S(1)}, u32[]{:S(2)}, u32[]{:S(2)}) collective-permute-start(f32[2,512,256]{2,1,0:T(8,128)} %rcv_ref.3), channel_id=1, source_target_pairs={{0,1},{1,0},{2,3},{3,2},{4,5},{5,4},{6,7},{7,6},{8,9},{9,8},{10,11... | collective-permute-start | bytes 3145736 | tf_op jit(solution)/shard_map/ppermute | solution.py:163
  0.5 1.9 %modelled_0.1 = (f32[256,128]{1,0:T(8,128)S(1)}, f32[2,256,256]{2,1,0:T(8,128)S(1)}, bf16[2,2,128,256]{3,2,1,0:T(8,128)(2,1)S(1)}) custom-call(s32[1]{0:T(128)} %bitcast.me_ref, f32[2,64,256]{2,1,0:T(8,128)} %refs_4_.1, f32[1,256]{1,0:T(1,128)} %bitcast.3, f32[2,512,256]{2,1,0:T(8,128)} %rcv_ref.3, f32[8,2,512]{2,1,0:T(2,128)} %obs_ref.3), custom_call_target="tpu_custom_call" | custom-call | flops 1000000000 | bytes 4000000 | tf_op jit(solution)/shard_map/modelled_0/pallas_call | solution.py:91
  2.3 2.6 %collective-permute-start = (f32[256,128]{1,0:T(8,128)S(1)}, f32[256,128]{1,0:T(8,128)S(1)}, u32[]{:S(2)}, u32[]{:S(2)}) collective-permute-start(f32[256,128]{1,0:T(8,128)S(1)} %get-tuple-element.10), channel_id=1, source_target_pairs={{0,2},{1,9},{2,0},{3,11},{4,6},{5,13},{6,4},{7,15},{8,10},{9,1},{1... | collective-permute-start | bytes 393224 | tf_op jit(solution)/shard_map/ppermute | solution.py:159
  4.9 1.7 %modelled_1.1 = (f32[256,128]{1,0:T(8,128)S(1)}, f32[2,256,256]{2,1,0:T(8,128)S(1)}) custom-call(s32[1]{0:T(128)} %bitcast.me_ref, f32[2,64,256]{2,1,0:T(8,128)} %refs_4_.1, f32[1,256]{1,0:T(1,128)} %bitcast.4, f32[2,512,256]{2,1,0:T(8,128)} %rcv_ref.3, f32[8,2,512]{2,1,0:T(2,128)} %obs_ref.3, bf16[2,2,128,256]{3,2,1,0:T(8,128)(2,1)S(1)} %get-tuple-element.11.refs_0_), custom_call_target="tpu_custom_call" | custom-call | flops 1000000000 | bytes 4000000 | tf_op jit(solution)/shard_map/modelled_1/pallas_call | solution.py:91
  6.6 0.1 collective-permute-start.3
  6.7 1.1 %collective-permute-done = f32[256,128]{1,0:T(8,128)S(1)} collective-permute-done((f32[256,128]{1,0:T(8,128)S(1)}, f32[256,128]{1,0:T(8,128)S(1)}, u32[]{:S(2)}, u32[]{:S(2)}) %collective-permute-start) | collective-permute-done | bytes 131104 | tf_op jit(solution)/shard_map/ppermute | solution.py:159
  7.8 2.2 %collective-permute-start.1 = (f32[256,128]{1,0:T(8,128)S(1)}, f32[256,128]{1,0:T(8,128)S(1)}, u32[]{:S(2)}, u32[]{:S(2)}) collective-permute-start(f32[256,128]{1,0:T(8,128)S(1)} %add.18), channel_id=1, source_target_pairs={{0,4},{1,3},{2,6},{3,1},{4,0},{5,7},{6,2},{7,5},{8,12},{9,11},{10,... | collective-permute-start | bytes 393224 | tf_op jit(solution)/shard_map/ppermute | solution.py:159
  10.0 1.6 %collective-permute-done.3 = f32[256,128]{1,0:T(8,128)S(1)} collective-permute-done((f32[256,128]{1,0:T(8,128)S(1)}, f32[256,128]{1,0:T(8,128)S(1)}, u32[]{:S(2)}, u32[]{:S(2)}) %collective-permute-start.3) | collective-permute-done | bytes 131104 | tf_op jit(solution)/shard_map/ppermute | solution.py:159
  11.7 1.6 %collective-permute-start.4 = (f32[256,128]{1,0:T(8,128)S(1)}, f32[256,128]{1,0:T(8,128)S(1)}, u32[]{:S(2)}, u32[]{:S(2)}) collective-permute-start(f32[256,128]{1,0:T(8,128)S(1)} %add.21), channel_id=1, source_target_pairs={{0,4},{1,3},{2,6},{3,1},{4,0},{5,7},{6,2},{7,5},{8,12},{9,11},{10,... | collective-permute-start | bytes 393224 | tf_op jit(solution)/shard_map/ppermute | solution.py:159
  13.3 0.7 %collective-permute-done.1 = f32[256,128]{1,0:T(8,128)S(1)} collective-permute-done((f32[256,128]{1,0:T(8,128)S(1)}, f32[256,128]{1,0:T(8,128)S(1)}, u32[]{:S(2)}, u32[]{:S(2)}) %collective-permute-start.1) | collective-permute-done | bytes 131104 | tf_op jit(solution)/shard_map/ppermute | solution.py:159
  14.0 2.1 %collective-permute-start.2 = (f32[256,128]{1,0:T(8,128)S(1)}, f32[256,128]{1,0:T(8,128)S(1)}, u32[]{:S(2)}, u32[]{:S(2)}) collective-permute-start(f32[256,128]{1,0:T(8,128)S(1)} %add.19), channel_id=1, source_target_pairs={{0,8},{1,5},{2,10},{3,7},{4,12},{5,1},{6,14},{7,3},{8,0},{9,13},{1... | collective-permute-start | bytes 393224 | tf_op jit(solution)/shard_map/ppermute | solution.py:159
  16.1 0.6 %collective-permute-done.4 = f32[256,128]{1,0:T(8,128)S(1)} collective-permute-done((f32[256,128]{1,0:T(8,128)S(1)}, f32[256,128]{1,0:T(8,128)S(1)}, u32[]{:S(2)}, u32[]{:S(2)}) %collective-permute-start.4) | collective-permute-done | bytes 131104 | tf_op jit(solution)/shard_map/ppermute | solution.py:159
  16.7 2.9 %collective-permute-start.5 = (f32[256,128]{1,0:T(8,128)S(1)}, f32[256,128]{1,0:T(8,128)S(1)}, u32[]{:S(2)}, u32[]{:S(2)}) collective-permute-start(f32[256,128]{1,0:T(8,128)S(1)} %add.22), channel_id=1, source_target_pairs={{0,8},{1,5},{2,10},{3,7},{4,12},{5,1},{6,14},{7,3},{8,0},{9,13},{1... | collective-permute-start | bytes 393224 | tf_op jit(solution)/shard_map/ppermute | solution.py:159
  19.6 1.3 %collective-permute-done.2 = f32[256,128]{1,0:T(8,128)S(1)} collective-permute-done((f32[256,128]{1,0:T(8,128)S(1)}, f32[256,128]{1,0:T(8,128)S(1)}, u32[]{:S(2)}, u32[]{:S(2)}) %collective-permute-start.2) | collective-permute-done | bytes 131104 | tf_op jit(solution)/shard_map/ppermute | solution.py:159
  20.9 0.0 copy-start
  20.9 0.2 collective-permute-start.6
  21.1 2.3 %collective-permute-done.5 = f32[256,128]{1,0:T(8,128)S(1)} collective-permute-done((f32[256,128]{1,0:T(8,128)S(1)}, f32[256,128]{1,0:T(8,128)S(1)}, u32[]{:S(2)}, u32[]{:S(2)}) %collective-permute-start.5) | collective-permute-done | bytes 131104 | tf_op jit(solution)/shard_map/ppermute | solution.py:159
  23.3 0.4 %collective-permute-start.7 = (f32[256,128]{1,0:T(8,128)S(1)}, f32[256,128]{1,0:T(8,128)S(1)}, u32[]{:S(2)}, u32[]{:S(2)}) collective-permute-start(f32[256,128]{1,0:T(8,128)S(1)} %add.23.refs_1_), channel_id=1, source_target_pairs={{0,1},{1,0},{2,3},{3,2},{4,5},{5,4},{6,7},{7,6},{8,9},{9,8},{10,11... | collective-permute-start | bytes 393224 | tf_op jit(solution)/shard_map/ppermute | solution.py:163
  23.7 0.0 collective-permute-done.6.refs_2_
  23.7 1.0 %collective-permute-done.7.refs_3_ = f32[256,128]{1,0:T(8,128)S(1)} collective-permute-done((f32[256,128]{1,0:T(8,128)S(1)}, f32[256,128]{1,0:T(8,128)S(1)}, u32[]{:S(2)}, u32[]{:S(2)}) %collective-permute-start.7) | collective-permute-done | bytes 131104 | tf_op jit(solution)/shard_map/ppermute | solution.py:163
  24.8 0.0 collective-permute-done.8.refs_7_
  24.8 0.0 copy-done
  24.8 1.5 %image.1 = f32[1,256]{1,0:T(1,128)} custom-call(f32[256,128]{1,0:T(8,128)S(1)} %add.20.refs_0_, f32[256,128]{1,0:T(8,128)S(1)} %add.23.refs_1_, f32[256,128]{1,0:T(8,128)S(1)} %collective-permute-done.6.refs_2_, f32[256,128]{1,0:T(8,128)S(1)} %collective-permute-done.7.refs_3_, f32[2,64,256]{2,1,0:T(8,128)S(1)} %copy-done, ...), custom_call_target="tpu_custom_call" | custom-call | tf_op jit(solution)/shard_map/image/pallas_call | solution.py:146
  (6 shorter events, 0.1 us)
Async XLA Ops:
  0.0 24.8 %collective-permute-start.8 = (f32[2,512,256]{2,1,0:T(8,128)}, f32[2,512,256]{2,1,0:T(8,128)S(1)}, u32[]{:S(2)}, u32[]{:S(2)}) collective-permute-start(f32[2,512,256]{2,1,0:T(8,128)} %rcv_ref.3), channel_id=1, source_target_pairs={{0,1},{1,0},{2,3},{3,2},{4,5},{5,4},{6,7},{7,6},{8,9},{9,8},{10,11... | collective-permute-start | bytes 3145736 | tf_op jit(solution)/shard_map/ppermute | solution.py:163
  2.3 5.5 %collective-permute-start = (f32[256,128]{1,0:T(8,128)S(1)}, f32[256,128]{1,0:T(8,128)S(1)}, u32[]{:S(2)}, u32[]{:S(2)}) collective-permute-start(f32[256,128]{1,0:T(8,128)S(1)} %get-tuple-element.10), channel_id=1, source_target_pairs={{0,2},{1,9},{2,0},{3,11},{4,6},{5,13},{6,4},{7,15},{8,10},{9,1},{1... | collective-permute-start | bytes 393224 | tf_op jit(solution)/shard_map/ppermute | solution.py:159
  6.6 5.0 %collective-permute-start.3 = (f32[256,128]{1,0:T(8,128)S(1)}, f32[256,128]{1,0:T(8,128)S(1)}, u32[]{:S(2)}, u32[]{:S(2)}) collective-permute-start(f32[256,128]{1,0:T(8,128)S(1)} %get-tuple-element.12), channel_id=1, source_target_pairs={{0,2},{1,9},{2,0},{3,11},{4,6},{5,13},{6,4},{7,15},{8,10},{9,1},{1... | collective-permute-start | bytes 393224 | tf_op jit(solution)/shard_map/ppermute | solution.py:159
  7.8 6.2 %collective-permute-start.1 = (f32[256,128]{1,0:T(8,128)S(1)}, f32[256,128]{1,0:T(8,128)S(1)}, u32[]{:S(2)}, u32[]{:S(2)}) collective-permute-start(f32[256,128]{1,0:T(8,128)S(1)} %add.18), channel_id=1, source_target_pairs={{0,4},{1,3},{2,6},{3,1},{4,0},{5,7},{6,2},{7,5},{8,12},{9,11},{10,... | collective-permute-start | bytes 393224 | tf_op jit(solution)/shard_map/ppermute | solution.py:159
  11.7 5.0 %collective-permute-start.4 = (f32[256,128]{1,0:T(8,128)S(1)}, f32[256,128]{1,0:T(8,128)S(1)}, u32[]{:S(2)}, u32[]{:S(2)}) collective-permute-start(f32[256,128]{1,0:T(8,128)S(1)} %add.21), channel_id=1, source_target_pairs={{0,4},{1,3},{2,6},{3,1},{4,0},{5,7},{6,2},{7,5},{8,12},{9,11},{10,... | collective-permute-start | bytes 393224 | tf_op jit(solution)/shard_map/ppermute | solution.py:159
  14.0 6.8 %collective-permute-start.2 = (f32[256,128]{1,0:T(8,128)S(1)}, f32[256,128]{1,0:T(8,128)S(1)}, u32[]{:S(2)}, u32[]{:S(2)}) collective-permute-start(f32[256,128]{1,0:T(8,128)S(1)} %add.19), channel_id=1, source_target_pairs={{0,8},{1,5},{2,10},{3,7},{4,12},{5,1},{6,14},{7,3},{8,0},{9,13},{1... | collective-permute-start | bytes 393224 | tf_op jit(solution)/shard_map/ppermute | solution.py:159
  16.7 6.6 %collective-permute-start.5 = (f32[256,128]{1,0:T(8,128)S(1)}, f32[256,128]{1,0:T(8,128)S(1)}, u32[]{:S(2)}, u32[]{:S(2)}) collective-permute-start(f32[256,128]{1,0:T(8,128)S(1)} %add.22), channel_id=1, source_target_pairs={{0,8},{1,5},{2,10},{3,7},{4,12},{5,1},{6,14},{7,3},{8,0},{9,13},{1... | collective-permute-start | bytes 393224 | tf_op jit(solution)/shard_map/ppermute | solution.py:159
  20.9 3.9 %copy-start = (f32[2,64,256]{2,1,0:T(8,128)S(1)}, f32[2,64,256]{2,1,0:T(8,128)}, u32[]{:S(2)}) copy-start(f32[2,64,256]{2,1,0:T(8,128)} %refs_4_.1) | copy-start | bytes 393220
  20.9 2.8 %collective-permute-start.6 = (f32[256,128]{1,0:T(8,128)S(1)}, f32[256,128]{1,0:T(8,128)S(1)}, u32[]{:S(2)}, u32[]{:S(2)}) collective-permute-start(f32[256,128]{1,0:T(8,128)S(1)} %add.20.refs_0_), channel_id=1, source_target_pairs={{0,1},{1,0},{2,3},{3,2},{4,5},{5,4},{6,7},{7,6},{8,9},{9,8},{10,11... | collective-permute-start | bytes 393224 | tf_op jit(solution)/shard_map/ppermute | solution.py:163
  23.3 1.4 %collective-permute-start.7 = (f32[256,128]{1,0:T(8,128)S(1)}, f32[256,128]{1,0:T(8,128)S(1)}, u32[]{:S(2)}, u32[]{:S(2)}) collective-permute-start(f32[256,128]{1,0:T(8,128)S(1)} %add.23.refs_1_), channel_id=1, source_target_pairs={{0,1},{1,0},{2,3},{3,2},{4,5},{5,4},{6,7},{7,6},{8,9},{9,8},{10,11... | collective-permute-start | bytes 393224 | tf_op jit(solution)/shard_map/ppermute | solution.py:163

commit v3 on v2

v3 whole, which is shorter than its diff:
```python
import functools

import jax
import jax.numpy as jnp
from jax import lax
from jax.experimental import pallas as pl
from jax.experimental.pallas import tpu as pltpu
from jax.sharding import PartitionSpec as P

CHUNKS = 2
LANES_LAST = (((1,), (1,)), ((), ()))
PLAIN = (((1,), (0,)), ((), ()))
VMEM_LIMIT = 24 * 1024 * 1024
SHARE = 8


def split(x):
    high = x.astype(jnp.bfloat16)
    return high, (x - high.astype(jnp.float32)).astype(jnp.bfloat16)


def dot(a, b, dims):
    return lax.dot_general(a, b, dims, preferred_element_type=jnp.float32)


def stacked(real, imag):
    return [jnp.concatenate(rows, axis=0) for rows in ([real, imag], [-imag, real])]


def modelled_rows(me_ref, obs_ref, rcv_ref, rows_ref, out_ref, placed_ref, first, wait):
    receivers = out_ref.shape[0]
    own, sources = obs_ref.shape[0], placed_ref.shape[0] // 2
    placed_ref[...] = jnp.zeros_like(placed_ref)
    for c in range(2):
        start = pl.multiple_of(c * sources + me_ref[0] * own, own)
        placed_ref[pl.ds(start, own), :] = obs_ref[:, c, first : first + receivers]
    total = -placed_ref[...].T
    for c in range(2):
        wait(c)
        high, low = split(rcv_ref[c, first : first + receivers, :])
        total += dot(high, rows_ref[c, 0], LANES_LAST)
        total += dot(high, rows_ref[c, 1], LANES_LAST)
        total += dot(low, rows_ref[c, 0], LANES_LAST)
    out_ref[...] = total


def first_kernel(me_ref, src_ref, model_ref, rcv_ref, obs_ref, *refs):
    out_ref, rcv_out, rows_ref, obs_out, placed_ref, src_held, model_held, sems = refs
    receivers, rest = out_ref.shape[0], rcv_ref.shape[1] - out_ref.shape[0]
    inputs = [
        pltpu.make_async_copy(model_ref, model_held, sems.at[0]),
        pltpu.make_async_copy(src_ref.at[0], src_held.at[0], sems.at[1]),
        pltpu.make_async_copy(src_ref.at[1], src_held.at[1], sems.at[2]),
    ]
    obs_copy = pltpu.make_async_copy(obs_ref, obs_out, sems.at[3])
    pieces = []
    for k, here in enumerate((pl.ds(0, receivers), pl.ds(receivers, rest))):
        for c in range(2):
            pieces.append(
                pltpu.make_async_copy(rcv_ref.at[c, here, :], rcv_out.at[c, here, :], sems.at[4 + 2 * k + c])
            )
    for copy in [*inputs, obs_copy, *pieces]:
        copy.start()
    for copy in inputs:
        copy.wait()
    model = model_held[...]
    for c, rows in enumerate(stacked(src_held[0] * model, src_held[1] * model)):
        rows_ref[c, 0], rows_ref[c, 1] = split(rows)
    obs_copy.wait()
    modelled_rows(me_ref, obs_out, rcv_out, rows_ref, out_ref, placed_ref, 0, lambda c: pieces[c].wait())
    for copy in pieces[2:]:
        copy.wait()


def next_kernel(first, me_ref, obs_ref, rcv_ref, rows_ref, out_ref, placed_ref):
    modelled_rows(me_ref, obs_ref, rcv_ref, rows_ref, out_ref, placed_ref, first, lambda c: None)


def modelled_parts(me, src_green, model, rcv_green, observed):
    _, sources, points = src_green.shape
    first = rcv_green.shape[1] * SHARE // 16
    sizes = [first, rcv_green.shape[1] - first]
    in_vmem, in_smem = pl.BlockSpec(memory_space=pltpu.VMEM), pl.BlockSpec(memory_space=pltpu.SMEM)
    params = pltpu.CompilerParams(vmem_limit_bytes=VMEM_LIMIT)
    outs = [jax.ShapeDtypeStruct((size, 2 * sources), jnp.float32) for size in sizes]
    placed = [pltpu.VMEM((2 * sources, size), jnp.float32) for size in sizes]
    inputs = [pltpu.with_memory_space_constraint(x, pltpu.HBM) for x in (src_green, model, rcv_green, observed)]
    resid, rcv_held, rows, obs_held = pl.pallas_call(
        first_kernel,
        out_shape=[
            outs[0],
            jax.ShapeDtypeStruct(rcv_green.shape, jnp.float32),
            jax.ShapeDtypeStruct((2, 2, 2 * sources, points), jnp.bfloat16),
            jax.ShapeDtypeStruct(observed.shape, jnp.float32),
        ],
        in_specs=[in_smem] + [pl.BlockSpec(memory_space=pltpu.HBM)] * 4,
        out_specs=[in_vmem] * 4,
        scratch_shapes=[
            placed[0],
            pltpu.VMEM(src_green.shape, jnp.float32),
            pltpu.VMEM(model.shape, jnp.float32),
            pltpu.SemaphoreType.DMA((8,)),
        ],
        compiler_params=params,
        name="modelled_0",
    )(me, *inputs)
    last = pl.pallas_call(
        functools.partial(next_kernel, first),
        out_shape=outs[1],
        in_specs=[in_smem] + [in_vmem] * 3,
        out_specs=in_vmem,
        scratch_shapes=[placed[1]],
        compiler_params=params,
        cost_estimate=pl.CostEstimate(flops=10**9, bytes_accessed=4 * 10**6, transcendentals=0),
        name="modelled_1",
    )(me, obs_held, rcv_held, rows)
    return [resid, last], rcv_held


def image_kernel(count, scale, firsts, *refs):
    resid = [refs[:CHUNKS], refs[CHUNKS : 2 * CHUNKS]]
    src_ref, *rcv = refs[2 * CHUNKS : 2 * CHUNKS + 3]
    out_ref = refs[-1]
    sources, points = src_ref.shape[1:]

    def energy(group):
        total = jnp.zeros((8, 2 * sources), jnp.float32)
        for ref in group:
            total += jnp.sum((ref[...] ** 2).reshape(-1, 8, 2 * sources), axis=0)
        return jnp.sum(total)

    spread_sq = (energy(resid[0]) + energy(resid[1])) / count + 1e-06
    stacks = []
    for part in ([src_ref[0], src_ref[1]], [-src_ref[1], src_ref[0]]):
        high, low = split(jnp.concatenate(part, axis=0))
        stacks.append((jnp.concatenate([high, high], axis=0), low))

    sums = []
    for group, rcv_ref in zip(resid, rcv):
        total = jnp.zeros((8, points), jnp.float32)
        for first, ref in zip(firsts, group):
            here = ref[...]
            square = here * here
            both = square + pltpu.roll(square, sources, 1)
            weighted_high, weighted_low = split(here / (1.0 + both / spread_sq))
            wide = jnp.concatenate([weighted_high, weighted_low], axis=1)
            for c, (double, low) in enumerate(stacks):
                terms = dot(wide, double, PLAIN) + dot(weighted_high, low, PLAIN)
                terms = terms * rcv_ref[c, first : first + here.shape[0], :]
                total += jnp.sum(terms.reshape(-1, 8, points), axis=0)
        sums.append(jnp.sum(total, axis=0, keepdims=True))
    out_ref[...] = (sums[0] + sums[1]) * scale


def image(own, other, src_green, rcv_own, rcv_other, count, scale):
    firsts = [own[0].shape[0], 0]
    points = src_green.shape[2]
    whole = pl.BlockSpec(memory_space=pltpu.VMEM)
    return pl.pallas_call(
        functools.partial(image_kernel, count, scale, firsts),
        out_shape=jax.ShapeDtypeStruct((1, points), jnp.float32),
        in_specs=[whole] * (2 * CHUNKS + 3),
        out_specs=whole,
        compiler_params=pltpu.CompilerParams(vmem_limit_bytes=VMEM_LIMIT),
        name="image",
    )(*reversed(own), *reversed(other), src_green, rcv_own, rcv_other)


def swap_points(array, bit_of):
    points, cores = lax.axis_size("pts"), lax.axis_size("rcv")
    pairs = [(p * cores + c, (p ^ (1 << bit_of[c])) * cores + c) for p in range(points) for c in range(cores)]
    return lax.ppermute(array, ("pts", "rcv"), pairs)


def swap_cores(array):
    return lax.ppermute(array, "rcv", [(0, 1), (1, 0)])


def local(src_green, rcv_green, model, observed):
    points, cores = lax.axis_size("pts"), lax.axis_size("rcv")
    bits = points.bit_length() - 1
    assert points == 1 << bits and cores == 2
    num_points = src_green.shape[2] * points
    count = src_green.shape[1] * rcv_green.shape[1] * cores
    scale = float((num_points / count) ** 0.5)
    me = lax.axis_index("pts").reshape(1)

    model = model.reshape(1, -1)
    resid, rcv_own = modelled_parts(me, src_green, model, rcv_green, observed)
    for step in range(bits):
        bit_of = [(step - c) % bits for c in range(cores)]
        resid = [x + swap_points(x, bit_of) for x in resid]
    other = [swap_cores(x) for x in resid]
    rcv_other = swap_cores(rcv_green)
    return image(resid, other, src_green, rcv_own, rcv_other, count, scale).reshape(-1)


def solution(mesh):
    placed = (
        P(None, "grp", "pts"),
        P(None, ("grp", "rcv"), "pts"),
        P(("grp", "pts")),
        P(("grp", "pts"), None, "rcv"),
    )
    return jax.shard_map(
        local, mesh=mesh, in_specs=placed, out_specs=P(("grp", "pts")), check_vma=False
    )
```

time: 26.4 us -> 26 us (0.985)
  Pallas kernels: 5.05 us -> 3.66 us
  waiting for transfers between devices: 8.66 us -> 9.6 us
    pallas_call x3, Pallas kernels: 5.05 us -> 3.66 us  [the longest x1 1.84 us: modelled_parts(): pl.pallas_call(first_kernel, out_shape=[outs[0], jax.ShapeDtypeStruct(rcv...]
    ppermute x6, waiting for transfers between devices: 7.61 us -> 8.45 us  [swap_points(): return lax.ppermute(array, ('pts', 'rcv'), pairs)]
  transfers between devices with their start and end apart: 9 -> 9, of which waited for: 7 -> 6; matrix products, arithmetic and copies ran while one was open for 0% -> 0% of each run, Pallas kernels for 14% -> 9%
where the time goes in v3:
time: 26 us; the launch traced here: 25.6 us
  starting transfers between devices  12.2 us (47%)
  waiting for transfers between devices  9.6 us (37%)
  Pallas kernels  3.66 us (14%)
    ppermute x6, starting transfers between devices, swap_points(): return lax.ppermute(array, ('pts', 'rcv'), pairs)  11.2 us
    ppermute x6, waiting for transfers between devices, swap_points(): return lax.ppermute(array, ('pts', 'rcv'), pairs)  8.45 us
    pallas_call x1, Pallas kernels, modelled_parts(): pl.pallas_call(first_kernel, out_shape=[outs[0], jax.ShapeDtypeStruct(rcv...  1.84 us
    pallas_call x1, Pallas kernels, image(): pl.pallas_call(functools.partial(image_kernel, count, scale, firsts), out...  1.46 us
    ppermute x3, waiting for transfers between devices, swap_cores(): return lax.ppermute(array, 'rcv', [(0, 1), (1, 0)])  1.16 us
    ppermute x3, starting transfers between devices, swap_cores(): return lax.ppermute(array, 'rcv', [(0, 1), (1, 0)])  1.05 us
  transfers between devices with their start and end apart: 9, of which 6 were waited for; matrix products, arithmetic and copies ran while one was open for 0% of the time, Pallas kernels for 9%

profile of v3, /device:TPU:0, one launch (start us, length us, event | category | flops | bytes accessed | tf_op | source)
XLA Modules:
  0.0 25.6 jit_solution(172033925611787186)
XLA Ops:
  0.0 0.5 %collective-permute-start.8 = (f32[2,512,256]{2,1,0:T(8,128)}, f32[2,512,256]{2,1,0:T(8,128)S(1)}, u32[]{:S(2)}, u32[]{:S(2)}) collective-permute-start(f32[2,512,256]{2,1,0:T(8,128)} %rcv_ref.1), channel_id=1, source_target_pairs={{0,1},{1,0},{2,3},{3,2},{4,5},{5,4},{6,7},{7,6},{8,9},{9,8},{10,11... | collective-permute-start | bytes 3145736 | tf_op jit(solution)/shard_map/ppermute | solution.py:176
  0.5 1.8 %modelled_0.1 = (f32[256,128]{1,0:T(8,128)S(1)}, f32[2,512,256]{2,1,0:T(8,128)S(1)}, bf16[2,2,128,256]{3,2,1,0:T(8,128)(2,1)S(1)}, f32[8,2,512]{2,1,0:T(2,128)S(1)}) custom-call(s32[1]{0:T(128)} %bitcast.me_ref, f32[2,64,256]{2,1,0:T(8,128)} %refs_4_.1, f32[1,256]{1,0:T(1,128)} %bitcast.3, f32[2,512,256]{2,1,0:T(8,128)} %rcv_ref.1, f32[8,2,512]{2,1,0:T(2,128)} %obs_ref.1), custom_call_target="tpu_custom_call" | custom-call | tf_op jit(solution)/shard_map/modelled_0/pallas_call | solution.py:88
  2.3 2.6 %collective-permute-start.3 = (f32[256,128]{1,0:T(8,128)S(1)}, f32[256,128]{1,0:T(8,128)S(1)}, u32[]{:S(2)}, u32[]{:S(2)}) collective-permute-start(f32[256,128]{1,0:T(8,128)S(1)} %get-tuple-element.12), channel_id=1, source_target_pairs={{0,2},{1,9},{2,0},{3,11},{4,6},{5,13},{6,4},{7,15},{8,10},{9,1},{1... | collective-permute-start | bytes 393224 | tf_op jit(solution)/shard_map/ppermute | solution.py:172
  4.9 0.4 %modelled_1.1 = f32[256,128]{1,0:T(8,128)S(1)} custom-call(s32[1]{0:T(128)} %bitcast.me_ref, f32[8,2,512]{2,1,0:T(2,128)S(1)} %get-tuple-element.9.obs_ref, f32[2,512,256]{2,1,0:T(8,128)S(1)} %get-tuple-element.10.rcv_ref.refs_5_, bf16[2,2,128,256]{3,2,1,0:T(8,128)(2,1)S(1)} %get-tuple-element.11.rows_ref), custom_call_target="tpu_custom_call" | custom-call | flops 1000000000 | bytes 4000000 | tf_op jit(solution)/shard_map/modelled_1/pallas_call | solution.py:107
  5.2 0.1 collective-permute-start
  5.3 2.5 %collective-permute-done.3 = f32[256,128]{1,0:T(8,128)S(1)} collective-permute-done((f32[256,128]{1,0:T(8,128)S(1)}, f32[256,128]{1,0:T(8,128)S(1)}, u32[]{:S(2)}, u32[]{:S(2)}) %collective-permute-start.3) | collective-permute-done | bytes 131104 | tf_op jit(solution)/shard_map/ppermute | solution.py:172
  7.8 2.2 %collective-permute-start.4 = (f32[256,128]{1,0:T(8,128)S(1)}, f32[256,128]{1,0:T(8,128)S(1)}, u32[]{:S(2)}, u32[]{:S(2)}) collective-permute-start(f32[256,128]{1,0:T(8,128)S(1)} %add.21), channel_id=1, source_target_pairs={{0,4},{1,3},{2,6},{3,1},{4,0},{5,7},{6,2},{7,5},{8,12},{9,11},{10,... | collective-permute-start | bytes 393224 | tf_op jit(solution)/shard_map/ppermute | solution.py:172
  10.0 0.3 %collective-permute-done = f32[256,128]{1,0:T(8,128)S(1)} collective-permute-done((f32[256,128]{1,0:T(8,128)S(1)}, f32[256,128]{1,0:T(8,128)S(1)}, u32[]{:S(2)}, u32[]{:S(2)}) %collective-permute-start) | collective-permute-done | bytes 131104 | tf_op jit(solution)/shard_map/ppermute | solution.py:172
  10.3 1.6 %collective-permute-start.1 = (f32[256,128]{1,0:T(8,128)S(1)}, f32[256,128]{1,0:T(8,128)S(1)}, u32[]{:S(2)}, u32[]{:S(2)}) collective-permute-start(f32[256,128]{1,0:T(8,128)S(1)} %add.18), channel_id=1, source_target_pairs={{0,4},{1,3},{2,6},{3,1},{4,0},{5,7},{6,2},{7,5},{8,12},{9,11},{10,... | collective-permute-start | bytes 393224 | tf_op jit(solution)/shard_map/ppermute | solution.py:172
  11.9 1.3 %collective-permute-done.4 = f32[256,128]{1,0:T(8,128)S(1)} collective-permute-done((f32[256,128]{1,0:T(8,128)S(1)}, f32[256,128]{1,0:T(8,128)S(1)}, u32[]{:S(2)}, u32[]{:S(2)}) %collective-permute-start.4) | collective-permute-done | bytes 131104 | tf_op jit(solution)/shard_map/ppermute | solution.py:172
  13.3 2.8 %collective-permute-start.5 = (f32[256,128]{1,0:T(8,128)S(1)}, f32[256,128]{1,0:T(8,128)S(1)}, u32[]{:S(2)}, u32[]{:S(2)}) collective-permute-start(f32[256,128]{1,0:T(8,128)S(1)} %add.22), channel_id=1, source_target_pairs={{0,8},{1,5},{2,10},{3,7},{4,12},{5,1},{6,14},{7,3},{8,0},{9,13},{1... | collective-permute-start | bytes 393224 | tf_op jit(solution)/shard_map/ppermute | solution.py:172
  16.1 0.0 collective-permute-done.1
  16.1 1.9 %collective-permute-start.2 = (f32[256,128]{1,0:T(8,128)S(1)}, f32[256,128]{1,0:T(8,128)S(1)}, u32[]{:S(2)}, u32[]{:S(2)}) collective-permute-start(f32[256,128]{1,0:T(8,128)S(1)} %add.19), channel_id=1, source_target_pairs={{0,8},{1,5},{2,10},{3,7},{4,12},{5,1},{6,14},{7,3},{8,0},{9,13},{1... | collective-permute-start | bytes 393224 | tf_op jit(solution)/shard_map/ppermute | solution.py:172
  18.0 1.9 %collective-permute-done.5 = f32[256,128]{1,0:T(8,128)S(1)} collective-permute-done((f32[256,128]{1,0:T(8,128)S(1)}, f32[256,128]{1,0:T(8,128)S(1)}, u32[]{:S(2)}, u32[]{:S(2)}) %collective-permute-start.5) | collective-permute-done | bytes 131104 | tf_op jit(solution)/shard_map/ppermute | solution.py:172
  19.9 0.0 copy-start
  19.9 0.3 %collective-permute-start.7 = (f32[256,128]{1,0:T(8,128)S(1)}, f32[256,128]{1,0:T(8,128)S(1)}, u32[]{:S(2)}, u32[]{:S(2)}) collective-permute-start(f32[256,128]{1,0:T(8,128)S(1)} %add.23.refs_1_), channel_id=1, source_target_pairs={{0,1},{1,0},{2,3},{3,2},{4,5},{5,4},{6,7},{7,6},{8,9},{9,8},{10,11... | collective-permute-start | bytes 393224 | tf_op jit(solution)/shard_map/ppermute | solution.py:176
  20.2 2.5 %collective-permute-done.2 = f32[256,128]{1,0:T(8,128)S(1)} collective-permute-done((f32[256,128]{1,0:T(8,128)S(1)}, f32[256,128]{1,0:T(8,128)S(1)}, u32[]{:S(2)}, u32[]{:S(2)}) %collective-permute-start.2) | collective-permute-done | bytes 131104 | tf_op jit(solution)/shard_map/ppermute | solution.py:172
  22.8 0.3 %collective-permute-start.6 = (f32[256,128]{1,0:T(8,128)S(1)}, f32[256,128]{1,0:T(8,128)S(1)}, u32[]{:S(2)}, u32[]{:S(2)}) collective-permute-start(f32[256,128]{1,0:T(8,128)S(1)} %add.20.refs_0_), channel_id=1, source_target_pairs={{0,1},{1,0},{2,3},{3,2},{4,5},{5,4},{6,7},{7,6},{8,9},{9,8},{10,11... | collective-permute-start | bytes 393224 | tf_op jit(solution)/shard_map/ppermute | solution.py:176
  23.0 0.0 collective-permute-done.7.refs_3_
  23.0 1.2 %collective-permute-done.6.refs_2_ = f32[256,128]{1,0:T(8,128)S(1)} collective-permute-done((f32[256,128]{1,0:T(8,128)S(1)}, f32[256,128]{1,0:T(8,128)S(1)}, u32[]{:S(2)}, u32[]{:S(2)}) %collective-permute-start.6) | collective-permute-done | bytes 131104 | tf_op jit(solution)/shard_map/ppermute | solution.py:176
  24.2 0.0 collective-permute-done.8.refs_6_
  24.2 0.0 copy-done
  24.2 1.5 %image.1 = f32[1,256]{1,0:T(1,128)} custom-call(f32[256,128]{1,0:T(8,128)S(1)} %add.20.refs_0_, f32[256,128]{1,0:T(8,128)S(1)} %add.23.refs_1_, f32[256,128]{1,0:T(8,128)S(1)} %collective-permute-done.6.refs_2_, f32[256,128]{1,0:T(8,128)S(1)} %collective-permute-done.7.refs_3_, f32[2,64,256]{2,1,0:T(8,128)S(1)} %copy-done, ...), custom_call_target="tpu_custom_call" | custom-call | tf_op jit(solution)/shard_map/image/pallas_call | solution.py:159
  (6 shorter events, 0.1 us)
Async XLA Ops:
  0.0 24.2 %collective-permute-start.8 = (f32[2,512,256]{2,1,0:T(8,128)}, f32[2,512,256]{2,1,0:T(8,128)S(1)}, u32[]{:S(2)}, u32[]{:S(2)}) collective-permute-start(f32[2,512,256]{2,1,0:T(8,128)} %rcv_ref.1), channel_id=1, source_target_pairs={{0,1},{1,0},{2,3},{3,2},{4,5},{5,4},{6,7},{7,6},{8,9},{9,8},{10,11... | collective-permute-start | bytes 3145736 | tf_op jit(solution)/shard_map/ppermute | solution.py:176
  2.3 5.5 %collective-permute-start.3 = (f32[256,128]{1,0:T(8,128)S(1)}, f32[256,128]{1,0:T(8,128)S(1)}, u32[]{:S(2)}, u32[]{:S(2)}) collective-permute-start(f32[256,128]{1,0:T(8,128)S(1)} %get-tuple-element.12), channel_id=1, source_target_pairs={{0,2},{1,9},{2,0},{3,11},{4,6},{5,13},{6,4},{7,15},{8,10},{9,1},{1... | collective-permute-start | bytes 393224 | tf_op jit(solution)/shard_map/ppermute | solution.py:172
  5.2 5.0 %collective-permute-start = (f32[256,128]{1,0:T(8,128)S(1)}, f32[256,128]{1,0:T(8,128)S(1)}, u32[]{:S(2)}, u32[]{:S(2)}) collective-permute-start(f32[256,128]{1,0:T(8,128)S(1)} %modelled_1.1), channel_id=1, source_target_pairs={{0,2},{1,9},{2,0},{3,11},{4,6},{5,13},{6,4},{7,15},{8,10},{9,1},{1... | collective-permute-start | bytes 393224 | tf_op jit(solution)/shard_map/ppermute | solution.py:172
  7.8 5.4 %collective-permute-start.4 = (f32[256,128]{1,0:T(8,128)S(1)}, f32[256,128]{1,0:T(8,128)S(1)}, u32[]{:S(2)}, u32[]{:S(2)}) collective-permute-start(f32[256,128]{1,0:T(8,128)S(1)} %add.21), channel_id=1, source_target_pairs={{0,4},{1,3},{2,6},{3,1},{4,0},{5,7},{6,2},{7,5},{8,12},{9,11},{10,... | collective-permute-start | bytes 393224 | tf_op jit(solution)/shard_map/ppermute | solution.py:172
  10.3 5.8 %collective-permute-start.1 = (f32[256,128]{1,0:T(8,128)S(1)}, f32[256,128]{1,0:T(8,128)S(1)}, u32[]{:S(2)}, u32[]{:S(2)}) collective-permute-start(f32[256,128]{1,0:T(8,128)S(1)} %add.18), channel_id=1, source_target_pairs={{0,4},{1,3},{2,6},{3,1},{4,0},{5,7},{6,2},{7,5},{8,12},{9,11},{10,... | collective-permute-start | bytes 393224 | tf_op jit(solution)/shard_map/ppermute | solution.py:172
  13.3 6.6 %collective-permute-start.5 = (f32[256,128]{1,0:T(8,128)S(1)}, f32[256,128]{1,0:T(8,128)S(1)}, u32[]{:S(2)}, u32[]{:S(2)}) collective-permute-start(f32[256,128]{1,0:T(8,128)S(1)} %add.22), channel_id=1, source_target_pairs={{0,8},{1,5},{2,10},{3,7},{4,12},{5,1},{6,14},{7,3},{8,0},{9,13},{1... | collective-permute-start | bytes 393224 | tf_op jit(solution)/shard_map/ppermute | solution.py:172
  16.1 6.7 %collective-permute-start.2 = (f32[256,128]{1,0:T(8,128)S(1)}, f32[256,128]{1,0:T(8,128)S(1)}, u32[]{:S(2)}, u32[]{:S(2)}) collective-permute-start(f32[256,128]{1,0:T(8,128)S(1)} %add.19), channel_id=1, source_target_pairs={{0,8},{1,5},{2,10},{3,7},{4,12},{5,1},{6,14},{7,3},{8,0},{9,13},{1... | collective-permute-start | bytes 393224 | tf_op jit(solution)/shard_map/ppermute | solution.py:172
  19.9 4.3 %copy-start = (f32[2,64,256]{2,1,0:T(8,128)S(1)}, f32[2,64,256]{2,1,0:T(8,128)}, u32[]{:S(2)}) copy-start(f32[2,64,256]{2,1,0:T(8,128)} %refs_4_.1) | copy-start | bytes 393220
  19.9 3.1 %collective-permute-start.7 = (f32[256,128]{1,0:T(8,128)S(1)}, f32[256,128]{1,0:T(8,128)S(1)}, u32[]{:S(2)}, u32[]{:S(2)}) collective-permute-start(f32[256,128]{1,0:T(8,128)S(1)} %add.23.refs_1_), channel_id=1, source_target_pairs={{0,1},{1,0},{2,3},{3,2},{4,5},{5,4},{6,7},{7,6},{8,9},{9,8},{10,11... | collective-permute-start | bytes 393224 | tf_op jit(solution)/shard_map/ppermute | solution.py:176
  22.8 1.4 %collective-permute-start.6 = (f32[256,128]{1,0:T(8,128)S(1)}, f32[256,128]{1,0:T(8,128)S(1)}, u32[]{:S(2)}, u32[]{:S(2)}) collective-permute-start(f32[256,128]{1,0:T(8,128)S(1)} %add.20.refs_0_), channel_id=1, source_target_pairs={{0,1},{1,0},{2,3},{3,2},{4,5},{5,4},{6,7},{7,6},{8,9},{9,8},{10,11... | collective-permute-start | bytes 393224 | tf_op jit(solution)/shard_map/ppermute | solution.py:176

commit v4 on v3

--- a/solution.py
+++ b/solution.py
@@ -30,18 +30,19 @@
 def modelled_rows(me_ref, obs_ref, rcv_ref, rows_ref, out_ref, placed_ref, first, wait):
     receivers = out_ref.shape[0]
     own, sources = obs_ref.shape[0], placed_ref.shape[0] // 2
+    width = 2 * sources
+    total = jnp.zeros((receivers, width), jnp.float32)
+    for c in range(2):
+        wait(c)
+        high, low = split(rcv_ref[c, first : first + receivers, :])
+        both = dot(high, rows_ref[c], LANES_LAST)
+        total += both[:, :width] + both[:, width:]
+        total += dot(low, rows_ref[c, :width], LANES_LAST)
     placed_ref[...] = jnp.zeros_like(placed_ref)
     for c in range(2):
         start = pl.multiple_of(c * sources + me_ref[0] * own, own)
         placed_ref[pl.ds(start, own), :] = obs_ref[:, c, first : first + receivers]
-    total = -placed_ref[...].T
-    for c in range(2):
-        wait(c)
-        high, low = split(rcv_ref[c, first : first + receivers, :])
-        total += dot(high, rows_ref[c, 0], LANES_LAST)
-        total += dot(high, rows_ref[c, 1], LANES_LAST)
-        total += dot(low, rows_ref[c, 0], LANES_LAST)
-    out_ref[...] = total
+    out_ref[...] = total - placed_ref[...].T
 
 
 def first_kernel(me_ref, src_ref, model_ref, rcv_ref, obs_ref, *refs):
@@ -59,13 +60,13 @@
             pieces.append(
                 pltpu.make_async_copy(rcv_ref.at[c, here, :], rcv_out.at[c, here, :], sems.at[4 + 2 * k + c])
             )
-    for copy in [*inputs, obs_copy, *pieces]:
+    for copy in [*inputs, *pieces[:2], obs_copy, *pieces[2:]]:
         copy.start()
     for copy in inputs:
         copy.wait()
     model = model_held[...]
     for c, rows in enumerate(stacked(src_held[0] * model, src_held[1] * model)):
-        rows_ref[c, 0], rows_ref[c, 1] = split(rows)
+        rows_ref[c, : rows.shape[0]], rows_ref[c, rows.shape[0] :] = split(rows)
     obs_copy.wait()
     modelled_rows(me_ref, obs_out, rcv_out, rows_ref, out_ref, placed_ref, 0, lambda c: pieces[c].wait())
     for copy in pieces[2:]:
@@ -90,7 +91,7 @@
         out_shape=[
             outs[0],
             jax.ShapeDtypeStruct(rcv_green.shape, jnp.float32),
-            jax.ShapeDtypeStruct((2, 2, 2 * sources, points), jnp.bfloat16),
+            jax.ShapeDtypeStruct((2, 4 * sources, points), jnp.bfloat16),
             jax.ShapeDtypeStruct(observed.shape, jnp.float32),
         ],
         in_specs=[in_smem] + [pl.BlockSpec(memory_space=pltpu.HBM)] * 4,
@@ -187,9 +188,12 @@
 
     model = model.reshape(1, -1)
     resid, rcv_own = modelled_parts(me, src_green, model, rcv_green, observed)
+    up = list(range(bits))
+    orders = [[up, up[::-1]], [up[:1] + up[:0:-1], up[::-1]]]
     for step in range(bits):
-        bit_of = [(step - c) % bits for c in range(cores)]
-        resid = [x + swap_points(x, bit_of) for x in resid]
+        resid = [
+            x + swap_points(x, [order[step] for order in by_core]) for x, by_core in zip(resid, orders)
+        ]
     other = [swap_cores(x) for x in resid]
     rcv_other = swap_cores(rcv_green)
     return image(resid, other, src_green, rcv_own, rcv_other, count, scale).reshape(-1)

time: 26 us -> 25 us (0.962)
  waiting for transfers between devices: 9.6 us -> 7.45 us
  starting transfers between devices: 12.2 us -> 13.8 us
    ppermute x6, waiting for transfers between devices: 8.45 us -> 6.12 us  [swap_points(): return lax.ppermute(array, ('pts', 'rcv'), pairs)]
    ppermute x6, starting transfers between devices: 11.2 us -> 12.8 us  [swap_points(): return lax.ppermute(array, ('pts', 'rcv'), pairs)]
  transfers between devices with their start and end apart: 9 -> 9, of which waited for: 6 -> 7; matrix products, arithmetic and copies ran while one was open for 0% -> 0% of each run, Pallas kernels for 9% -> 8%
where the time goes in v4:
time: 25 us; the launch traced here: 24.8 us
  starting transfers between devices  13.8 us (55%)
  waiting for transfers between devices  7.45 us (30%)
  Pallas kernels  3.42 us (14%)
    ppermute x6, starting transfers between devices, swap_points(): return lax.ppermute(array, ('pts', 'rcv'), pairs)  12.8 us
    ppermute x6, waiting for transfers between devices, swap_points(): return lax.ppermute(array, ('pts', 'rcv'), pairs)  6.12 us
    pallas_call x1, Pallas kernels, modelled_parts(): pl.pallas_call(first_kernel, out_shape=[outs[0], jax.ShapeDtypeStruct(rcv...  1.65 us
    pallas_call x1, Pallas kernels, image(): pl.pallas_call(functools.partial(image_kernel, count, scale, firsts), out...  1.46 us
    ppermute x3, waiting for transfers between devices, swap_cores(): return lax.ppermute(array, 'rcv', [(0, 1), (1, 0)])  1.33 us
    ppermute x3, starting transfers between devices, swap_cores(): return lax.ppermute(array, 'rcv', [(0, 1), (1, 0)])  0.98 us
  transfers between devices with their start and end apart: 9, of which 7 were waited for; matrix products, arithmetic and copies ran while one was open for 0% of the time, Pallas kernels for 8%

profile of v4, /device:TPU:0, one launch (start us, length us, event | category | flops | bytes accessed | tf_op | source)
XLA Modules:
  0.0 24.8 jit_solution(3398805423966306265)
XLA Ops:
  0.0 0.5 %collective-permute-start.8 = (f32[2,512,256]{2,1,0:T(8,128)}, f32[2,512,256]{2,1,0:T(8,128)S(1)}, u32[]{:S(2)}, u32[]{:S(2)}) collective-permute-start(f32[2,512,256]{2,1,0:T(8,128)} %rcv_ref.1), channel_id=1, source_target_pairs={{0,1},{1,0},{2,3},{3,2},{4,5},{5,4},{6,7},{7,6},{8,9},{9,8},{10,11... | collective-permute-start | bytes 3145736 | tf_op jit(solution)/shard_map/ppermute | solution.py:177
  0.5 1.6 %modelled_0.1 = (f32[256,128]{1,0:T(8,128)S(1)}, f32[2,512,256]{2,1,0:T(8,128)S(1)}, bf16[2,256,256]{2,1,0:T(8,128)(2,1)S(1)}, f32[8,2,512]{2,1,0:T(2,128)S(1)}) custom-call(s32[1]{0:T(128)} %bitcast.me_ref, f32[2,64,256]{2,1,0:T(8,128)} %refs_4_.1, f32[1,256]{1,0:T(1,128)} %bitcast.3, f32[2,512,256]{2,1,0:T(8,128)} %rcv_ref.1, f32[8,2,512]{2,1,0:T(2,128)} %obs_ref.1), custom_call_target="tpu_custom_call" | custom-call | tf_op jit(solution)/shard_map/modelled_0/pallas_call | solution.py:89
  2.1 2.6 %collective-permute-start.3 = (f32[256,128]{1,0:T(8,128)S(1)}, f32[256,128]{1,0:T(8,128)S(1)}, u32[]{:S(2)}, u32[]{:S(2)}) collective-permute-start(f32[256,128]{1,0:T(8,128)S(1)} %get-tuple-element.12), channel_id=1, source_target_pairs={{0,2},{1,9},{2,0},{3,11},{4,6},{5,13},{6,4},{7,15},{8,10},{9,1},{1... | collective-permute-start | bytes 393224 | tf_op jit(solution)/shard_map/ppermute | solution.py:173
  4.7 0.3 %modelled_1.1 = f32[256,128]{1,0:T(8,128)S(1)} custom-call(s32[1]{0:T(128)} %bitcast.me_ref, f32[8,2,512]{2,1,0:T(2,128)S(1)} %get-tuple-element.9.obs_ref, f32[2,512,256]{2,1,0:T(8,128)S(1)} %get-tuple-element.10.rcv_ref.refs_5_, bf16[2,256,256]{2,1,0:T(8,128)(2,1)S(1)} %get-tuple-element.11.rows_ref), custom_call_target="tpu_custom_call" | custom-call | flops 1000000000 | bytes 4000000 | tf_op jit(solution)/shard_map/modelled_1/pallas_call | solution.py:108
  5.0 0.1 collective-permute-start
  5.1 2.5 %collective-permute-done.3 = f32[256,128]{1,0:T(8,128)S(1)} collective-permute-done((f32[256,128]{1,0:T(8,128)S(1)}, f32[256,128]{1,0:T(8,128)S(1)}, u32[]{:S(2)}, u32[]{:S(2)}) %collective-permute-start.3) | collective-permute-done | bytes 131104 | tf_op jit(solution)/shard_map/ppermute | solution.py:173
  7.6 2.2 %collective-permute-start.4 = (f32[256,128]{1,0:T(8,128)S(1)}, f32[256,128]{1,0:T(8,128)S(1)}, u32[]{:S(2)}, u32[]{:S(2)}) collective-permute-start(f32[256,128]{1,0:T(8,128)S(1)} %add.21), channel_id=1, source_target_pairs={{0,4},{1,5},{2,6},{3,7},{4,0},{5,1},{6,2},{7,3},{8,12},{9,13},{10,... | collective-permute-start | bytes 393224 | tf_op jit(solution)/shard_map/ppermute | solution.py:173
  9.8 0.2 collective-permute-done
  10.0 2.7 %collective-permute-start.1 = (f32[256,128]{1,0:T(8,128)S(1)}, f32[256,128]{1,0:T(8,128)S(1)}, u32[]{:S(2)}, u32[]{:S(2)}) collective-permute-start(f32[256,128]{1,0:T(8,128)S(1)} %add.18), channel_id=1, source_target_pairs={{0,8},{1,5},{2,10},{3,7},{4,12},{5,1},{6,14},{7,3},{8,0},{9,13},{1... | collective-permute-start | bytes 393224 | tf_op jit(solution)/shard_map/ppermute | solution.py:173
  12.7 0.4 %collective-permute-done.4 = f32[256,128]{1,0:T(8,128)S(1)} collective-permute-done((f32[256,128]{1,0:T(8,128)S(1)}, f32[256,128]{1,0:T(8,128)S(1)}, u32[]{:S(2)}, u32[]{:S(2)}) %collective-permute-start.4) | collective-permute-done | bytes 131104 | tf_op jit(solution)/shard_map/ppermute | solution.py:173
  13.1 3.0 %collective-permute-start.5 = (f32[256,128]{1,0:T(8,128)S(1)}, f32[256,128]{1,0:T(8,128)S(1)}, u32[]{:S(2)}, u32[]{:S(2)}) collective-permute-start(f32[256,128]{1,0:T(8,128)S(1)} %add.22), channel_id=1, source_target_pairs={{0,8},{1,3},{2,10},{3,1},{4,12},{5,7},{6,14},{7,5},{8,0},{9,11},{1... | collective-permute-start | bytes 393224 | tf_op jit(solution)/shard_map/ppermute | solution.py:173
  16.1 0.5 %collective-permute-done.1 = f32[256,128]{1,0:T(8,128)S(1)} collective-permute-done((f32[256,128]{1,0:T(8,128)S(1)}, f32[256,128]{1,0:T(8,128)S(1)}, u32[]{:S(2)}, u32[]{:S(2)}) %collective-permute-start.1) | collective-permute-done | bytes 131104 | tf_op jit(solution)/shard_map/ppermute | solution.py:173
  16.6 2.4 %collective-permute-start.2 = (f32[256,128]{1,0:T(8,128)S(1)}, f32[256,128]{1,0:T(8,128)S(1)}, u32[]{:S(2)}, u32[]{:S(2)}) collective-permute-start(f32[256,128]{1,0:T(8,128)S(1)} %add.19), channel_id=1, source_target_pairs={{0,4},{1,3},{2,6},{3,1},{4,0},{5,7},{6,2},{7,5},{8,12},{9,11},{10,... | collective-permute-start | bytes 393224 | tf_op jit(solution)/shard_map/ppermute | solution.py:173
  19.0 0.4 %collective-permute-done.5 = f32[256,128]{1,0:T(8,128)S(1)} collective-permute-done((f32[256,128]{1,0:T(8,128)S(1)}, f32[256,128]{1,0:T(8,128)S(1)}, u32[]{:S(2)}, u32[]{:S(2)}) %collective-permute-start.5) | collective-permute-done | bytes 131104 | tf_op jit(solution)/shard_map/ppermute | solution.py:173
  19.4 0.0 copy-start
  19.4 0.5 %collective-permute-start.7 = (f32[256,128]{1,0:T(8,128)S(1)}, f32[256,128]{1,0:T(8,128)S(1)}, u32[]{:S(2)}, u32[]{:S(2)}) collective-permute-start(f32[256,128]{1,0:T(8,128)S(1)} %add.23.refs_1_), channel_id=1, source_target_pairs={{0,1},{1,0},{2,3},{3,2},{4,5},{5,4},{6,7},{7,6},{8,9},{9,8},{10,11... | collective-permute-start | bytes 393224 | tf_op jit(solution)/shard_map/ppermute | solution.py:177
  19.9 2.1 %collective-permute-done.2 = f32[256,128]{1,0:T(8,128)S(1)} collective-permute-done((f32[256,128]{1,0:T(8,128)S(1)}, f32[256,128]{1,0:T(8,128)S(1)}, u32[]{:S(2)}, u32[]{:S(2)}) %collective-permute-start.2) | collective-permute-done | bytes 131104 | tf_op jit(solution)/shard_map/ppermute | solution.py:173
  22.0 0.1 collective-permute-start.6
  22.0 0.0 collective-permute-done.7.refs_3_
  22.0 1.3 %collective-permute-done.6.refs_2_ = f32[256,128]{1,0:T(8,128)S(1)} collective-permute-done((f32[256,128]{1,0:T(8,128)S(1)}, f32[256,128]{1,0:T(8,128)S(1)}, u32[]{:S(2)}, u32[]{:S(2)}) %collective-permute-start.6) | collective-permute-done | bytes 131104 | tf_op jit(solution)/shard_map/ppermute | solution.py:177
  23.4 0.0 collective-permute-done.8.refs_6_
  23.4 0.0 copy-done
  23.4 1.5 %image.1 = f32[1,256]{1,0:T(1,128)} custom-call(f32[256,128]{1,0:T(8,128)S(1)} %add.20.refs_0_, f32[256,128]{1,0:T(8,128)S(1)} %add.23.refs_1_, f32[256,128]{1,0:T(8,128)S(1)} %collective-permute-done.6.refs_2_, f32[256,128]{1,0:T(8,128)S(1)} %collective-permute-done.7.refs_3_, f32[2,64,256]{2,1,0:T(8,128)S(1)} %copy-done, ...), custom_call_target="tpu_custom_call" | custom-call | tf_op jit(solution)/shard_map/image/pallas_call | solution.py:160
  (6 shorter events, 0.1 us)
Async XLA Ops:
  0.0 23.4 %collective-permute-start.8 = (f32[2,512,256]{2,1,0:T(8,128)}, f32[2,512,256]{2,1,0:T(8,128)S(1)}, u32[]{:S(2)}, u32[]{:S(2)}) collective-permute-start(f32[2,512,256]{2,1,0:T(8,128)} %rcv_ref.1), channel_id=1, source_target_pairs={{0,1},{1,0},{2,3},{3,2},{4,5},{5,4},{6,7},{7,6},{8,9},{9,8},{10,11... | collective-permute-start | bytes 3145736 | tf_op jit(solution)/shard_map/ppermute | solution.py:177
  2.1 5.5 %collective-permute-start.3 = (f32[256,128]{1,0:T(8,128)S(1)}, f32[256,128]{1,0:T(8,128)S(1)}, u32[]{:S(2)}, u32[]{:S(2)}) collective-permute-start(f32[256,128]{1,0:T(8,128)S(1)} %get-tuple-element.12), channel_id=1, source_target_pairs={{0,2},{1,9},{2,0},{3,11},{4,6},{5,13},{6,4},{7,15},{8,10},{9,1},{1... | collective-permute-start | bytes 393224 | tf_op jit(solution)/shard_map/ppermute | solution.py:173
  5.0 5.0 %collective-permute-start = (f32[256,128]{1,0:T(8,128)S(1)}, f32[256,128]{1,0:T(8,128)S(1)}, u32[]{:S(2)}, u32[]{:S(2)}) collective-permute-start(f32[256,128]{1,0:T(8,128)S(1)} %modelled_1.1), channel_id=1, source_target_pairs={{0,2},{1,9},{2,0},{3,11},{4,6},{5,13},{6,4},{7,15},{8,10},{9,1},{1... | collective-permute-start | bytes 393224 | tf_op jit(solution)/shard_map/ppermute | solution.py:173
  7.6 5.5 %collective-permute-start.4 = (f32[256,128]{1,0:T(8,128)S(1)}, f32[256,128]{1,0:T(8,128)S(1)}, u32[]{:S(2)}, u32[]{:S(2)}) collective-permute-start(f32[256,128]{1,0:T(8,128)S(1)} %add.21), channel_id=1, source_target_pairs={{0,4},{1,5},{2,6},{3,7},{4,0},{5,1},{6,2},{7,3},{8,12},{9,13},{10,... | collective-permute-start | bytes 393224 | tf_op jit(solution)/shard_map/ppermute | solution.py:173
  10.0 6.6 %collective-permute-start.1 = (f32[256,128]{1,0:T(8,128)S(1)}, f32[256,128]{1,0:T(8,128)S(1)}, u32[]{:S(2)}, u32[]{:S(2)}) collective-permute-start(f32[256,128]{1,0:T(8,128)S(1)} %add.18), channel_id=1, source_target_pairs={{0,8},{1,5},{2,10},{3,7},{4,12},{5,1},{6,14},{7,3},{8,0},{9,13},{1... | collective-permute-start | bytes 393224 | tf_op jit(solution)/shard_map/ppermute | solution.py:173
  13.1 6.3 %collective-permute-start.5 = (f32[256,128]{1,0:T(8,128)S(1)}, f32[256,128]{1,0:T(8,128)S(1)}, u32[]{:S(2)}, u32[]{:S(2)}) collective-permute-start(f32[256,128]{1,0:T(8,128)S(1)} %add.22), channel_id=1, source_target_pairs={{0,8},{1,3},{2,10},{3,1},{4,12},{5,7},{6,14},{7,5},{8,0},{9,11},{1... | collective-permute-start | bytes 393224 | tf_op jit(solution)/shard_map/ppermute | solution.py:173
  16.6 5.3 %collective-permute-start.2 = (f32[256,128]{1,0:T(8,128)S(1)}, f32[256,128]{1,0:T(8,128)S(1)}, u32[]{:S(2)}, u32[]{:S(2)}) collective-permute-start(f32[256,128]{1,0:T(8,128)S(1)} %add.19), channel_id=1, source_target_pairs={{0,4},{1,3},{2,6},{3,1},{4,0},{5,7},{6,2},{7,5},{8,12},{9,11},{10,... | collective-permute-start | bytes 393224 | tf_op jit(solution)/shard_map/ppermute | solution.py:173
  19.4 4.0 %copy-start = (f32[2,64,256]{2,1,0:T(8,128)S(1)}, f32[2,64,256]{2,1,0:T(8,128)}, u32[]{:S(2)}) copy-start(f32[2,64,256]{2,1,0:T(8,128)} %refs_4_.1) | copy-start | bytes 393220
  19.4 2.6 %collective-permute-start.7 = (f32[256,128]{1,0:T(8,128)S(1)}, f32[256,128]{1,0:T(8,128)S(1)}, u32[]{:S(2)}, u32[]{:S(2)}) collective-permute-start(f32[256,128]{1,0:T(8,128)S(1)} %add.23.refs_1_), channel_id=1, source_target_pairs={{0,1},{1,0},{2,3},{3,2},{4,5},{5,4},{6,7},{7,6},{8,9},{9,8},{10,11... | collective-permute-start | bytes 393224 | tf_op jit(solution)/shard_map/ppermute | solution.py:177
  22.0 1.4 %collective-permute-start.6 = (f32[256,128]{1,0:T(8,128)S(1)}, f32[256,128]{1,0:T(8,128)S(1)}, u32[]{:S(2)}, u32[]{:S(2)}) collective-permute-start(f32[256,128]{1,0:T(8,128)S(1)} %add.20.refs_0_), channel_id=1, source_target_pairs={{0,1},{1,0},{2,3},{3,2},{4,5},{5,4},{6,7},{7,6},{8,9},{9,8},{10,11... | collective-permute-start | bytes 393224 | tf_op jit(solution)/shard_map/ppermute | solution.py:177

commit v5 on v4

v5 whole, which is shorter than its diff:
```python
import functools

import jax
import jax.numpy as jnp
from jax import lax
from jax.experimental import pallas as pl
from jax.experimental.pallas import tpu as pltpu
from jax.sharding import PartitionSpec as P

GROUPS = 3
LANES_LAST = (((1,), (1,)), ((), ()))
PLAIN = (((1,), (0,)), ((), ()))
VMEM_LIMIT = 24 * 1024 * 1024
SHARE = 20


def split(x):
    high = x.astype(jnp.bfloat16)
    return high, (x - high.astype(jnp.float32)).astype(jnp.bfloat16)


def dot(a, b, dims):
    return lax.dot_general(a, b, dims, preferred_element_type=jnp.float32)


def stacked(real, imag):
    return [jnp.concatenate(rows, axis=0) for rows in ([real, imag], [-imag, real])]


def side_of(me, core, last):
    return lax.rem(lax.shift_right_logical(me, core * last), 2)


def modelled_rows(rcv_ref, rows_ref, data_ref, out_ref, start):
    width = out_ref.shape[1]
    here = pl.ds(start, out_ref.shape[0])
    total = -data_ref[here, :]
    for c in range(2):
        high, low = split(rcv_ref[c, here, :])
        both = dot(high, rows_ref[c], LANES_LAST)
        total += both[:, :width] + both[:, width:]
        total += dot(low, rows_ref[c, :width], LANES_LAST)
    out_ref[...] = total


def first_kernel(last, me_ref, core_ref, src_ref, model_ref, rcv_ref, obs_ref, *refs):
    out_ref, rcv_out, rows_ref, data_ref, placed_ref, src_held, model_held, obs_held, sems = refs
    half, receivers = out_ref.shape[0], rcv_ref.shape[1]
    own, sources = obs_ref.shape[0], src_ref.shape[1]
    sent = pl.multiple_of((1 - side_of(me_ref[0], core_ref[0], last)) * half, 8)
    kept = pl.multiple_of(side_of(me_ref[0], core_ref[0], last) * half, 8)
    inputs = [
        pltpu.make_async_copy(model_ref, model_held, sems.at[0]),
        pltpu.make_async_copy(src_ref.at[0], src_held.at[0], sems.at[1]),
        pltpu.make_async_copy(src_ref.at[1], src_held.at[1], sems.at[2]),
    ]
    obs_copy = pltpu.make_async_copy(obs_ref, obs_held, sems.at[3])
    pieces = []
    for k, here in enumerate((pl.ds(sent, half), pl.ds(kept, half), pl.ds(2 * half, receivers - 2 * half))):
        for c in range(2):
            n = 2 * k + c
            pieces.append(pltpu.make_async_copy(rcv_ref.at[c, here, :], rcv_out.at[c, here, :], sems.at[4 + n]))
    for copy in [*inputs, obs_copy, *pieces]:
        copy.start()
    placed_ref[...] = jnp.zeros_like(placed_ref)
    for copy in inputs:
        copy.wait()
    model = model_held[...]
    for c, rows in enumerate(stacked(src_held[0] * model, src_held[1] * model)):
        rows_ref[c, : rows.shape[0]], rows_ref[c, rows.shape[0] :] = split(rows)
    obs_copy.wait()
    for c in range(2):
        start = pl.multiple_of(c * sources + me_ref[0] * own, own)
        placed_ref[pl.ds(start, own), :] = obs_held[:, c, :]
    data_ref[...] = placed_ref[...].T
    for copy in pieces[:2]:
        copy.wait()
    modelled_rows(rcv_out, rows_ref, data_ref, out_ref, sent)
    for copy in pieces[2:]:
        copy.wait()


def next_kernel(last, me_ref, core_ref, data_ref, rcv_ref, rows_ref, keep_ref, full_ref):
    half = keep_ref.shape[0]
    kept = pl.multiple_of(side_of(me_ref[0], core_ref[0], last) * half, 8)
    modelled_rows(rcv_ref, rows_ref, data_ref, keep_ref, kept)
    modelled_rows(rcv_ref, rows_ref, data_ref, full_ref, 2 * half)


def modelled_parts(last, place, src_green, model, rcv_green, observed):
    _, sources, points = src_green.shape
    receivers, width = rcv_green.shape[1], 2 * sources
    half = receivers * SHARE // 64
    in_vmem, in_smem = pl.BlockSpec(memory_space=pltpu.VMEM), pl.BlockSpec(memory_space=pltpu.SMEM)
    params = pltpu.CompilerParams(vmem_limit_bytes=VMEM_LIMIT)
    inputs = [pltpu.with_memory_space_constraint(x, pltpu.HBM) for x in (src_green, model, rcv_green, observed)]
    sent, rcv_held, rows, data = pl.pallas_call(
        functools.partial(first_kernel, last),
        out_shape=[
            jax.ShapeDtypeStruct((half, width), jnp.float32),
            jax.ShapeDtypeStruct(rcv_green.shape, jnp.float32),
            jax.ShapeDtypeStruct((2, 2 * width, points), jnp.bfloat16),
            jax.ShapeDtypeStruct((receivers, width), jnp.float32),
        ],
        in_specs=[in_smem] * 2 + [pl.BlockSpec(memory_space=pltpu.HBM)] * 4,
        out_specs=[in_vmem] * 4,
        scratch_shapes=[
            pltpu.VMEM((width, receivers), jnp.float32),
            pltpu.VMEM(src_green.shape, jnp.float32),
            pltpu.VMEM(model.shape, jnp.float32),
            pltpu.VMEM(observed.shape, jnp.float32),
            pltpu.SemaphoreType.DMA((10,)),
        ],
        compiler_params=params,
        name="modelled_sent",
    )(*place, *inputs)
    kept, full = pl.pallas_call(
        functools.partial(next_kernel, last),
        out_shape=[
            jax.ShapeDtypeStruct((half, width), jnp.float32),
            jax.ShapeDtypeStruct((receivers - 2 * half, width), jnp.float32),
        ],
        in_specs=[in_smem] * 2 + [in_vmem] * 3,
        out_specs=[in_vmem] * 2,
        compiler_params=params,
        cost_estimate=pl.CostEstimate(flops=10**9, bytes_accessed=4 * 10**6, transcendentals=0),
        name="modelled_rest",
    )(*place, data, rcv_held, rows)
    return sent, kept, full, rcv_held


def image_kernel(last, count, scale, me_ref, core_ref, *refs):
    rcv = refs[:2]
    src_ref, *resid = refs[2:-1]
    resid = [resid[:GROUPS], resid[GROUPS:]]
    out_ref = refs[-1]
    sources, points = src_ref.shape[1:]

    def energy(group):
        total = jnp.zeros((8, 2 * sources), jnp.float32)
        for ref in group:
            total += jnp.sum((ref[...] ** 2).reshape(-1, 8, 2 * sources), axis=0)
        return jnp.sum(total)

    spread_sq = (energy(resid[0]) + energy(resid[1])) / count + 1e-06
    stacks = []
    for part in ([src_ref[0], src_ref[1]], [-src_ref[1], src_ref[0]]):
        high, low = split(jnp.concatenate(part, axis=0))
        stacks.append((jnp.concatenate([high, high], axis=0), low))

    sums = []
    half = resid[0][0].shape[0]
    for group, rcv_ref, core in zip(resid, rcv, (core_ref[0], 1 - core_ref[0])):
        side = side_of(me_ref[0], core, last)
        firsts = [pl.multiple_of(side * half, 8), pl.multiple_of((1 - side) * half, 8), 2 * half]
        total = jnp.zeros((8, points), jnp.float32)
        for first, ref in zip(firsts, group):
            here = ref[...]
            square = here * here
            both = square + pltpu.roll(square, sources, 1)
            weighted_high, weighted_low = split(here / (1.0 + both / spread_sq))
            wide = jnp.concatenate([weighted_high, weighted_low], axis=1)
            for c, (double, low) in enumerate(stacks):
                terms = dot(wide, double, PLAIN) + dot(weighted_high, low, PLAIN)
                terms = terms * rcv_ref[c, pl.ds(first, here.shape[0]), :]
                total += jnp.sum(terms.reshape(-1, 8, points), axis=0)
        sums.append(jnp.sum(total, axis=0, keepdims=True))
    out_ref[...] = (sums[0] + sums[1]) * scale


def image(last, place, own, other, src_green, rcv_own, rcv_other, count, scale):
    points = src_green.shape[2]
    whole = pl.BlockSpec(memory_space=pltpu.VMEM)
    return pl.pallas_call(
        functools.partial(image_kernel, last, count, scale),
        out_shape=jax.ShapeDtypeStruct((1, points), jnp.float32),
        in_specs=[pl.BlockSpec(memory_space=pltpu.SMEM)] * 2 + [whole] * (2 * GROUPS + 3),
        out_specs=whole,
        compiler_params=pltpu.CompilerParams(vmem_limit_bytes=VMEM_LIMIT),
        name="image",
    )(*place, rcv_own, rcv_other, src_green, *own, *other)


def swap_points(array, bit_of):
    points, cores = lax.axis_size("pts"), lax.axis_size("rcv")
    pairs = [(p * cores + c, (p ^ (1 << bit_of[c])) * cores + c) for p in range(points) for c in range(cores)]
    return lax.ppermute(array, ("pts", "rcv"), pairs)


def swap_cores(array):
    return lax.ppermute(array, "rcv", [(0, 1), (1, 0)])


def local(src_green, rcv_green, model, observed):
    points, cores = lax.axis_size("pts"), lax.axis_size("rcv")
    bits = points.bit_length() - 1
    assert points == 1 << bits and cores == 2
    num_points = src_green.shape[2] * points
    count = src_green.shape[1] * rcv_green.shape[1] * cores
    scale = float((num_points / count) ** 0.5)
    place = [lax.axis_index(name).astype(jnp.int32).reshape(1) for name in ("pts", "rcv")]

    model = model.reshape(1, -1)
    sent, kept, full, rcv_own = modelled_parts(bits - 1, place, src_green, model, rcv_green, observed)
    up = list(range(bits))
    halves = [up, up[::-1]]
    wholes = [up[:1] + up[:0:-1], up[-1:] + up[:-1]]
    for step in range(bits):
        got = swap_points(sent if step == 0 else kept, [order[step] for order in halves])
        kept = kept + got
        full = full + swap_points(full, [order[step] for order in wholes])
    own = [kept, swap_points(kept, [order[0] for order in halves]), full]
    other = [swap_cores(x) for x in own]
    rcv_other = swap_cores(rcv_green)
    return image(bits - 1, place, own, other, src_green, rcv_own, rcv_other, count, scale).reshape(-1)


def solution(mesh):
    placed = (
        P(None, "grp", "pts"),
        P(None, ("grp", "rcv"), "pts"),
        P(("grp", "pts")),
        P(("grp", "pts"), None, "rcv"),
    )
    return jax.shard_map(
        local, mesh=mesh, in_specs=placed, out_specs=P(("grp", "pts")), check_vma=False
    )
```

time: 25 us -> 25.2 us (level)
  starting transfers between devices: 13.8 us -> 14.5 us
  waiting for transfers between devices: 7.45 us -> 7.04 us
    ppermute x6 -> x7, starting transfers between devices: 12.8 us -> 13.4 us  [swap_points(): return lax.ppermute(array, ('pts', 'rcv'), pairs)]
    ppermute x6 -> x7, waiting for transfers between devices: 6.12 us -> 5.81 us  [swap_points(): return lax.ppermute(array, ('pts', 'rcv'), pairs)]
    ppermute x3 -> x4, waiting for transfers between devices: 1.33 us -> 1.23 us  [swap_cores(): return lax.ppermute(array, 'rcv', [(0, 1), (1, 0)])]
    ppermute x3 -> x4, starting transfers between devices: 0.98 us -> 1.07 us  [swap_cores(): return lax.ppermute(array, 'rcv', [(0, 1), (1, 0)])]
  transfers between devices with their start and end apart: 9 -> 11, of which waited for: 7 -> 7; matrix products, arithmetic and copies ran while one was open for 0% -> 0% of each run, Pallas kernels for 8% -> 7%
where the time goes in v5:
time: 25.2 us; the launch traced here: 25 us
  starting transfers between devices  14.5 us (58%)
  waiting for transfers between devices  7.04 us (28%)
  Pallas kernels  3.35 us (13%)
    ppermute x7, starting transfers between devices, swap_points(): return lax.ppermute(array, ('pts', 'rcv'), pairs)  13.4 us
    ppermute x7, waiting for transfers between devices, swap_points(): return lax.ppermute(array, ('pts', 'rcv'), pairs)  5.81 us
    pallas_call x1, Pallas kernels, image(): pl.pallas_call(functools.partial(image_kernel, last, count, scale), out_s...  1.48 us
    pallas_call x1, Pallas kernels, modelled_parts(): pl.pallas_call(functools.partial(first_kernel, last), out_shape=[jax.Shap...  1.47 us
    ppermute x4, waiting for transfers between devices, swap_cores(): return lax.ppermute(array, 'rcv', [(0, 1), (1, 0)])  1.23 us
    ppermute x4, starting transfers between devices, swap_cores(): return lax.ppermute(array, 'rcv', [(0, 1), (1, 0)])  1.07 us
  transfers between devices with their start and end apart: 11, of which 7 were waited for; matrix products, arithmetic and copies ran while one was open for 0% of the time, Pallas kernels for 7%

profile of v5, /device:TPU:0, one launch (start us, length us, event | category | flops | bytes accessed | tf_op | source)
XLA Modules:
  0.0 25.0 jit_solution(11849308630731986969)
XLA Ops:
  0.0 0.5 %collective-permute-start = (f32[2,512,256]{2,1,0:T(8,128)}, f32[2,512,256]{2,1,0:T(8,128)S(1)}, u32[]{:S(2)}, u32[]{:S(2)}) collective-permute-start(f32[2,512,256]{2,1,0:T(8,128)} %rcv_ref.1), channel_id=1, source_target_pairs={{0,1},{1,0},{2,3},{3,2},{4,5},{5,4},{6,7},{7,6},{8,9},{9,8},{10,11... | collective-permute-start | bytes 3145736 | tf_op jit(solution)/shard_map/ppermute | solution.py:191
  0.5 1.5 %modelled_sent.1 = (f32[160,128]{1,0:T(8,128)S(1)}, f32[2,512,256]{2,1,0:T(8,128)S(1)}, bf16[2,256,256]{2,1,0:T(8,128)(2,1)S(1)}, f32[512,128]{1,0:T(8,128)S(1)}) custom-call(s32[1]{0:T(128)} %bitcast.me_ref, s32[1]{0:T(128)} %bitcast.1.core_ref, f32[2,64,256]{2,1,0:T(8,128)} %refs_2_.1, f32[1,256]{1,0:T(1,128)} %bitcast.4, f32[2,512,256]{2,1,0:T(8,128)} %rcv_ref.1, ...), custom_call_target="tpu_custom_call" | custom-call | tf_op jit(solution)/shard_map/modelled_sent/pallas_call | solution.py:97
  1.9 2.6 %collective-permute-start.1 = (f32[160,128]{1,0:T(8,128)S(1)}, f32[160,128]{1,0:T(8,128)S(1)}, u32[]{:S(2)}, u32[]{:S(2)}) collective-permute-start(f32[160,128]{1,0:T(8,128)S(1)} %get-tuple-element.15), channel_id=1, source_target_pairs={{0,2},{1,9},{2,0},{3,11},{4,6},{5,13},{6,4},{7,15},{8,10},{9,1},{1... | collective-permute-start | bytes 245768 | tf_op jit(solution)/shard_map/ppermute | solution.py:187
  4.5 0.4 %modelled_rest.1 = (f32[160,128]{1,0:T(8,128)S(1)}, f32[192,128]{1,0:T(8,128)S(1)}) custom-call(s32[1]{0:T(128)} %bitcast.me_ref, s32[1]{0:T(128)} %bitcast.1.core_ref, f32[512,128]{1,0:T(8,128)S(1)} %get-tuple-element.12.data_ref, f32[2,512,256]{2,1,0:T(8,128)S(1)} %get-tuple-element.11.rcv_ref.refs_0_, bf16[2,256,256]{2,1,0:T(8,128)(2,1)S(1)} %get-tuple-element.13.rows_ref), custom_call_target="tpu_custom_call" | custom-call | flops 1000000000 | bytes 4000000 | tf_op jit(solution)/shard_map/modelled_rest/pallas_call | solution.py:117
  4.9 0.1 collective-permute-start.5
  5.0 1.9 %collective-permute-done.1 = f32[160,128]{1,0:T(8,128)S(1)} collective-permute-done((f32[160,128]{1,0:T(8,128)S(1)}, f32[160,128]{1,0:T(8,128)S(1)}, u32[]{:S(2)}, u32[]{:S(2)}) %collective-permute-start.1) | collective-permute-done | bytes 81952 | tf_op jit(solution)/shard_map/ppermute | solution.py:187
  6.9 2.2 %collective-permute-start.2 = (f32[160,128]{1,0:T(8,128)S(1)}, f32[160,128]{1,0:T(8,128)S(1)}, u32[]{:S(2)}, u32[]{:S(2)}) collective-permute-start(f32[160,128]{1,0:T(8,128)S(1)} %add.18), channel_id=1, source_target_pairs={{0,4},{1,5},{2,6},{3,7},{4,0},{5,1},{6,2},{7,3},{8,12},{9,13},{10,... | collective-permute-start | bytes 245768 | tf_op jit(solution)/shard_map/ppermute | solution.py:187
  9.1 0.5 %collective-permute-done.5 = f32[192,128]{1,0:T(8,128)S(1)} collective-permute-done((f32[192,128]{1,0:T(8,128)S(1)}, f32[192,128]{1,0:T(8,128)S(1)}, u32[]{:S(2)}, u32[]{:S(2)}) %collective-permute-start.5) | collective-permute-done | bytes 98336 | tf_op jit(solution)/shard_map/ppermute | solution.py:187
  9.6 2.7 %collective-permute-start.6 = (f32[192,128]{1,0:T(8,128)S(1)}, f32[192,128]{1,0:T(8,128)S(1)}, u32[]{:S(2)}, u32[]{:S(2)}) collective-permute-start(f32[192,128]{1,0:T(8,128)S(1)} %add.21), channel_id=1, source_target_pairs={{0,8},{1,3},{2,10},{3,1},{4,12},{5,7},{6,14},{7,5},{8,0},{9,11},{1... | collective-permute-start | bytes 294920 | tf_op jit(solution)/shard_map/ppermute | solution.py:187
  12.2 0.0 collective-permute-done.2
  12.3 2.4 %collective-permute-start.3 = (f32[160,128]{1,0:T(8,128)S(1)}, f32[160,128]{1,0:T(8,128)S(1)}, u32[]{:S(2)}, u32[]{:S(2)}) collective-permute-start(f32[160,128]{1,0:T(8,128)S(1)} %add.19), channel_id=1, source_target_pairs={{0,8},{1,3},{2,10},{3,1},{4,12},{5,7},{6,14},{7,5},{8,0},{9,11},{1... | collective-permute-start | bytes 245768 | tf_op jit(solution)/shard_map/ppermute | solution.py:187
  14.6 0.6 %collective-permute-done.6 = f32[192,128]{1,0:T(8,128)S(1)} collective-permute-done((f32[192,128]{1,0:T(8,128)S(1)}, f32[192,128]{1,0:T(8,128)S(1)}, u32[]{:S(2)}, u32[]{:S(2)}) %collective-permute-start.6) | collective-permute-done | bytes 98336 | tf_op jit(solution)/shard_map/ppermute | solution.py:187
  15.2 1.8 %collective-permute-start.7 = (f32[192,128]{1,0:T(8,128)S(1)}, f32[192,128]{1,0:T(8,128)S(1)}, u32[]{:S(2)}, u32[]{:S(2)}) collective-permute-start(f32[192,128]{1,0:T(8,128)S(1)} %add.22), channel_id=1, source_target_pairs={{0,4},{1,5},{2,6},{3,7},{4,0},{5,1},{6,2},{7,3},{8,12},{9,13},{10,... | collective-permute-start | bytes 294920 | tf_op jit(solution)/shard_map/ppermute | solution.py:187
  17.0 0.7 %collective-permute-done.3 = f32[160,128]{1,0:T(8,128)S(1)} collective-permute-done((f32[160,128]{1,0:T(8,128)S(1)}, f32[160,128]{1,0:T(8,128)S(1)}, u32[]{:S(2)}, u32[]{:S(2)}) %collective-permute-start.3) | collective-permute-done | bytes 81952 | tf_op jit(solution)/shard_map/ppermute | solution.py:187
  17.7 0.0 copy-start
  17.7 1.8 %collective-permute-start.4 = (f32[160,128]{1,0:T(8,128)S(1)}, f32[160,128]{1,0:T(8,128)S(1)}, u32[]{:S(2)}, u32[]{:S(2)}) collective-permute-start(f32[160,128]{1,0:T(8,128)S(1)} %add.20.refs_3_), channel_id=1, source_target_pairs={{0,2},{1,9},{2,0},{3,11},{4,6},{5,13},{6,4},{7,15},{8,10},{9,1},{1... | collective-permute-start | bytes 245768 | tf_op jit(solution)/shard_map/ppermute | solution.py:187
  19.6 0.3 %collective-permute-done.7 = f32[192,128]{1,0:T(8,128)S(1)} collective-permute-done((f32[192,128]{1,0:T(8,128)S(1)}, f32[192,128]{1,0:T(8,128)S(1)}, u32[]{:S(2)}, u32[]{:S(2)}) %collective-permute-start.7) | collective-permute-done | bytes 98336 | tf_op jit(solution)/shard_map/ppermute | solution.py:187
  19.9 0.1 collective-permute-start.10
  20.0 0.5 %collective-permute-start.8 = (f32[160,128]{1,0:T(8,128)S(1)}, f32[160,128]{1,0:T(8,128)S(1)}, u32[]{:S(2)}, u32[]{:S(2)}) collective-permute-start(f32[160,128]{1,0:T(8,128)S(1)} %add.20.refs_3_), channel_id=1, source_target_pairs={{0,1},{1,0},{2,3},{3,2},{4,5},{5,4},{6,7},{7,6},{8,9},{9,8},{10,11... | collective-permute-start | bytes 245768 | tf_op jit(solution)/shard_map/ppermute | solution.py:191
  20.5 1.8 %collective-permute-done.4.refs_4_ = f32[160,128]{1,0:T(8,128)S(1)} collective-permute-done((f32[160,128]{1,0:T(8,128)S(1)}, f32[160,128]{1,0:T(8,128)S(1)}, u32[]{:S(2)}, u32[]{:S(2)}) %collective-permute-start.4) | collective-permute-done | bytes 81952 | tf_op jit(solution)/shard_map/ppermute | solution.py:187
  22.2 0.0 collective-permute-start.9
  22.3 0.0 collective-permute-done.8.refs_6_
  22.3 1.2 %collective-permute-done.9.refs_7_ = f32[160,128]{1,0:T(8,128)S(1)} collective-permute-done((f32[160,128]{1,0:T(8,128)S(1)}, f32[160,128]{1,0:T(8,128)S(1)}, u32[]{:S(2)}, u32[]{:S(2)}) %collective-permute-start.9) | collective-permute-done | bytes 81952 | tf_op jit(solution)/shard_map/ppermute | solution.py:191
  23.5 1.5 %image.1 = f32[1,256]{1,0:T(1,128)} custom-call(s32[1]{0:T(128)} %bitcast.me_ref, s32[1]{0:T(128)} %bitcast.1.core_ref, f32[2,512,256]{2,1,0:T(8,128)S(1)} %get-tuple-element.11.rcv_ref.refs_0_, f32[2,512,256]{2,1,0:T(8,128)S(1)} %collective-permute-done.refs_1_, f32[2,64,256]{2,1,0:T(8,128)S(1)} %copy-done, f32[160,128]{1,0:T(8,128)S(1)} %add.20.refs_3_, ...), custom_call_target="tpu_custom_call" | custom-call | tf_op jit(solution)/shard_map/image/pallas_call | solution.py:174
  (9 shorter events, 0.1 us)
Async XLA Ops:
  0.0 23.5 %collective-permute-start = (f32[2,512,256]{2,1,0:T(8,128)}, f32[2,512,256]{2,1,0:T(8,128)S(1)}, u32[]{:S(2)}, u32[]{:S(2)}) collective-permute-start(f32[2,512,256]{2,1,0:T(8,128)} %rcv_ref.1), channel_id=1, source_target_pairs={{0,1},{1,0},{2,3},{3,2},{4,5},{5,4},{6,7},{7,6},{8,9},{9,8},{10,11... | collective-permute-start | bytes 3145736 | tf_op jit(solution)/shard_map/ppermute | solution.py:191
  1.9 5.0 %collective-permute-start.1 = (f32[160,128]{1,0:T(8,128)S(1)}, f32[160,128]{1,0:T(8,128)S(1)}, u32[]{:S(2)}, u32[]{:S(2)}) collective-permute-start(f32[160,128]{1,0:T(8,128)S(1)} %get-tuple-element.15), channel_id=1, source_target_pairs={{0,2},{1,9},{2,0},{3,11},{4,6},{5,13},{6,4},{7,15},{8,10},{9,1},{1... | collective-permute-start | bytes 245768 | tf_op jit(solution)/shard_map/ppermute | solution.py:187
  4.9 4.7 %collective-permute-start.5 = (f32[192,128]{1,0:T(8,128)S(1)}, f32[192,128]{1,0:T(8,128)S(1)}, u32[]{:S(2)}, u32[]{:S(2)}) collective-permute-start(f32[192,128]{1,0:T(8,128)S(1)} %get-tuple-element.16), channel_id=1, source_target_pairs={{0,2},{1,9},{2,0},{3,11},{4,6},{5,13},{6,4},{7,15},{8,10},{9,1},{1... | collective-permute-start | bytes 294920 | tf_op jit(solution)/shard_map/ppermute | solution.py:187
  6.9 5.3 %collective-permute-start.2 = (f32[160,128]{1,0:T(8,128)S(1)}, f32[160,128]{1,0:T(8,128)S(1)}, u32[]{:S(2)}, u32[]{:S(2)}) collective-permute-start(f32[160,128]{1,0:T(8,128)S(1)} %add.18), channel_id=1, source_target_pairs={{0,4},{1,5},{2,6},{3,7},{4,0},{5,1},{6,2},{7,3},{8,12},{9,13},{10,... | collective-permute-start | bytes 245768 | tf_op jit(solution)/shard_map/ppermute | solution.py:187
  9.6 5.6 %collective-permute-start.6 = (f32[192,128]{1,0:T(8,128)S(1)}, f32[192,128]{1,0:T(8,128)S(1)}, u32[]{:S(2)}, u32[]{:S(2)}) collective-permute-start(f32[192,128]{1,0:T(8,128)S(1)} %add.21), channel_id=1, source_target_pairs={{0,8},{1,3},{2,10},{3,1},{4,12},{5,7},{6,14},{7,5},{8,0},{9,11},{1... | collective-permute-start | bytes 294920 | tf_op jit(solution)/shard_map/ppermute | solution.py:187
  12.3 5.5 %collective-permute-start.3 = (f32[160,128]{1,0:T(8,128)S(1)}, f32[160,128]{1,0:T(8,128)S(1)}, u32[]{:S(2)}, u32[]{:S(2)}) collective-permute-start(f32[160,128]{1,0:T(8,128)S(1)} %add.19), channel_id=1, source_target_pairs={{0,8},{1,3},{2,10},{3,1},{4,12},{5,7},{6,14},{7,5},{8,0},{9,11},{1... | collective-permute-start | bytes 245768 | tf_op jit(solution)/shard_map/ppermute | solution.py:187
  15.2 4.7 %collective-permute-start.7 = (f32[192,128]{1,0:T(8,128)S(1)}, f32[192,128]{1,0:T(8,128)S(1)}, u32[]{:S(2)}, u32[]{:S(2)}) collective-permute-start(f32[192,128]{1,0:T(8,128)S(1)} %add.22), channel_id=1, source_target_pairs={{0,4},{1,5},{2,6},{3,7},{4,0},{5,1},{6,2},{7,3},{8,12},{9,13},{10,... | collective-permute-start | bytes 294920 | tf_op jit(solution)/shard_map/ppermute | solution.py:187
  17.7 5.8 %copy-start = (f32[2,64,256]{2,1,0:T(8,128)S(1)}, f32[2,64,256]{2,1,0:T(8,128)}, u32[]{:S(2)}) copy-start(f32[2,64,256]{2,1,0:T(8,128)} %refs_2_.1) | copy-start | bytes 393220
  17.7 4.5 %collective-permute-start.4 = (f32[160,128]{1,0:T(8,128)S(1)}, f32[160,128]{1,0:T(8,128)S(1)}, u32[]{:S(2)}, u32[]{:S(2)}) collective-permute-start(f32[160,128]{1,0:T(8,128)S(1)} %add.20.refs_3_), channel_id=1, source_target_pairs={{0,2},{1,9},{2,0},{3,11},{4,6},{5,13},{6,4},{7,15},{8,10},{9,1},{1... | collective-permute-start | bytes 245768 | tf_op jit(solution)/shard_map/ppermute | solution.py:187
  19.9 2.4 %collective-permute-start.10 = (f32[192,128]{1,0:T(8,128)S(1)}, f32[192,128]{1,0:T(8,128)S(1)}, u32[]{:S(2)}, u32[]{:S(2)}) collective-permute-start(f32[192,128]{1,0:T(8,128)S(1)} %add.23.refs_5_), channel_id=1, source_target_pairs={{0,1},{1,0},{2,3},{3,2},{4,5},{5,4},{6,7},{7,6},{8,9},{9,8},{10,11... | collective-permute-start | bytes 294920 | tf_op jit(solution)/shard_map/ppermute | solution.py:191
  20.0 2.3 %collective-permute-start.8 = (f32[160,128]{1,0:T(8,128)S(1)}, f32[160,128]{1,0:T(8,128)S(1)}, u32[]{:S(2)}, u32[]{:S(2)}) collective-permute-start(f32[160,128]{1,0:T(8,128)S(1)} %add.20.refs_3_), channel_id=1, source_target_pairs={{0,1},{1,0},{2,3},{3,2},{4,5},{5,4},{6,7},{7,6},{8,9},{9,8},{10,11... | collective-permute-start | bytes 245768 | tf_op jit(solution)/shard_map/ppermute | solution.py:191
  22.2 1.3 %collective-permute-start.9 = (f32[160,128]{1,0:T(8,128)S(1)}, f32[160,128]{1,0:T(8,128)S(1)}, u32[]{:S(2)}, u32[]{:S(2)}) collective-permute-start(f32[160,128]{1,0:T(8,128)S(1)} %collective-permute-done.4.refs_4_), channel_id=1, source_target_pairs={{0,1},{1,0},{2,3},{3,2},{4,5},{5,4},{6,7},{7,6},{8,9},{9,8},{10,11... | collective-permute-start | bytes 245768 | tf_op jit(solution)/shard_map/ppermute | solution.py:191

commit v6 on v5

v6 whole, which is shorter than its diff:
```python
import functools

import jax
import jax.numpy as jnp
from jax import lax
from jax.experimental import pallas as pl
from jax.experimental.pallas import tpu as pltpu
from jax.sharding import PartitionSpec as P

GROUPS = 2
LANES_LAST = (((1,), (1,)), ((), ()))
PLAIN = (((1,), (0,)), ((), ()))
VMEM_LIMIT = 24 * 1024 * 1024
SHARE = 32


def split(x):
    high = x.astype(jnp.bfloat16)
    return high, (x - high.astype(jnp.float32)).astype(jnp.bfloat16)


def dot(a, b, dims):
    return lax.dot_general(a, b, dims, preferred_element_type=jnp.float32)


def stacked(real, imag):
    return [jnp.concatenate(rows, axis=0) for rows in ([real, imag], [-imag, real])]


def modelled_rows(rcv_ref, rows_ref, data_ref, out_ref, start):
    width = out_ref.shape[1]
    here = pl.ds(start, out_ref.shape[0])
    total = -data_ref[here, :]
    for c in range(2):
        high, low = split(rcv_ref[c, here, :])
        both = dot(high, rows_ref[c], LANES_LAST)
        total += both[:, :width] + both[:, width:]
        total += dot(low, rows_ref[c, :width], LANES_LAST)
    out_ref[...] = total


def first_kernel(me_ref, src_ref, model_ref, rcv_ref, obs_ref, *refs):
    out_ref, rcv_out, rows_ref, data_ref, placed_ref, src_held, model_held, obs_held, sems = refs
    half, receivers = out_ref.shape[0], rcv_ref.shape[1]
    own, sources = obs_ref.shape[0], src_ref.shape[1]
    inputs = [
        pltpu.make_async_copy(model_ref, model_held, sems.at[0]),
        pltpu.make_async_copy(src_ref.at[0], src_held.at[0], sems.at[1]),
        pltpu.make_async_copy(src_ref.at[1], src_held.at[1], sems.at[2]),
    ]
    obs_copy = pltpu.make_async_copy(obs_ref, obs_held, sems.at[3])
    pieces = []
    for k, here in enumerate((pl.ds(0, half), pl.ds(half, receivers - half))):
        for c in range(2):
            n = 2 * k + c
            pieces.append(pltpu.make_async_copy(rcv_ref.at[c, here, :], rcv_out.at[c, here, :], sems.at[4 + n]))
    for copy in [*inputs, obs_copy, *pieces]:
        copy.start()
    placed_ref[...] = jnp.zeros_like(placed_ref)
    for copy in inputs:
        copy.wait()
    model = model_held[...]
    for c, rows in enumerate(stacked(src_held[0] * model, src_held[1] * model)):
        rows_ref[c, : rows.shape[0]], rows_ref[c, rows.shape[0] :] = split(rows)
    obs_copy.wait()
    for c in range(2):
        start = pl.multiple_of(c * sources + me_ref[0] * own, own)
        placed_ref[pl.ds(start, own), :] = obs_held[:, c, :]
    data_ref[...] = placed_ref[...].T
    for copy in pieces[:2]:
        copy.wait()
    modelled_rows(rcv_out, rows_ref, data_ref, out_ref, 0)
    for copy in pieces[2:]:
        copy.wait()


def next_kernel(data_ref, rcv_ref, rows_ref, *out_refs):
    start = rcv_ref.shape[1] - sum(ref.shape[0] for ref in out_refs)
    for ref in out_refs:
        modelled_rows(rcv_ref, rows_ref, data_ref, ref, start)
        start += ref.shape[0]


def modelled_parts(me, src_green, model, rcv_green, observed):
    _, sources, points = src_green.shape
    receivers, width = rcv_green.shape[1], 2 * sources
    half = receivers * SHARE // 64
    in_vmem, in_smem = pl.BlockSpec(memory_space=pltpu.VMEM), pl.BlockSpec(memory_space=pltpu.SMEM)
    params = pltpu.CompilerParams(vmem_limit_bytes=VMEM_LIMIT)
    inputs = [pltpu.with_memory_space_constraint(x, pltpu.HBM) for x in (src_green, model, rcv_green, observed)]
    sent, rcv_held, rows, data = pl.pallas_call(
        first_kernel,
        out_shape=[
            jax.ShapeDtypeStruct((half, width), jnp.float32),
            jax.ShapeDtypeStruct(rcv_green.shape, jnp.float32),
            jax.ShapeDtypeStruct((2, 2 * width, points), jnp.bfloat16),
            jax.ShapeDtypeStruct((receivers, width), jnp.float32),
        ],
        in_specs=[in_smem] + [pl.BlockSpec(memory_space=pltpu.HBM)] * 4,
        out_specs=[in_vmem] * 4,
        scratch_shapes=[
            pltpu.VMEM((width, receivers), jnp.float32),
            pltpu.VMEM(src_green.shape, jnp.float32),
            pltpu.VMEM(model.shape, jnp.float32),
            pltpu.VMEM(observed.shape, jnp.float32),
            pltpu.SemaphoreType.DMA((10,)),
        ],
        compiler_params=params,
        name="modelled_sent",
    )(me, *inputs)
    sizes = [receivers - half]
    rest = pl.pallas_call(
        next_kernel,
        out_shape=[
            jax.ShapeDtypeStruct((size, width), jnp.float32) for size in sizes
        ],
        in_specs=[in_vmem] * 3,
        out_specs=[in_vmem],
        compiler_params=params,
        cost_estimate=pl.CostEstimate(flops=10**9, bytes_accessed=4 * 10**6, transcendentals=0),
        name="modelled_rest",
    )(data, rcv_held, rows)
    return [sent, *rest], rcv_held


def fold(ref):
    return jnp.sum((ref[...] ** 2).reshape(-1, 8, ref.shape[1]), axis=0)


def energy_kernel(own_last_ref, own_first_ref, other_first_ref, out_ref):
    out_ref[0] = fold(own_first_ref) + fold(own_last_ref)
    out_ref[1] = fold(other_first_ref)


def energies(own, other):
    whole = pl.BlockSpec(memory_space=pltpu.VMEM)
    return pl.pallas_call(
        energy_kernel,
        out_shape=jax.ShapeDtypeStruct((2, 8, own[0].shape[1]), jnp.float32),
        in_specs=[whole] * 3,
        out_specs=whole,
        compiler_params=pltpu.CompilerParams(vmem_limit_bytes=VMEM_LIMIT),
        name="energies",
    )(own[1], own[0], other[0])


def image_kernel(count, scale, ready_ref, *refs):
    rcv = refs[:2]
    src_ref, *resid = refs[2:-1]
    resid = [resid[:GROUPS], resid[GROUPS:]]
    out_ref = refs[-1]
    sources, points = src_ref.shape[1:]

    own_energy = ready_ref[0]
    other_energy = ready_ref[1] + fold(resid[1][0])
    spread_sq = (jnp.sum(own_energy) + jnp.sum(other_energy)) / count + 1e-06
    stacks = []
    for part in ([src_ref[0], src_ref[1]], [-src_ref[1], src_ref[0]]):
        high, low = split(jnp.concatenate(part, axis=0))
        stacks.append((jnp.concatenate([high, high], axis=0), low))

    sums = []
    firsts = [sum(ref.shape[0] for ref in resid[0][k + 1 :]) for k in range(GROUPS)]
    for group, rcv_ref in zip(resid, rcv):
        total = jnp.zeros((8, points), jnp.float32)
        for first, ref in zip(firsts, group):
            here = ref[...]
            square = here * here
            both = square + pltpu.roll(square, sources, 1)
            weighted_high, weighted_low = split(here / (1.0 + both / spread_sq))
            wide = jnp.concatenate([weighted_high, weighted_low], axis=1)
            for c, (double, low) in enumerate(stacks):
                terms = dot(wide, double, PLAIN) + dot(weighted_high, low, PLAIN)
                terms = terms * rcv_ref[c, pl.ds(first, here.shape[0]), :]
                total += jnp.sum(terms.reshape(-1, 8, points), axis=0)
        sums.append(jnp.sum(total, axis=0, keepdims=True))
    out_ref[...] = (sums[0] + sums[1]) * scale


def image(own, other, src_green, rcv_own, rcv_other, count, scale):
    points = src_green.shape[2]
    whole = pl.BlockSpec(memory_space=pltpu.VMEM)
    return pl.pallas_call(
        functools.partial(image_kernel, count, scale),
        out_shape=jax.ShapeDtypeStruct((1, points), jnp.float32),
        in_specs=[whole] * (2 * GROUPS + 4),
        out_specs=whole,
        compiler_params=pltpu.CompilerParams(vmem_limit_bytes=VMEM_LIMIT),
        name="image",
    )(energies(own, other), rcv_own, rcv_other, src_green, *reversed(own), *reversed(other))


def swap_points(array, bit_of):
    points, cores = lax.axis_size("pts"), lax.axis_size("rcv")
    pairs = [(p * cores + c, (p ^ (1 << bit_of[c])) * cores + c) for p in range(points) for c in range(cores)]
    return lax.ppermute(array, ("pts", "rcv"), pairs)


def swap_cores(array):
    return lax.ppermute(array, "rcv", [(0, 1), (1, 0)])


def local(src_green, rcv_green, model, observed):
    points, cores = lax.axis_size("pts"), lax.axis_size("rcv")
    bits = points.bit_length() - 1
    assert points == 1 << bits and cores == 2
    num_points = src_green.shape[2] * points
    count = src_green.shape[1] * rcv_green.shape[1] * cores
    scale = float((num_points / count) ** 0.5)
    me = lax.axis_index("pts").reshape(1)

    model = model.reshape(1, -1)
    own, rcv_own = modelled_parts(me, src_green, model, rcv_green, observed)
    up = list(range(bits))
    orders = [[up, up[::-1]], [up[:1] + up[:0:-1], up[::-1]]]
    for step in range(bits):
        own = [x + swap_points(x, [order[step] for order in by_core]) for x, by_core in zip(own, orders)]
    other = [swap_cores(x) for x in own]
    rcv_other = swap_cores(rcv_green)
    return image(own, other, src_green, rcv_own, rcv_other, count, scale).reshape(-1)


def solution(mesh):
    placed = (
        P(None, "grp", "pts"),
        P(None, ("grp", "rcv"), "pts"),
        P(("grp", "pts")),
        P(("grp", "pts"), None, "rcv"),
    )
    return jax.shard_map(
        local, mesh=mesh, in_specs=placed, out_specs=P(("grp", "pts")), check_vma=False
    )
```

time: 25.2 us -> 24.9 us (0.988)
  starting transfers between devices: 14.5 us -> 13.8 us
  waiting for transfers between devices: 7.04 us -> 7.42 us
    ppermute x7 -> x6, starting transfers between devices: 13.4 us -> 12.8 us  [swap_points(): return lax.ppermute(array, ('pts', 'rcv'), pairs)]
    ppermute x7 -> x6, waiting for transfers between devices: 5.81 us -> 6.14 us  [swap_points(): return lax.ppermute(array, ('pts', 'rcv'), pairs)]
    ppermute x4 -> x3, starting transfers between devices: 1.07 us -> 1.02 us  [swap_cores(): return lax.ppermute(array, 'rcv', [(0, 1), (1, 0)])]
    ppermute x4 -> x3, waiting for transfers between devices: 1.23 us -> 1.28 us  [swap_cores(): return lax.ppermute(array, 'rcv', [(0, 1), (1, 0)])]
    pallas_call x3 -> x4, Pallas kernels: 3.35 us -> 3.38 us  [the longest x1 1.55 us: modelled_parts(): pl.pallas_call(first_kernel, out_shape=[jax.ShapeDtypeStruct((half, width...]
  transfers between devices with their start and end apart: 11 -> 9, of which waited for: 7 -> 7; matrix products, arithmetic and copies ran while one was open for 0% -> 0% of each run, Pallas kernels for 7% -> 8%
where the time goes in v6:
time: 24.9 us; the launch traced here: 24.7 us
  starting transfers between devices  13.8 us (55%)
  waiting for transfers between devices  7.42 us (30%)
  Pallas kernels  3.38 us (14%)
    ppermute x6, starting transfers between devices, swap_points(): return lax.ppermute(array, ('pts', 'rcv'), pairs)  12.8 us
    ppermute x6, waiting for transfers between devices, swap_points(): return lax.ppermute(array, ('pts', 'rcv'), pairs)  6.14 us
    pallas_call x1, Pallas kernels, modelled_parts(): pl.pallas_call(first_kernel, out_shape=[jax.ShapeDtypeStruct((half, width...  1.55 us
    pallas_call x1, Pallas kernels, image(): pl.pallas_call(functools.partial(image_kernel, count, scale), out_shape=j...  1.47 us
    ppermute x3, waiting for transfers between devices, swap_cores(): return lax.ppermute(array, 'rcv', [(0, 1), (1, 0)])  1.28 us
    ppermute x3, starting transfers between devices, swap_cores(): return lax.ppermute(array, 'rcv', [(0, 1), (1, 0)])  1.02 us
  transfers between devices with their start and end apart: 9, of which 7 were waited for; matrix products, arithmetic and copies ran while one was open for 0% of the time, Pallas kernels for 8%

profile of v6, /device:TPU:0, one launch (start us, length us, event | category | flops | bytes accessed | tf_op | source)
XLA Modules:
  0.0 24.7 jit_solution(2347022692108581110)
XLA Ops:
  0.0 0.5 %collective-permute-start.7 = (f32[2,512,256]{2,1,0:T(8,128)}, f32[2,512,256]{2,1,0:T(8,128)S(1)}, u32[]{:S(2)}, u32[]{:S(2)}) collective-permute-start(f32[2,512,256]{2,1,0:T(8,128)} %rcv_ref.1), channel_id=1, source_target_pairs={{0,1},{1,0},{2,3},{3,2},{4,5},{5,4},{6,7},{7,6},{8,9},{9,8},{10,11... | collective-permute-start | bytes 3145736 | tf_op jit(solution)/shard_map/ppermute | solution.py:200
  0.5 1.5 %modelled_sent.1 = (f32[256,128]{1,0:T(8,128)S(1)}, f32[2,512,256]{2,1,0:T(8,128)S(1)}, bf16[2,256,256]{2,1,0:T(8,128)(2,1)S(1)}, f32[512,128]{1,0:T(8,128)S(1)}) custom-call(s32[1]{0:T(128)} %bitcast.me_ref, f32[2,64,256]{2,1,0:T(8,128)} %refs_2_.1, f32[1,256]{1,0:T(1,128)} %bitcast.3, f32[2,512,256]{2,1,0:T(8,128)} %rcv_ref.1, f32[8,2,512]{2,1,0:T(2,128)} %obs_ref.1), custom_call_target="tpu_custom_call" | custom-call | tf_op jit(solution)/shard_map/modelled_sent/pallas_call | solution.py:91
  2.0 2.6 %collective-permute-start.3 = (f32[256,128]{1,0:T(8,128)S(1)}, f32[256,128]{1,0:T(8,128)S(1)}, u32[]{:S(2)}, u32[]{:S(2)}) collective-permute-start(f32[256,128]{1,0:T(8,128)S(1)} %get-tuple-element.12), channel_id=1, source_target_pairs={{0,2},{1,9},{2,0},{3,11},{4,6},{5,13},{6,4},{7,15},{8,10},{9,1},{1... | collective-permute-start | bytes 393224 | tf_op jit(solution)/shard_map/ppermute | solution.py:196
  4.6 0.3 %modelled_rest.1 = f32[256,128]{1,0:T(8,128)S(1)} custom-call(f32[512,128]{1,0:T(8,128)S(1)} %get-tuple-element.9.data_ref, f32[2,512,256]{2,1,0:T(8,128)S(1)} %get-tuple-element.10.rcv_ref.refs_0_, bf16[2,256,256]{2,1,0:T(8,128)(2,1)S(1)} %get-tuple-element.11.rows_ref), custom_call_target="tpu_custom_call" | custom-call | flops 1000000000 | bytes 4000000 | tf_op jit(solution)/shard_map/modelled_rest/pallas_call | solution.py:112
  4.9 0.1 collective-permute-start
  5.0 2.6 %collective-permute-done.3 = f32[256,128]{1,0:T(8,128)S(1)} collective-permute-done((f32[256,128]{1,0:T(8,128)S(1)}, f32[256,128]{1,0:T(8,128)S(1)}, u32[]{:S(2)}, u32[]{:S(2)}) %collective-permute-start.3) | collective-permute-done | bytes 131104 | tf_op jit(solution)/shard_map/ppermute | solution.py:196
  7.5 2.2 %collective-permute-start.4 = (f32[256,128]{1,0:T(8,128)S(1)}, f32[256,128]{1,0:T(8,128)S(1)}, u32[]{:S(2)}, u32[]{:S(2)}) collective-permute-start(f32[256,128]{1,0:T(8,128)S(1)} %add.21), channel_id=1, source_target_pairs={{0,4},{1,5},{2,6},{3,7},{4,0},{5,1},{6,2},{7,3},{8,12},{9,13},{10,... | collective-permute-start | bytes 393224 | tf_op jit(solution)/shard_map/ppermute | solution.py:196
  9.7 0.2 collective-permute-done
  9.9 2.7 %collective-permute-start.1 = (f32[256,128]{1,0:T(8,128)S(1)}, f32[256,128]{1,0:T(8,128)S(1)}, u32[]{:S(2)}, u32[]{:S(2)}) collective-permute-start(f32[256,128]{1,0:T(8,128)S(1)} %add.18), channel_id=1, source_target_pairs={{0,8},{1,5},{2,10},{3,7},{4,12},{5,1},{6,14},{7,3},{8,0},{9,13},{1... | collective-permute-start | bytes 393224 | tf_op jit(solution)/shard_map/ppermute | solution.py:196
  12.6 0.4 %collective-permute-done.4 = f32[256,128]{1,0:T(8,128)S(1)} collective-permute-done((f32[256,128]{1,0:T(8,128)S(1)}, f32[256,128]{1,0:T(8,128)S(1)}, u32[]{:S(2)}, u32[]{:S(2)}) %collective-permute-start.4) | collective-permute-done | bytes 131104 | tf_op jit(solution)/shard_map/ppermute | solution.py:196
  13.0 3.0 %collective-permute-start.5 = (f32[256,128]{1,0:T(8,128)S(1)}, f32[256,128]{1,0:T(8,128)S(1)}, u32[]{:S(2)}, u32[]{:S(2)}) collective-permute-start(f32[256,128]{1,0:T(8,128)S(1)} %add.22), channel_id=1, source_target_pairs={{0,8},{1,3},{2,10},{3,1},{4,12},{5,7},{6,14},{7,5},{8,0},{9,11},{1... | collective-permute-start | bytes 393224 | tf_op jit(solution)/shard_map/ppermute | solution.py:196
  16.0 0.5 %collective-permute-done.1 = f32[256,128]{1,0:T(8,128)S(1)} collective-permute-done((f32[256,128]{1,0:T(8,128)S(1)}, f32[256,128]{1,0:T(8,128)S(1)}, u32[]{:S(2)}, u32[]{:S(2)}) %collective-permute-start.1) | collective-permute-done | bytes 131104 | tf_op jit(solution)/shard_map/ppermute | solution.py:196
  16.5 2.3 %collective-permute-start.2 = (f32[256,128]{1,0:T(8,128)S(1)}, f32[256,128]{1,0:T(8,128)S(1)}, u32[]{:S(2)}, u32[]{:S(2)}) collective-permute-start(f32[256,128]{1,0:T(8,128)S(1)} %add.19), channel_id=1, source_target_pairs={{0,4},{1,3},{2,6},{3,1},{4,0},{5,7},{6,2},{7,5},{8,12},{9,11},{10,... | collective-permute-start | bytes 393224 | tf_op jit(solution)/shard_map/ppermute | solution.py:196
  18.9 0.4 %collective-permute-done.5 = f32[256,128]{1,0:T(8,128)S(1)} collective-permute-done((f32[256,128]{1,0:T(8,128)S(1)}, f32[256,128]{1,0:T(8,128)S(1)}, u32[]{:S(2)}, u32[]{:S(2)}) %collective-permute-start.5) | collective-permute-done | bytes 131104 | tf_op jit(solution)/shard_map/ppermute | solution.py:196
  19.3 0.5 %collective-permute-start.6 = (f32[256,128]{1,0:T(8,128)S(1)}, f32[256,128]{1,0:T(8,128)S(1)}, u32[]{:S(2)}, u32[]{:S(2)}) collective-permute-start(f32[256,128]{1,0:T(8,128)S(1)} %add.23.own_first_ref.refs_4_), channel_id=1, source_target_pairs={{0,1},{1,0},{2,3},{3,2},{4,5},{5,4},{6,7},{7,6},{8,9},{9,8},{10,11... | collective-permute-start | bytes 393224 | tf_op jit(solution)/shard_map/ppermute | solution.py:200
  19.8 2.0 %collective-permute-done.2 = f32[256,128]{1,0:T(8,128)S(1)} collective-permute-done((f32[256,128]{1,0:T(8,128)S(1)}, f32[256,128]{1,0:T(8,128)S(1)}, u32[]{:S(2)}, u32[]{:S(2)}) %collective-permute-start.2) | collective-permute-done | bytes 131104 | tf_op jit(solution)/shard_map/ppermute | solution.py:196
  21.8 0.0 copy-start
  21.9 0.1 collective-permute-start.8
  21.9 0.0 collective-permute-done.6.other_first_ref.refs_6_
  21.9 0.1 energies.1.ready_ref
  22.0 1.3 %collective-permute-done.8.refs_5_ = f32[256,128]{1,0:T(8,128)S(1)} collective-permute-done((f32[256,128]{1,0:T(8,128)S(1)}, f32[256,128]{1,0:T(8,128)S(1)}, u32[]{:S(2)}, u32[]{:S(2)}) %collective-permute-start.8) | collective-permute-done | bytes 131104 | tf_op jit(solution)/shard_map/ppermute | solution.py:200
  23.3 0.0 collective-permute-done.7.refs_1_
  23.3 0.0 copy-done
  23.3 1.5 %image.1 = f32[1,256]{1,0:T(1,128)} custom-call(f32[2,8,128]{2,1,0:T(8,128)S(1)} %energies.1.ready_ref, f32[2,512,256]{2,1,0:T(8,128)S(1)} %get-tuple-element.10.rcv_ref.refs_0_, f32[2,512,256]{2,1,0:T(8,128)S(1)} %collective-permute-done.7.refs_1_, f32[2,64,256]{2,1,0:T(8,128)S(1)} %copy-done, f32[256,128]{1,0:T(8,128)S(1)} %add.20.own_last_ref.refs_3_, ...), custom_call_target="tpu_custom_call" | custom-call | tf_op jit(solution)/shard_map/image/pallas_call | solution.py:183
  (6 shorter events, 0.1 us)
Async XLA Ops:
  0.0 23.3 %collective-permute-start.7 = (f32[2,512,256]{2,1,0:T(8,128)}, f32[2,512,256]{2,1,0:T(8,128)S(1)}, u32[]{:S(2)}, u32[]{:S(2)}) collective-permute-start(f32[2,512,256]{2,1,0:T(8,128)} %rcv_ref.1), channel_id=1, source_target_pairs={{0,1},{1,0},{2,3},{3,2},{4,5},{5,4},{6,7},{7,6},{8,9},{9,8},{10,11... | collective-permute-start | bytes 3145736 | tf_op jit(solution)/shard_map/ppermute | solution.py:200
  2.0 5.5 %collective-permute-start.3 = (f32[256,128]{1,0:T(8,128)S(1)}, f32[256,128]{1,0:T(8,128)S(1)}, u32[]{:S(2)}, u32[]{:S(2)}) collective-permute-start(f32[256,128]{1,0:T(8,128)S(1)} %get-tuple-element.12), channel_id=1, source_target_pairs={{0,2},{1,9},{2,0},{3,11},{4,6},{5,13},{6,4},{7,15},{8,10},{9,1},{1... | collective-permute-start | bytes 393224 | tf_op jit(solution)/shard_map/ppermute | solution.py:196
  4.9 5.0 %collective-permute-start = (f32[256,128]{1,0:T(8,128)S(1)}, f32[256,128]{1,0:T(8,128)S(1)}, u32[]{:S(2)}, u32[]{:S(2)}) collective-permute-start(f32[256,128]{1,0:T(8,128)S(1)} %modelled_rest.1), channel_id=1, source_target_pairs={{0,2},{1,9},{2,0},{3,11},{4,6},{5,13},{6,4},{7,15},{8,10},{9,1},{1... | collective-permute-start | bytes 393224 | tf_op jit(solution)/shard_map/ppermute | solution.py:196
  7.5 5.5 %collective-permute-start.4 = (f32[256,128]{1,0:T(8,128)S(1)}, f32[256,128]{1,0:T(8,128)S(1)}, u32[]{:S(2)}, u32[]{:S(2)}) collective-permute-start(f32[256,128]{1,0:T(8,128)S(1)} %add.21), channel_id=1, source_target_pairs={{0,4},{1,5},{2,6},{3,7},{4,0},{5,1},{6,2},{7,3},{8,12},{9,13},{10,... | collective-permute-start | bytes 393224 | tf_op jit(solution)/shard_map/ppermute | solution.py:196
  9.9 6.6 %collective-permute-start.1 = (f32[256,128]{1,0:T(8,128)S(1)}, f32[256,128]{1,0:T(8,128)S(1)}, u32[]{:S(2)}, u32[]{:S(2)}) collective-permute-start(f32[256,128]{1,0:T(8,128)S(1)} %add.18), channel_id=1, source_target_pairs={{0,8},{1,5},{2,10},{3,7},{4,12},{5,1},{6,14},{7,3},{8,0},{9,13},{1... | collective-permute-start | bytes 393224 | tf_op jit(solution)/shard_map/ppermute | solution.py:196
  13.0 6.3 %collective-permute-start.5 = (f32[256,128]{1,0:T(8,128)S(1)}, f32[256,128]{1,0:T(8,128)S(1)}, u32[]{:S(2)}, u32[]{:S(2)}) collective-permute-start(f32[256,128]{1,0:T(8,128)S(1)} %add.22), channel_id=1, source_target_pairs={{0,8},{1,3},{2,10},{3,1},{4,12},{5,7},{6,14},{7,5},{8,0},{9,11},{1... | collective-permute-start | bytes 393224 | tf_op jit(solution)/shard_map/ppermute | solution.py:196
  16.5 5.3 %collective-permute-start.2 = (f32[256,128]{1,0:T(8,128)S(1)}, f32[256,128]{1,0:T(8,128)S(1)}, u32[]{:S(2)}, u32[]{:S(2)}) collective-permute-start(f32[256,128]{1,0:T(8,128)S(1)} %add.19), channel_id=1, source_target_pairs={{0,4},{1,3},{2,6},{3,1},{4,0},{5,7},{6,2},{7,5},{8,12},{9,11},{10,... | collective-permute-start | bytes 393224 | tf_op jit(solution)/shard_map/ppermute | solution.py:196
  19.3 2.6 %collective-permute-start.6 = (f32[256,128]{1,0:T(8,128)S(1)}, f32[256,128]{1,0:T(8,128)S(1)}, u32[]{:S(2)}, u32[]{:S(2)}) collective-permute-start(f32[256,128]{1,0:T(8,128)S(1)} %add.23.own_first_ref.refs_4_), channel_id=1, source_target_pairs={{0,1},{1,0},{2,3},{3,2},{4,5},{5,4},{6,7},{7,6},{8,9},{9,8},{10,11... | collective-permute-start | bytes 393224 | tf_op jit(solution)/shard_map/ppermute | solution.py:200
  21.8 1.4 %copy-start = (f32[2,64,256]{2,1,0:T(8,128)S(1)}, f32[2,64,256]{2,1,0:T(8,128)}, u32[]{:S(2)}) copy-start(f32[2,64,256]{2,1,0:T(8,128)} %refs_2_.1) | copy-start | bytes 393220
  21.9 1.4 %collective-permute-start.8 = (f32[256,128]{1,0:T(8,128)S(1)}, f32[256,128]{1,0:T(8,128)S(1)}, u32[]{:S(2)}, u32[]{:S(2)}) collective-permute-start(f32[256,128]{1,0:T(8,128)S(1)} %add.20.own_last_ref.refs_3_), channel_id=1, source_target_pairs={{0,1},{1,0},{2,3},{3,2},{4,5},{5,4},{6,7},{7,6},{8,9},{9,8},{10,11... | collective-permute-start | bytes 393224 | tf_op jit(solution)/shard_map/ppermute | solution.py:200

commit v7 on v6

--- a/solution.py
+++ b/solution.py
@@ -11,7 +11,7 @@
 LANES_LAST = (((1,), (1,)), ((), ()))
 PLAIN = (((1,), (0,)), ((), ()))
 VMEM_LIMIT = 24 * 1024 * 1024
-SHARE = 32
+SHARE = 34
 
 
 def split(x):

time: 24.9 us -> 24.6 us (0.988)
  waiting for transfers between devices: 7.42 us -> 6.63 us
  starting transfers between devices: 13.8 us -> 14.3 us
    ppermute x3, starting transfers between devices: 1.02 us -> 1.82 us  [swap_cores(): return lax.ppermute(array, 'rcv', [(0, 1), (1, 0)])]
    ppermute x6, waiting for transfers between devices: 6.14 us -> 5.47 us  [swap_points(): return lax.ppermute(array, ('pts', 'rcv'), pairs)]
    ppermute x6, starting transfers between devices: 12.8 us -> 12.4 us  [swap_points(): return lax.ppermute(array, ('pts', 'rcv'), pairs)]
  transfers between devices with their start and end apart: 9 -> 9, of which waited for: 7 -> 6; matrix products, arithmetic and copies ran while one was open for 0% -> 0% of each run, Pallas kernels for 8% -> 8%
where the time goes in v7:
time: 24.6 us; the launch traced here: 24.4 us
  starting transfers between devices  14.3 us (58%)
  waiting for transfers between devices  6.63 us (27%)
  Pallas kernels  3.38 us (14%)
    ppermute x6, starting transfers between devices, swap_points(): return lax.ppermute(array, ('pts', 'rcv'), pairs)  12.4 us
    ppermute x6, waiting for transfers between devices, swap_points(): return lax.ppermute(array, ('pts', 'rcv'), pairs)  5.47 us
    ppermute x3, starting transfers between devices, swap_cores(): return lax.ppermute(array, 'rcv', [(0, 1), (1, 0)])  1.82 us
    pallas_call x1, Pallas kernels, modelled_parts(): pl.pallas_call(first_kernel, out_shape=[jax.ShapeDtypeStruct((half, width...  1.56 us
    pallas_call x1, Pallas kernels, image(): pl.pallas_call(functools.partial(image_kernel, count, scale), out_shape=j...  1.46 us
    ppermute x3, waiting for transfers between devices, swap_cores(): return lax.ppermute(array, 'rcv', [(0, 1), (1, 0)])  1.16 us
  transfers between devices with their start and end apart: 9, of which 6 were waited for; matrix products, arithmetic and copies ran while one was open for 0% of the time, Pallas kernels for 8%

profile of v7, /device:TPU:0, one launch (start us, length us, event | category | flops | bytes accessed | tf_op | source)
XLA Modules:
  0.0 24.4 jit_solution(157910683268669871)
XLA Ops:
  0.0 0.5 %collective-permute-start.7 = (f32[2,512,256]{2,1,0:T(8,128)}, f32[2,512,256]{2,1,0:T(8,128)S(1)}, u32[]{:S(2)}, u32[]{:S(2)}) collective-permute-start(f32[2,512,256]{2,1,0:T(8,128)} %rcv_ref.1), channel_id=1, source_target_pairs={{0,1},{1,0},{2,3},{3,2},{4,5},{5,4},{6,7},{7,6},{8,9},{9,8},{10,11... | collective-permute-start | bytes 3145736 | tf_op jit(solution)/shard_map/ppermute | solution.py:200
  0.5 1.6 %modelled_sent.1 = (f32[272,128]{1,0:T(8,128)S(1)}, f32[2,512,256]{2,1,0:T(8,128)S(1)}, bf16[2,256,256]{2,1,0:T(8,128)(2,1)S(1)}, f32[512,128]{1,0:T(8,128)S(1)}) custom-call(s32[1]{0:T(128)} %bitcast.me_ref, f32[2,64,256]{2,1,0:T(8,128)} %refs_2_.1, f32[1,256]{1,0:T(1,128)} %bitcast.3, f32[2,512,256]{2,1,0:T(8,128)} %rcv_ref.1, f32[8,2,512]{2,1,0:T(2,128)} %obs_ref.1), custom_call_target="tpu_custom_call" | custom-call | tf_op jit(solution)/shard_map/modelled_sent/pallas_call | solution.py:91
  2.0 2.6 %collective-permute-start.3 = (f32[272,128]{1,0:T(8,128)S(1)}, f32[272,128]{1,0:T(8,128)S(1)}, u32[]{:S(2)}, u32[]{:S(2)}) collective-permute-start(f32[272,128]{1,0:T(8,128)S(1)} %get-tuple-element.12), channel_id=1, source_target_pairs={{0,2},{1,9},{2,0},{3,11},{4,6},{5,13},{6,4},{7,15},{8,10},{9,1},{1... | collective-permute-start | bytes 417800 | tf_op jit(solution)/shard_map/ppermute | solution.py:196
  4.6 0.3 %modelled_rest.1 = f32[240,128]{1,0:T(8,128)S(1)} custom-call(f32[512,128]{1,0:T(8,128)S(1)} %get-tuple-element.9.data_ref, f32[2,512,256]{2,1,0:T(8,128)S(1)} %get-tuple-element.10.rcv_ref.refs_0_, bf16[2,256,256]{2,1,0:T(8,128)(2,1)S(1)} %get-tuple-element.11.rows_ref), custom_call_target="tpu_custom_call" | custom-call | flops 1000000000 | bytes 4000000 | tf_op jit(solution)/shard_map/modelled_rest/pallas_call | solution.py:112
  4.9 0.1 collective-permute-start
  5.0 2.6 %collective-permute-done.3 = f32[272,128]{1,0:T(8,128)S(1)} collective-permute-done((f32[272,128]{1,0:T(8,128)S(1)}, f32[272,128]{1,0:T(8,128)S(1)}, u32[]{:S(2)}, u32[]{:S(2)}) %collective-permute-start.3) | collective-permute-done | bytes 139296 | tf_op jit(solution)/shard_map/ppermute | solution.py:196
  7.6 2.2 %collective-permute-start.4 = (f32[272,128]{1,0:T(8,128)S(1)}, f32[272,128]{1,0:T(8,128)S(1)}, u32[]{:S(2)}, u32[]{:S(2)}) collective-permute-start(f32[272,128]{1,0:T(8,128)S(1)} %add.21), channel_id=1, source_target_pairs={{0,4},{1,5},{2,6},{3,7},{4,0},{5,1},{6,2},{7,3},{8,12},{9,13},{10,... | collective-permute-start | bytes 417800 | tf_op jit(solution)/shard_map/ppermute | solution.py:196
  9.8 0.0 collective-permute-done
  9.8 2.7 %collective-permute-start.1 = (f32[240,128]{1,0:T(8,128)S(1)}, f32[240,128]{1,0:T(8,128)S(1)}, u32[]{:S(2)}, u32[]{:S(2)}) collective-permute-start(f32[240,128]{1,0:T(8,128)S(1)} %add.18), channel_id=1, source_target_pairs={{0,8},{1,5},{2,10},{3,7},{4,12},{5,1},{6,14},{7,3},{8,0},{9,13},{1... | collective-permute-start | bytes 368648 | tf_op jit(solution)/shard_map/ppermute | solution.py:196
  12.5 0.9 %collective-permute-done.4 = f32[272,128]{1,0:T(8,128)S(1)} collective-permute-done((f32[272,128]{1,0:T(8,128)S(1)}, f32[272,128]{1,0:T(8,128)S(1)}, u32[]{:S(2)}, u32[]{:S(2)}) %collective-permute-start.4) | collective-permute-done | bytes 139296 | tf_op jit(solution)/shard_map/ppermute | solution.py:196
  13.4 2.7 %collective-permute-start.5 = (f32[272,128]{1,0:T(8,128)S(1)}, f32[272,128]{1,0:T(8,128)S(1)}, u32[]{:S(2)}, u32[]{:S(2)}) collective-permute-start(f32[272,128]{1,0:T(8,128)S(1)} %add.22), channel_id=1, source_target_pairs={{0,8},{1,3},{2,10},{3,1},{4,12},{5,7},{6,14},{7,5},{8,0},{9,11},{1... | collective-permute-start | bytes 417800 | tf_op jit(solution)/shard_map/ppermute | solution.py:196
  16.1 0.2 collective-permute-done.1
  16.4 2.3 %collective-permute-start.2 = (f32[240,128]{1,0:T(8,128)S(1)}, f32[240,128]{1,0:T(8,128)S(1)}, u32[]{:S(2)}, u32[]{:S(2)}) collective-permute-start(f32[240,128]{1,0:T(8,128)S(1)} %add.19), channel_id=1, source_target_pairs={{0,4},{1,3},{2,6},{3,1},{4,0},{5,7},{6,2},{7,5},{8,12},{9,11},{10,... | collective-permute-start | bytes 368648 | tf_op jit(solution)/shard_map/ppermute | solution.py:196
  18.7 0.8 %collective-permute-done.5 = f32[272,128]{1,0:T(8,128)S(1)} collective-permute-done((f32[272,128]{1,0:T(8,128)S(1)}, f32[272,128]{1,0:T(8,128)S(1)}, u32[]{:S(2)}, u32[]{:S(2)}) %collective-permute-start.5) | collective-permute-done | bytes 139296 | tf_op jit(solution)/shard_map/ppermute | solution.py:196
  19.5 1.2 %collective-permute-start.6 = (f32[272,128]{1,0:T(8,128)S(1)}, f32[272,128]{1,0:T(8,128)S(1)}, u32[]{:S(2)}, u32[]{:S(2)}) collective-permute-start(f32[272,128]{1,0:T(8,128)S(1)} %add.23.own_first_ref.refs_4_), channel_id=1, source_target_pairs={{0,1},{1,0},{2,3},{3,2},{4,5},{5,4},{6,7},{7,6},{8,9},{9,8},{10,11... | collective-permute-start | bytes 417800 | tf_op jit(solution)/shard_map/ppermute | solution.py:200
  20.7 0.9 %collective-permute-done.2 = f32[240,128]{1,0:T(8,128)S(1)} collective-permute-done((f32[240,128]{1,0:T(8,128)S(1)}, f32[240,128]{1,0:T(8,128)S(1)}, u32[]{:S(2)}, u32[]{:S(2)}) %collective-permute-start.2) | collective-permute-done | bytes 122912 | tf_op jit(solution)/shard_map/ppermute | solution.py:196
  21.5 0.0 copy-start
  21.6 0.2 collective-permute-start.8
  21.7 0.0 collective-permute-done.6.other_first_ref.refs_6_
  21.7 0.1 energies.1.ready_ref
  21.8 1.2 %collective-permute-done.8.refs_5_ = f32[240,128]{1,0:T(8,128)S(1)} collective-permute-done((f32[240,128]{1,0:T(8,128)S(1)}, f32[240,128]{1,0:T(8,128)S(1)}, u32[]{:S(2)}, u32[]{:S(2)}) %collective-permute-start.8) | collective-permute-done | bytes 122912 | tf_op jit(solution)/shard_map/ppermute | solution.py:200
  23.0 0.0 collective-permute-done.7.refs_1_
  23.0 0.0 copy-done
  23.0 1.5 %image.1 = f32[1,256]{1,0:T(1,128)} custom-call(f32[2,8,128]{2,1,0:T(8,128)S(1)} %energies.1.ready_ref, f32[2,512,256]{2,1,0:T(8,128)S(1)} %get-tuple-element.10.rcv_ref.refs_0_, f32[2,512,256]{2,1,0:T(8,128)S(1)} %collective-permute-done.7.refs_1_, f32[2,64,256]{2,1,0:T(8,128)S(1)} %copy-done, f32[240,128]{1,0:T(8,128)S(1)} %add.20.own_last_ref.refs_3_, ...), custom_call_target="tpu_custom_call" | custom-call | tf_op jit(solution)/shard_map/image/pallas_call | solution.py:183
  (6 shorter events, 0.1 us)
Async XLA Ops:
  0.0 23.0 %collective-permute-start.7 = (f32[2,512,256]{2,1,0:T(8,128)}, f32[2,512,256]{2,1,0:T(8,128)S(1)}, u32[]{:S(2)}, u32[]{:S(2)}) collective-permute-start(f32[2,512,256]{2,1,0:T(8,128)} %rcv_ref.1), channel_id=1, source_target_pairs={{0,1},{1,0},{2,3},{3,2},{4,5},{5,4},{6,7},{7,6},{8,9},{9,8},{10,11... | collective-permute-start | bytes 3145736 | tf_op jit(solution)/shard_map/ppermute | solution.py:200
  2.0 5.6 %collective-permute-start.3 = (f32[272,128]{1,0:T(8,128)S(1)}, f32[272,128]{1,0:T(8,128)S(1)}, u32[]{:S(2)}, u32[]{:S(2)}) collective-permute-start(f32[272,128]{1,0:T(8,128)S(1)} %get-tuple-element.12), channel_id=1, source_target_pairs={{0,2},{1,9},{2,0},{3,11},{4,6},{5,13},{6,4},{7,15},{8,10},{9,1},{1... | collective-permute-start | bytes 417800 | tf_op jit(solution)/shard_map/ppermute | solution.py:196
  4.9 4.9 %collective-permute-start = (f32[240,128]{1,0:T(8,128)S(1)}, f32[240,128]{1,0:T(8,128)S(1)}, u32[]{:S(2)}, u32[]{:S(2)}) collective-permute-start(f32[240,128]{1,0:T(8,128)S(1)} %modelled_rest.1), channel_id=1, source_target_pairs={{0,2},{1,9},{2,0},{3,11},{4,6},{5,13},{6,4},{7,15},{8,10},{9,1},{1... | collective-permute-start | bytes 368648 | tf_op jit(solution)/shard_map/ppermute | solution.py:196
  7.6 5.8 %collective-permute-start.4 = (f32[272,128]{1,0:T(8,128)S(1)}, f32[272,128]{1,0:T(8,128)S(1)}, u32[]{:S(2)}, u32[]{:S(2)}) collective-permute-start(f32[272,128]{1,0:T(8,128)S(1)} %add.21), channel_id=1, source_target_pairs={{0,4},{1,5},{2,6},{3,7},{4,0},{5,1},{6,2},{7,3},{8,12},{9,13},{10,... | collective-permute-start | bytes 417800 | tf_op jit(solution)/shard_map/ppermute | solution.py:196
  9.8 6.5 %collective-permute-start.1 = (f32[240,128]{1,0:T(8,128)S(1)}, f32[240,128]{1,0:T(8,128)S(1)}, u32[]{:S(2)}, u32[]{:S(2)}) collective-permute-start(f32[240,128]{1,0:T(8,128)S(1)} %add.18), channel_id=1, source_target_pairs={{0,8},{1,5},{2,10},{3,7},{4,12},{5,1},{6,14},{7,3},{8,0},{9,13},{1... | collective-permute-start | bytes 368648 | tf_op jit(solution)/shard_map/ppermute | solution.py:196
  13.4 6.0 %collective-permute-start.5 = (f32[272,128]{1,0:T(8,128)S(1)}, f32[272,128]{1,0:T(8,128)S(1)}, u32[]{:S(2)}, u32[]{:S(2)}) collective-permute-start(f32[272,128]{1,0:T(8,128)S(1)} %add.22), channel_id=1, source_target_pairs={{0,8},{1,3},{2,10},{3,1},{4,12},{5,7},{6,14},{7,5},{8,0},{9,11},{1... | collective-permute-start | bytes 417800 | tf_op jit(solution)/shard_map/ppermute | solution.py:196
  16.4 5.2 %collective-permute-start.2 = (f32[240,128]{1,0:T(8,128)S(1)}, f32[240,128]{1,0:T(8,128)S(1)}, u32[]{:S(2)}, u32[]{:S(2)}) collective-permute-start(f32[240,128]{1,0:T(8,128)S(1)} %add.19), channel_id=1, source_target_pairs={{0,4},{1,3},{2,6},{3,1},{4,0},{5,7},{6,2},{7,5},{8,12},{9,11},{10,... | collective-permute-start | bytes 368648 | tf_op jit(solution)/shard_map/ppermute | solution.py:196
  19.5 2.3 %collective-permute-start.6 = (f32[272,128]{1,0:T(8,128)S(1)}, f32[272,128]{1,0:T(8,128)S(1)}, u32[]{:S(2)}, u32[]{:S(2)}) collective-permute-start(f32[272,128]{1,0:T(8,128)S(1)} %add.23.own_first_ref.refs_4_), channel_id=1, source_target_pairs={{0,1},{1,0},{2,3},{3,2},{4,5},{5,4},{6,7},{7,6},{8,9},{9,8},{10,11... | collective-permute-start | bytes 417800 | tf_op jit(solution)/shard_map/ppermute | solution.py:200
  21.5 1.4 %copy-start = (f32[2,64,256]{2,1,0:T(8,128)S(1)}, f32[2,64,256]{2,1,0:T(8,128)}, u32[]{:S(2)}) copy-start(f32[2,64,256]{2,1,0:T(8,128)} %refs_2_.1) | copy-start | bytes 393220
  21.6 1.4 %collective-permute-start.8 = (f32[240,128]{1,0:T(8,128)S(1)}, f32[240,128]{1,0:T(8,128)S(1)}, u32[]{:S(2)}, u32[]{:S(2)}) collective-permute-start(f32[240,128]{1,0:T(8,128)S(1)} %add.20.own_last_ref.refs_3_), channel_id=1, source_target_pairs={{0,1},{1,0},{2,3},{3,2},{4,5},{5,4},{6,7},{7,6},{8,9},{9,8},{10,11... | collective-permute-start | bytes 368648 | tf_op jit(solution)/shard_map/ppermute | solution.py:200

commit v8 on v7

--- a/solution.py
+++ b/solution.py
@@ -169,10 +169,11 @@
             both = square + pltpu.roll(square, sources, 1)
             weighted_high, weighted_low = split(here / (1.0 + both / spread_sq))
             wide = jnp.concatenate([weighted_high, weighted_low], axis=1)
-            for c, (double, low) in enumerate(stacks):
-                terms = dot(wide, double, PLAIN) + dot(weighted_high, low, PLAIN)
-                terms = terms * rcv_ref[c, pl.ds(first, here.shape[0]), :]
-                total += jnp.sum(terms.reshape(-1, 8, points), axis=0)
+            terms = [
+                (dot(wide, double, PLAIN) + dot(weighted_high, low, PLAIN)) * rcv_ref[c, pl.ds(first, here.shape[0]), :]
+                for c, (double, low) in enumerate(stacks)
+            ]
+            total += jnp.sum((terms[0] + terms[1]).reshape(-1, 8, points), axis=0)
         sums.append(jnp.sum(total, axis=0, keepdims=True))
     out_ref[...] = (sums[0] + sums[1]) * scale
 

time: 24.6 us -> 24.6 us (level)
  no operation moved by 1% of the time
where the time goes in v8:
time: 24.6 us; the launch traced here: 24.4 us
  starting transfers between devices  14.3 us (58%)
  waiting for transfers between devices  6.63 us (27%)
  Pallas kernels  3.38 us (14%)
    ppermute x6, starting transfers between devices, swap_points(): return lax.ppermute(array, ('pts', 'rcv'), pairs)  12.4 us
    ppermute x6, waiting for transfers between devices, swap_points(): return lax.ppermute(array, ('pts', 'rcv'), pairs)  5.47 us
    ppermute x3, starting transfers between devices, swap_cores(): return lax.ppermute(array, 'rcv', [(0, 1), (1, 0)])  1.82 us
    pallas_call x1, Pallas kernels, modelled_parts(): pl.pallas_call(first_kernel, out_shape=[jax.ShapeDtypeStruct((half, width...  1.56 us
    pallas_call x1, Pallas kernels, image(): pl.pallas_call(functools.partial(image_kernel, count, scale), out_shape=j...  1.47 us
    ppermute x3, waiting for transfers between devices, swap_cores(): return lax.ppermute(array, 'rcv', [(0, 1), (1, 0)])  1.16 us
  transfers between devices with their start and end apart: 9, of which 6 were waited for; matrix products, arithmetic and copies ran while one was open for 0% of the time, Pallas kernels for 8%

profile of v8, /device:TPU:0, one launch (start us, length us, event | category | flops | bytes accessed | tf_op | source)
XLA Modules:
  0.0 24.4 jit_solution(11887227830788725439)
XLA Ops:
  0.0 0.5 %collective-permute-start.7 = (f32[2,512,256]{2,1,0:T(8,128)}, f32[2,512,256]{2,1,0:T(8,128)S(1)}, u32[]{:S(2)}, u32[]{:S(2)}) collective-permute-start(f32[2,512,256]{2,1,0:T(8,128)} %rcv_ref.1), channel_id=1, source_target_pairs={{0,1},{1,0},{2,3},{3,2},{4,5},{5,4},{6,7},{7,6},{8,9},{9,8},{10,11... | collective-permute-start | bytes 3145736 | tf_op jit(solution)/shard_map/ppermute | solution.py:201
  0.5 1.6 %modelled_sent.1 = (f32[272,128]{1,0:T(8,128)S(1)}, f32[2,512,256]{2,1,0:T(8,128)S(1)}, bf16[2,256,256]{2,1,0:T(8,128)(2,1)S(1)}, f32[512,128]{1,0:T(8,128)S(1)}) custom-call(s32[1]{0:T(128)} %bitcast.me_ref, f32[2,64,256]{2,1,0:T(8,128)} %refs_2_.1, f32[1,256]{1,0:T(1,128)} %bitcast.3, f32[2,512,256]{2,1,0:T(8,128)} %rcv_ref.1, f32[8,2,512]{2,1,0:T(2,128)} %obs_ref.1), custom_call_target="tpu_custom_call" | custom-call | tf_op jit(solution)/shard_map/modelled_sent/pallas_call | solution.py:91
  2.0 2.6 %collective-permute-start.3 = (f32[272,128]{1,0:T(8,128)S(1)}, f32[272,128]{1,0:T(8,128)S(1)}, u32[]{:S(2)}, u32[]{:S(2)}) collective-permute-start(f32[272,128]{1,0:T(8,128)S(1)} %get-tuple-element.12), channel_id=1, source_target_pairs={{0,2},{1,9},{2,0},{3,11},{4,6},{5,13},{6,4},{7,15},{8,10},{9,1},{1... | collective-permute-start | bytes 417800 | tf_op jit(solution)/shard_map/ppermute | solution.py:197
  4.6 0.3 %modelled_rest.1 = f32[240,128]{1,0:T(8,128)S(1)} custom-call(f32[512,128]{1,0:T(8,128)S(1)} %get-tuple-element.9.data_ref, f32[2,512,256]{2,1,0:T(8,128)S(1)} %get-tuple-element.10.rcv_ref.refs_0_, bf16[2,256,256]{2,1,0:T(8,128)(2,1)S(1)} %get-tuple-element.11.rows_ref), custom_call_target="tpu_custom_call" | custom-call | flops 1000000000 | bytes 4000000 | tf_op jit(solution)/shard_map/modelled_rest/pallas_call | solution.py:112
  4.9 0.1 collective-permute-start
  5.0 2.6 %collective-permute-done.3 = f32[272,128]{1,0:T(8,128)S(1)} collective-permute-done((f32[272,128]{1,0:T(8,128)S(1)}, f32[272,128]{1,0:T(8,128)S(1)}, u32[]{:S(2)}, u32[]{:S(2)}) %collective-permute-start.3) | collective-permute-done | bytes 139296 | tf_op jit(solution)/shard_map/ppermute | solution.py:197
  7.6 2.2 %collective-permute-start.4 = (f32[272,128]{1,0:T(8,128)S(1)}, f32[272,128]{1,0:T(8,128)S(1)}, u32[]{:S(2)}, u32[]{:S(2)}) collective-permute-start(f32[272,128]{1,0:T(8,128)S(1)} %add.21), channel_id=1, source_target_pairs={{0,4},{1,5},{2,6},{3,7},{4,0},{5,1},{6,2},{7,3},{8,12},{9,13},{10,... | collective-permute-start | bytes 417800 | tf_op jit(solution)/shard_map/ppermute | solution.py:197
  9.8 0.0 collective-permute-done
  9.8 2.7 %collective-permute-start.1 = (f32[240,128]{1,0:T(8,128)S(1)}, f32[240,128]{1,0:T(8,128)S(1)}, u32[]{:S(2)}, u32[]{:S(2)}) collective-permute-start(f32[240,128]{1,0:T(8,128)S(1)} %add.18), channel_id=1, source_target_pairs={{0,8},{1,5},{2,10},{3,7},{4,12},{5,1},{6,14},{7,3},{8,0},{9,13},{1... | collective-permute-start | bytes 368648 | tf_op jit(solution)/shard_map/ppermute | solution.py:197
  12.5 0.9 %collective-permute-done.4 = f32[272,128]{1,0:T(8,128)S(1)} collective-permute-done((f32[272,128]{1,0:T(8,128)S(1)}, f32[272,128]{1,0:T(8,128)S(1)}, u32[]{:S(2)}, u32[]{:S(2)}) %collective-permute-start.4) | collective-permute-done | bytes 139296 | tf_op jit(solution)/shard_map/ppermute | solution.py:197
  13.4 2.7 %collective-permute-start.5 = (f32[272,128]{1,0:T(8,128)S(1)}, f32[272,128]{1,0:T(8,128)S(1)}, u32[]{:S(2)}, u32[]{:S(2)}) collective-permute-start(f32[272,128]{1,0:T(8,128)S(1)} %add.22), channel_id=1, source_target_pairs={{0,8},{1,3},{2,10},{3,1},{4,12},{5,7},{6,14},{7,5},{8,0},{9,11},{1... | collective-permute-start | bytes 417800 | tf_op jit(solution)/shard_map/ppermute | solution.py:197
  16.1 0.2 collective-permute-done.1
  16.4 2.3 %collective-permute-start.2 = (f32[240,128]{1,0:T(8,128)S(1)}, f32[240,128]{1,0:T(8,128)S(1)}, u32[]{:S(2)}, u32[]{:S(2)}) collective-permute-start(f32[240,128]{1,0:T(8,128)S(1)} %add.19), channel_id=1, source_target_pairs={{0,4},{1,3},{2,6},{3,1},{4,0},{5,7},{6,2},{7,5},{8,12},{9,11},{10,... | collective-permute-start | bytes 368648 | tf_op jit(solution)/shard_map/ppermute | solution.py:197
  18.7 0.8 %collective-permute-done.5 = f32[272,128]{1,0:T(8,128)S(1)} collective-permute-done((f32[272,128]{1,0:T(8,128)S(1)}, f32[272,128]{1,0:T(8,128)S(1)}, u32[]{:S(2)}, u32[]{:S(2)}) %collective-permute-start.5) | collective-permute-done | bytes 139296 | tf_op jit(solution)/shard_map/ppermute | solution.py:197
  19.5 1.2 %collective-permute-start.6 = (f32[272,128]{1,0:T(8,128)S(1)}, f32[272,128]{1,0:T(8,128)S(1)}, u32[]{:S(2)}, u32[]{:S(2)}) collective-permute-start(f32[272,128]{1,0:T(8,128)S(1)} %add.23.own_first_ref.refs_4_), channel_id=1, source_target_pairs={{0,1},{1,0},{2,3},{3,2},{4,5},{5,4},{6,7},{7,6},{8,9},{9,8},{10,11... | collective-permute-start | bytes 417800 | tf_op jit(solution)/shard_map/ppermute | solution.py:201
  20.7 0.9 %collective-permute-done.2 = f32[240,128]{1,0:T(8,128)S(1)} collective-permute-done((f32[240,128]{1,0:T(8,128)S(1)}, f32[240,128]{1,0:T(8,128)S(1)}, u32[]{:S(2)}, u32[]{:S(2)}) %collective-permute-start.2) | collective-permute-done | bytes 122912 | tf_op jit(solution)/shard_map/ppermute | solution.py:197
  21.5 0.0 copy-start
  21.6 0.2 collective-permute-start.8
  21.7 0.0 collective-permute-done.6.other_first_ref.refs_6_
  21.7 0.1 energies.1.ready_ref
  21.8 1.2 %collective-permute-done.8.refs_5_ = f32[240,128]{1,0:T(8,128)S(1)} collective-permute-done((f32[240,128]{1,0:T(8,128)S(1)}, f32[240,128]{1,0:T(8,128)S(1)}, u32[]{:S(2)}, u32[]{:S(2)}) %collective-permute-start.8) | collective-permute-done | bytes 122912 | tf_op jit(solution)/shard_map/ppermute | solution.py:201
  23.0 0.0 collective-permute-done.7.refs_1_
  23.0 0.0 copy-done
  23.0 1.5 %image.1 = f32[1,256]{1,0:T(1,128)} custom-call(f32[2,8,128]{2,1,0:T(8,128)S(1)} %energies.1.ready_ref, f32[2,512,256]{2,1,0:T(8,128)S(1)} %get-tuple-element.10.rcv_ref.refs_0_, f32[2,512,256]{2,1,0:T(8,128)S(1)} %collective-permute-done.7.refs_1_, f32[2,64,256]{2,1,0:T(8,128)S(1)} %copy-done, f32[240,128]{1,0:T(8,128)S(1)} %add.20.own_last_ref.refs_3_, ...), custom_call_target="tpu_custom_call" | custom-call | tf_op jit(solution)/shard_map/image/pallas_call | solution.py:184
  (6 shorter events, 0.1 us)
Async XLA Ops:
  0.0 23.0 %collective-permute-start.7 = (f32[2,512,256]{2,1,0:T(8,128)}, f32[2,512,256]{2,1,0:T(8,128)S(1)}, u32[]{:S(2)}, u32[]{:S(2)}) collective-permute-start(f32[2,512,256]{2,1,0:T(8,128)} %rcv_ref.1), channel_id=1, source_target_pairs={{0,1},{1,0},{2,3},{3,2},{4,5},{5,4},{6,7},{7,6},{8,9},{9,8},{10,11... | collective-permute-start | bytes 3145736 | tf_op jit(solution)/shard_map/ppermute | solution.py:201
  2.0 5.6 %collective-permute-start.3 = (f32[272,128]{1,0:T(8,128)S(1)}, f32[272,128]{1,0:T(8,128)S(1)}, u32[]{:S(2)}, u32[]{:S(2)}) collective-permute-start(f32[272,128]{1,0:T(8,128)S(1)} %get-tuple-element.12), channel_id=1, source_target_pairs={{0,2},{1,9},{2,0},{3,11},{4,6},{5,13},{6,4},{7,15},{8,10},{9,1},{1... | collective-permute-start | bytes 417800 | tf_op jit(solution)/shard_map/ppermute | solution.py:197
  4.9 4.9 %collective-permute-start = (f32[240,128]{1,0:T(8,128)S(1)}, f32[240,128]{1,0:T(8,128)S(1)}, u32[]{:S(2)}, u32[]{:S(2)}) collective-permute-start(f32[240,128]{1,0:T(8,128)S(1)} %modelled_rest.1), channel_id=1, source_target_pairs={{0,2},{1,9},{2,0},{3,11},{4,6},{5,13},{6,4},{7,15},{8,10},{9,1},{1... | collective-permute-start | bytes 368648 | tf_op jit(solution)/shard_map/ppermute | solution.py:197
  7.6 5.8 %collective-permute-start.4 = (f32[272,128]{1,0:T(8,128)S(1)}, f32[272,128]{1,0:T(8,128)S(1)}, u32[]{:S(2)}, u32[]{:S(2)}) collective-permute-start(f32[272,128]{1,0:T(8,128)S(1)} %add.21), channel_id=1, source_target_pairs={{0,4},{1,5},{2,6},{3,7},{4,0},{5,1},{6,2},{7,3},{8,12},{9,13},{10,... | collective-permute-start | bytes 417800 | tf_op jit(solution)/shard_map/ppermute | solution.py:197
  9.8 6.5 %collective-permute-start.1 = (f32[240,128]{1,0:T(8,128)S(1)}, f32[240,128]{1,0:T(8,128)S(1)}, u32[]{:S(2)}, u32[]{:S(2)}) collective-permute-start(f32[240,128]{1,0:T(8,128)S(1)} %add.18), channel_id=1, source_target_pairs={{0,8},{1,5},{2,10},{3,7},{4,12},{5,1},{6,14},{7,3},{8,0},{9,13},{1... | collective-permute-start | bytes 368648 | tf_op jit(solution)/shard_map/ppermute | solution.py:197
  13.4 6.0 %collective-permute-start.5 = (f32[272,128]{1,0:T(8,128)S(1)}, f32[272,128]{1,0:T(8,128)S(1)}, u32[]{:S(2)}, u32[]{:S(2)}) collective-permute-start(f32[272,128]{1,0:T(8,128)S(1)} %add.22), channel_id=1, source_target_pairs={{0,8},{1,3},{2,10},{3,1},{4,12},{5,7},{6,14},{7,5},{8,0},{9,11},{1... | collective-permute-start | bytes 417800 | tf_op jit(solution)/shard_map/ppermute | solution.py:197
  16.4 5.2 %collective-permute-start.2 = (f32[240,128]{1,0:T(8,128)S(1)}, f32[240,128]{1,0:T(8,128)S(1)}, u32[]{:S(2)}, u32[]{:S(2)}) collective-permute-start(f32[240,128]{1,0:T(8,128)S(1)} %add.19), channel_id=1, source_target_pairs={{0,4},{1,3},{2,6},{3,1},{4,0},{5,7},{6,2},{7,5},{8,12},{9,11},{10,... | collective-permute-start | bytes 368648 | tf_op jit(solution)/shard_map/ppermute | solution.py:197
  19.5 2.3 %collective-permute-start.6 = (f32[272,128]{1,0:T(8,128)S(1)}, f32[272,128]{1,0:T(8,128)S(1)}, u32[]{:S(2)}, u32[]{:S(2)}) collective-permute-start(f32[272,128]{1,0:T(8,128)S(1)} %add.23.own_first_ref.refs_4_), channel_id=1, source_target_pairs={{0,1},{1,0},{2,3},{3,2},{4,5},{5,4},{6,7},{7,6},{8,9},{9,8},{10,11... | collective-permute-start | bytes 417800 | tf_op jit(solution)/shard_map/ppermute | solution.py:201
  21.5 1.4 %copy-start = (f32[2,64,256]{2,1,0:T(8,128)S(1)}, f32[2,64,256]{2,1,0:T(8,128)}, u32[]{:S(2)}) copy-start(f32[2,64,256]{2,1,0:T(8,128)} %refs_2_.1) | copy-start | bytes 393220
  21.6 1.4 %collective-permute-start.8 = (f32[240,128]{1,0:T(8,128)S(1)}, f32[240,128]{1,0:T(8,128)S(1)}, u32[]{:S(2)}, u32[]{:S(2)}) collective-permute-start(f32[240,128]{1,0:T(8,128)S(1)} %add.20.own_last_ref.refs_3_), channel_id=1, source_target_pairs={{0,1},{1,0},{2,3},{3,2},{4,5},{5,4},{6,7},{7,6},{8,9},{9,8},{10,11... | collective-permute-start | bytes 368648 | tf_op jit(solution)/shard_map/ppermute | solution.py:201

commit v9 on v7

--- a/solution.py
+++ b/solution.py
@@ -54,7 +54,7 @@
         for c in range(2):
             n = 2 * k + c
             pieces.append(pltpu.make_async_copy(rcv_ref.at[c, here, :], rcv_out.at[c, here, :], sems.at[4 + n]))
-    for copy in [*inputs, obs_copy, *pieces]:
+    for copy in [*inputs, *pieces[:2], obs_copy, *pieces[2:]]:
         copy.start()
     placed_ref[...] = jnp.zeros_like(placed_ref)
     for copy in inputs:

time: 24.6 us -> 24.6 us (level)
  no operation moved by 1% of the time
where the time goes in v9:
time: 24.6 us; the launch traced here: 24.4 us
  starting transfers between devices  14.2 us (58%)
  waiting for transfers between devices  6.66 us (27%)
  Pallas kernels  3.39 us (14%)
    ppermute x6, starting transfers between devices, swap_points(): return lax.ppermute(array, ('pts', 'rcv'), pairs)  12.4 us
    ppermute x6, waiting for transfers between devices, swap_points(): return lax.ppermute(array, ('pts', 'rcv'), pairs)  5.49 us
    ppermute x3, starting transfers between devices, swap_cores(): return lax.ppermute(array, 'rcv', [(0, 1), (1, 0)])  1.8 us
    pallas_call x1, Pallas kernels, modelled_parts(): pl.pallas_call(first_kernel, out_shape=[jax.ShapeDtypeStruct((half, width...  1.57 us
    pallas_call x1, Pallas kernels, image(): pl.pallas_call(functools.partial(image_kernel, count, scale), out_shape=j...  1.46 us
    ppermute x3, waiting for transfers between devices, swap_cores(): return lax.ppermute(array, 'rcv', [(0, 1), (1, 0)])  1.17 us
  transfers between devices with their start and end apart: 9, of which 6 were waited for; matrix products, arithmetic and copies ran while one was open for 0% of the time, Pallas kernels for 8%

profile of v9, /device:TPU:0, one launch (start us, length us, event | category | flops | bytes accessed | tf_op | source)
XLA Modules:
  0.0 24.4 jit_solution(4478810625916274706)
XLA Ops:
  0.0 0.5 %collective-permute-start.7 = (f32[2,512,256]{2,1,0:T(8,128)}, f32[2,512,256]{2,1,0:T(8,128)S(1)}, u32[]{:S(2)}, u32[]{:S(2)}) collective-permute-start(f32[2,512,256]{2,1,0:T(8,128)} %rcv_ref.1), channel_id=1, source_target_pairs={{0,1},{1,0},{2,3},{3,2},{4,5},{5,4},{6,7},{7,6},{8,9},{9,8},{10,11... | collective-permute-start | bytes 3145736 | tf_op jit(solution)/shard_map/ppermute | solution.py:200
  0.5 1.6 %modelled_sent.1 = (f32[272,128]{1,0:T(8,128)S(1)}, f32[2,512,256]{2,1,0:T(8,128)S(1)}, bf16[2,256,256]{2,1,0:T(8,128)(2,1)S(1)}, f32[512,128]{1,0:T(8,128)S(1)}) custom-call(s32[1]{0:T(128)} %bitcast.me_ref, f32[2,64,256]{2,1,0:T(8,128)} %refs_2_.1, f32[1,256]{1,0:T(1,128)} %bitcast.3, f32[2,512,256]{2,1,0:T(8,128)} %rcv_ref.1, f32[8,2,512]{2,1,0:T(2,128)} %obs_ref.1), custom_call_target="tpu_custom_call" | custom-call | tf_op jit(solution)/shard_map/modelled_sent/pallas_call | solution.py:91
  2.0 2.6 %collective-permute-start.3 = (f32[272,128]{1,0:T(8,128)S(1)}, f32[272,128]{1,0:T(8,128)S(1)}, u32[]{:S(2)}, u32[]{:S(2)}) collective-permute-start(f32[272,128]{1,0:T(8,128)S(1)} %get-tuple-element.12), channel_id=1, source_target_pairs={{0,2},{1,9},{2,0},{3,11},{4,6},{5,13},{6,4},{7,15},{8,10},{9,1},{1... | collective-permute-start | bytes 417800 | tf_op jit(solution)/shard_map/ppermute | solution.py:196
  4.6 0.3 %modelled_rest.1 = f32[240,128]{1,0:T(8,128)S(1)} custom-call(f32[512,128]{1,0:T(8,128)S(1)} %get-tuple-element.9.data_ref, f32[2,512,256]{2,1,0:T(8,128)S(1)} %get-tuple-element.10.rcv_ref.refs_0_, bf16[2,256,256]{2,1,0:T(8,128)(2,1)S(1)} %get-tuple-element.11.rows_ref), custom_call_target="tpu_custom_call" | custom-call | flops 1000000000 | bytes 4000000 | tf_op jit(solution)/shard_map/modelled_rest/pallas_call | solution.py:112
  4.9 0.1 collective-permute-start
  5.0 2.6 %collective-permute-done.3 = f32[272,128]{1,0:T(8,128)S(1)} collective-permute-done((f32[272,128]{1,0:T(8,128)S(1)}, f32[272,128]{1,0:T(8,128)S(1)}, u32[]{:S(2)}, u32[]{:S(2)}) %collective-permute-start.3) | collective-permute-done | bytes 139296 | tf_op jit(solution)/shard_map/ppermute | solution.py:196
  7.6 2.2 %collective-permute-start.4 = (f32[272,128]{1,0:T(8,128)S(1)}, f32[272,128]{1,0:T(8,128)S(1)}, u32[]{:S(2)}, u32[]{:S(2)}) collective-permute-start(f32[272,128]{1,0:T(8,128)S(1)} %add.21), channel_id=1, source_target_pairs={{0,4},{1,5},{2,6},{3,7},{4,0},{5,1},{6,2},{7,3},{8,12},{9,13},{10,... | collective-permute-start | bytes 417800 | tf_op jit(solution)/shard_map/ppermute | solution.py:196
  9.8 0.0 collective-permute-done
  9.9 2.7 %collective-permute-start.1 = (f32[240,128]{1,0:T(8,128)S(1)}, f32[240,128]{1,0:T(8,128)S(1)}, u32[]{:S(2)}, u32[]{:S(2)}) collective-permute-start(f32[240,128]{1,0:T(8,128)S(1)} %add.18), channel_id=1, source_target_pairs={{0,8},{1,5},{2,10},{3,7},{4,12},{5,1},{6,14},{7,3},{8,0},{9,13},{1... | collective-permute-start | bytes 368648 | tf_op jit(solution)/shard_map/ppermute | solution.py:196
  12.5 0.9 %collective-permute-done.4 = f32[272,128]{1,0:T(8,128)S(1)} collective-permute-done((f32[272,128]{1,0:T(8,128)S(1)}, f32[272,128]{1,0:T(8,128)S(1)}, u32[]{:S(2)}, u32[]{:S(2)}) %collective-permute-start.4) | collective-permute-done | bytes 139296 | tf_op jit(solution)/shard_map/ppermute | solution.py:196
  13.4 2.7 %collective-permute-start.5 = (f32[272,128]{1,0:T(8,128)S(1)}, f32[272,128]{1,0:T(8,128)S(1)}, u32[]{:S(2)}, u32[]{:S(2)}) collective-permute-start(f32[272,128]{1,0:T(8,128)S(1)} %add.22), channel_id=1, source_target_pairs={{0,8},{1,3},{2,10},{3,1},{4,12},{5,7},{6,14},{7,5},{8,0},{9,11},{1... | collective-permute-start | bytes 417800 | tf_op jit(solution)/shard_map/ppermute | solution.py:196
  16.1 0.2 collective-permute-done.1
  16.4 2.3 %collective-permute-start.2 = (f32[240,128]{1,0:T(8,128)S(1)}, f32[240,128]{1,0:T(8,128)S(1)}, u32[]{:S(2)}, u32[]{:S(2)}) collective-permute-start(f32[240,128]{1,0:T(8,128)S(1)} %add.19), channel_id=1, source_target_pairs={{0,4},{1,3},{2,6},{3,1},{4,0},{5,7},{6,2},{7,5},{8,12},{9,11},{10,... | collective-permute-start | bytes 368648 | tf_op jit(solution)/shard_map/ppermute | solution.py:196
  18.7 0.8 %collective-permute-done.5 = f32[272,128]{1,0:T(8,128)S(1)} collective-permute-done((f32[272,128]{1,0:T(8,128)S(1)}, f32[272,128]{1,0:T(8,128)S(1)}, u32[]{:S(2)}, u32[]{:S(2)}) %collective-permute-start.5) | collective-permute-done | bytes 139296 | tf_op jit(solution)/shard_map/ppermute | solution.py:196
  19.5 1.2 %collective-permute-start.6 = (f32[272,128]{1,0:T(8,128)S(1)}, f32[272,128]{1,0:T(8,128)S(1)}, u32[]{:S(2)}, u32[]{:S(2)}) collective-permute-start(f32[272,128]{1,0:T(8,128)S(1)} %add.23.own_first_ref.refs_4_), channel_id=1, source_target_pairs={{0,1},{1,0},{2,3},{3,2},{4,5},{5,4},{6,7},{7,6},{8,9},{9,8},{10,11... | collective-permute-start | bytes 417800 | tf_op jit(solution)/shard_map/ppermute | solution.py:200
  20.6 0.9 %collective-permute-done.2 = f32[240,128]{1,0:T(8,128)S(1)} collective-permute-done((f32[240,128]{1,0:T(8,128)S(1)}, f32[240,128]{1,0:T(8,128)S(1)}, u32[]{:S(2)}, u32[]{:S(2)}) %collective-permute-start.2) | collective-permute-done | bytes 122912 | tf_op jit(solution)/shard_map/ppermute | solution.py:196
  21.5 0.0 copy-start
  21.6 0.2 collective-permute-start.8
  21.7 0.0 collective-permute-done.6.other_first_ref.refs_6_
  21.7 0.1 energies.1.ready_ref
  21.8 1.2 %collective-permute-done.8.refs_5_ = f32[240,128]{1,0:T(8,128)S(1)} collective-permute-done((f32[240,128]{1,0:T(8,128)S(1)}, f32[240,128]{1,0:T(8,128)S(1)}, u32[]{:S(2)}, u32[]{:S(2)}) %collective-permute-start.8) | collective-permute-done | bytes 122912 | tf_op jit(solution)/shard_map/ppermute | solution.py:200
  23.0 0.0 collective-permute-done.7.refs_1_
  23.0 0.0 copy-done
  23.0 1.5 %image.1 = f32[1,256]{1,0:T(1,128)} custom-call(f32[2,8,128]{2,1,0:T(8,128)S(1)} %energies.1.ready_ref, f32[2,512,256]{2,1,0:T(8,128)S(1)} %get-tuple-element.10.rcv_ref.refs_0_, f32[2,512,256]{2,1,0:T(8,128)S(1)} %collective-permute-done.7.refs_1_, f32[2,64,256]{2,1,0:T(8,128)S(1)} %copy-done, f32[240,128]{1,0:T(8,128)S(1)} %add.20.own_last_ref.refs_3_, ...), custom_call_target="tpu_custom_call" | custom-call | tf_op jit(solution)/shard_map/image/pallas_call | solution.py:183
  (6 shorter events, 0.1 us)
Async XLA Ops:
  0.0 23.0 %collective-permute-start.7 = (f32[2,512,256]{2,1,0:T(8,128)}, f32[2,512,256]{2,1,0:T(8,128)S(1)}, u32[]{:S(2)}, u32[]{:S(2)}) collective-permute-start(f32[2,512,256]{2,1,0:T(8,128)} %rcv_ref.1), channel_id=1, source_target_pairs={{0,1},{1,0},{2,3},{3,2},{4,5},{5,4},{6,7},{7,6},{8,9},{9,8},{10,11... | collective-permute-start | bytes 3145736 | tf_op jit(solution)/shard_map/ppermute | solution.py:200
  2.0 5.6 %collective-permute-start.3 = (f32[272,128]{1,0:T(8,128)S(1)}, f32[272,128]{1,0:T(8,128)S(1)}, u32[]{:S(2)}, u32[]{:S(2)}) collective-permute-start(f32[272,128]{1,0:T(8,128)S(1)} %get-tuple-element.12), channel_id=1, source_target_pairs={{0,2},{1,9},{2,0},{3,11},{4,6},{5,13},{6,4},{7,15},{8,10},{9,1},{1... | collective-permute-start | bytes 417800 | tf_op jit(solution)/shard_map/ppermute | solution.py:196
  4.9 4.9 %collective-permute-start = (f32[240,128]{1,0:T(8,128)S(1)}, f32[240,128]{1,0:T(8,128)S(1)}, u32[]{:S(2)}, u32[]{:S(2)}) collective-permute-start(f32[240,128]{1,0:T(8,128)S(1)} %modelled_rest.1), channel_id=1, source_target_pairs={{0,2},{1,9},{2,0},{3,11},{4,6},{5,13},{6,4},{7,15},{8,10},{9,1},{1... | collective-permute-start | bytes 368648 | tf_op jit(solution)/shard_map/ppermute | solution.py:196
  7.6 5.8 %collective-permute-start.4 = (f32[272,128]{1,0:T(8,128)S(1)}, f32[272,128]{1,0:T(8,128)S(1)}, u32[]{:S(2)}, u32[]{:S(2)}) collective-permute-start(f32[272,128]{1,0:T(8,128)S(1)} %add.21), channel_id=1, source_target_pairs={{0,4},{1,5},{2,6},{3,7},{4,0},{5,1},{6,2},{7,3},{8,12},{9,13},{10,... | collective-permute-start | bytes 417800 | tf_op jit(solution)/shard_map/ppermute | solution.py:196
  9.9 6.5 %collective-permute-start.1 = (f32[240,128]{1,0:T(8,128)S(1)}, f32[240,128]{1,0:T(8,128)S(1)}, u32[]{:S(2)}, u32[]{:S(2)}) collective-permute-start(f32[240,128]{1,0:T(8,128)S(1)} %add.18), channel_id=1, source_target_pairs={{0,8},{1,5},{2,10},{3,7},{4,12},{5,1},{6,14},{7,3},{8,0},{9,13},{1... | collective-permute-start | bytes 368648 | tf_op jit(solution)/shard_map/ppermute | solution.py:196
  13.4 6.0 %collective-permute-start.5 = (f32[272,128]{1,0:T(8,128)S(1)}, f32[272,128]{1,0:T(8,128)S(1)}, u32[]{:S(2)}, u32[]{:S(2)}) collective-permute-start(f32[272,128]{1,0:T(8,128)S(1)} %add.22), channel_id=1, source_target_pairs={{0,8},{1,3},{2,10},{3,1},{4,12},{5,7},{6,14},{7,5},{8,0},{9,11},{1... | collective-permute-start | bytes 417800 | tf_op jit(solution)/shard_map/ppermute | solution.py:196
  16.4 5.2 %collective-permute-start.2 = (f32[240,128]{1,0:T(8,128)S(1)}, f32[240,128]{1,0:T(8,128)S(1)}, u32[]{:S(2)}, u32[]{:S(2)}) collective-permute-start(f32[240,128]{1,0:T(8,128)S(1)} %add.19), channel_id=1, source_target_pairs={{0,4},{1,3},{2,6},{3,1},{4,0},{5,7},{6,2},{7,5},{8,12},{9,11},{10,... | collective-permute-start | bytes 368648 | tf_op jit(solution)/shard_map/ppermute | solution.py:196
  19.5 2.3 %collective-permute-start.6 = (f32[272,128]{1,0:T(8,128)S(1)}, f32[272,128]{1,0:T(8,128)S(1)}, u32[]{:S(2)}, u32[]{:S(2)}) collective-permute-start(f32[272,128]{1,0:T(8,128)S(1)} %add.23.own_first_ref.refs_4_), channel_id=1, source_target_pairs={{0,1},{1,0},{2,3},{3,2},{4,5},{5,4},{6,7},{7,6},{8,9},{9,8},{10,11... | collective-permute-start | bytes 417800 | tf_op jit(solution)/shard_map/ppermute | solution.py:200
  21.5 1.4 %copy-start = (f32[2,64,256]{2,1,0:T(8,128)S(1)}, f32[2,64,256]{2,1,0:T(8,128)}, u32[]{:S(2)}) copy-start(f32[2,64,256]{2,1,0:T(8,128)} %refs_2_.1) | copy-start | bytes 393220
  21.6 1.4 %collective-permute-start.8 = (f32[240,128]{1,0:T(8,128)S(1)}, f32[240,128]{1,0:T(8,128)S(1)}, u32[]{:S(2)}, u32[]{:S(2)}) collective-permute-start(f32[240,128]{1,0:T(8,128)S(1)} %add.20.own_last_ref.refs_3_), channel_id=1, source_target_pairs={{0,1},{1,0},{2,3},{3,2},{4,5},{5,4},{6,7},{7,6},{8,9},{9,8},{10,11... | collective-permute-start | bytes 368648 | tf_op jit(solution)/shard_map/ppermute | solution.py:200
